TPU v7x, 32 devices: a whole 2x2x4 slice. The times are simulated.
32 devices in a mesh: dp: 8 (over z, x), fsdp: 4 (over y, core).
Axes of the slice: x: 2, y: 2, z: 4, core: 2. Of those that a mesh axis runs over, the one named last changes fastest.
Arguments:
- latents: bfloat16 [16, 512, 1408], P('dp', 'fsdp'), may hold values from -6 to 6
- skip_input: bfloat16 [16, 512, 1408], P('dp', 'fsdp'), may hold values from -6 to 6
- text_tokens: bfloat16 [16, 336, 1024], P('dp', 'fsdp'), may hold values from -6 to 6
- cotangent: bfloat16 [16, 512, 1408], P('dp', 'fsdp'), may hold values from -6 to 6
- timesteps: int32 [16], P('dp'), may hold values from 0 to 999
- text_lengths: int32 [16], P('dp'), may hold values from 84 to 336
- positions: int32 [16, 2, 512], P('dp', None, 'fsdp'), may hold values from 0 to 127, as said below
- skip_weight: float32 [2816, 1408], P('dp', 'fsdp'), as said below
- skip_rows: float32 [2816], P('dp'), may hold values from 81 to 4096
- skip_columns: float32 [1408], P('fsdp'), may hold values from 81 to 4096
- square_weight: float32 [2, 1408, 1408], P(None, 'dp', 'fsdp'), as said below
- square_rows: float32 [2, 1408], P(None, 'dp'), may hold values from 81 to 4096
- square_columns: float32 [2, 1408], P(None, 'fsdp'), may hold values from 81 to 4096
- self_weight: float32 [1408, 4224], P('dp', 'fsdp'), as said below
- self_rows: float32 [1408], P('dp'), may hold values from 81 to 4096
- self_columns: float32 [4224], P('fsdp'), may hold values from 81 to 4096
- output_weight: float32 [2, 1408, 1408], P(None, 'dp', 'fsdp'), as said below
- output_rows: float32 [2, 1408], P(None, 'dp'), may hold values from 81 to 4096
- output_columns: float32 [2, 1408], P(None, 'fsdp'), may hold values from 81 to 4096
- text_weight: float32 [1024, 2816], P('dp', 'fsdp'), as said below
- text_rows: float32 [1024], P('dp'), may hold values from 81 to 4096
- text_columns: float32 [2816], P('fsdp'), may hold values from 81 to 4096
- up_weight: float32 [1408, 6144], P('dp', 'fsdp'), as said below
- up_rows: float32 [1408], P('dp'), may hold values from 81 to 4096
- up_columns: float32 [6144], P('fsdp'), may hold values from 81 to 4096
- down_weight: float32 [6144, 1408], P('dp', 'fsdp'), as said below
- down_rows: float32 [6144], P('dp'), may hold values from 81 to 4096
- down_columns: float32 [1408], P('fsdp'), may hold values from 81 to 4096
- norm_gains: float32 [5, 1408], replicated, may hold values from 0.1 to 1.9
- gain_state: float32 [5, 1408], replicated, may hold values from 81 to 4096
Outputs:
- block_output: bfloat16 [16, 512, 1408], P('dp', 'fsdp')
- latents_grad: bfloat16 [16, 512, 1408], P('dp', 'fsdp')
- skip_input_grad: bfloat16 [16, 512, 1408], P('dp', 'fsdp')
- skip_new: float32 [2816, 1408], P('dp', 'fsdp')
- skip_rows_new: float32 [2816], P('dp')
- skip_columns_new: float32 [1408], P('fsdp')
- skip_gradient: float32 [2816, 1408], P('dp', 'fsdp')
- square_new: float32 [2, 1408, 1408], P(None, 'dp', 'fsdp')
- square_rows_new: float32 [2, 1408], P(None, 'dp')
- square_columns_new: float32 [2, 1408], P(None, 'fsdp')
- square_gradient: float32 [2, 1408, 1408], P(None, 'dp', 'fsdp')
- self_new: float32 [1408, 4224], P('dp', 'fsdp')
- self_rows_new: float32 [1408], P('dp')
- self_columns_new: float32 [4224], P('fsdp')
- self_gradient: float32 [1408, 4224], P('dp', 'fsdp')
- output_new: float32 [2, 1408, 1408], P(None, 'dp', 'fsdp')
- output_rows_new: float32 [2, 1408], P(None, 'dp')
- output_columns_new: float32 [2, 1408], P(None, 'fsdp')
- output_gradient: float32 [2, 1408, 1408], P(None, 'dp', 'fsdp')
- text_new: float32 [1024, 2816], P('dp', 'fsdp')
- text_rows_new: float32 [1024], P('dp')
- text_columns_new: float32 [2816], P('fsdp')
- text_gradient: float32 [1024, 2816], P('dp', 'fsdp')
- up_new: float32 [1408, 6144], P('dp', 'fsdp')
- up_rows_new: float32 [1408], P('dp')
- up_columns_new: float32 [6144], P('fsdp')
- up_gradient: float32 [1408, 6144], P('dp', 'fsdp')
- down_new: float32 [6144, 1408], P('dp', 'fsdp')
- down_rows_new: float32 [6144], P('dp')
- down_columns_new: float32 [1408], P('fsdp')
- down_gradient: float32 [6144, 1408], P('dp', 'fsdp')
- gains_new: float32 [5, 1408], replicated
- gain_state_new: float32 [5, 1408], replicated
- gains_gradient: float32 [5, 1408], replicated
Inputs may be any that keep to these rules, and one draw needn't show every extreme that they name: Each latent's tokens lie row by row on a grid of 4, 8, 16 or 32 columns: positions[b, 0] is a token's row and positions[b, 1] its column. Latent 0 has 4 columns and latent 1 has 32. `skip_weight`: independent entries of mean zero. `square_weight`: independent entries of mean zero. `self_weight`: independent entries of mean zero. `output_weight`: independent entries of mean zero. `text_weight`: independent entries of mean zero. `up_weight`: independent entries of mean zero. `down_weight`: independent entries of mean zero.
All inputs are finite; a program needn't handle non-finite values.
Results may differ from a plain program's by a relative error of at most 0.02.
Values may be sent and summed in bfloat16 or wider, within the bound.
No kernel may reach another device: no remote copies, remote signals or barrier semaphores. Data moves between devices by JAX's collectives and lax.ppermute only.
A program may use at most 448 MiB of HBM per device.

v0:
```python
import math

import jax
import jax.numpy as jnp
from jax import lax
from jax.sharding import PartitionSpec as P

D = 1408
HEADS = 16


EPS_NORM = 1e-06
EPS_SQUARE = 1e-30
EPS_SCALE = 0.001
DECAY = 0.5
CLIP = 1.0
RATE = 0.5


def matmul(left, right):
    return jnp.dot(left, right, preferred_element_type=jnp.float32)


def matmul_left(left, right):
    return lax.dot_general(
        left, right, (((0,), (0,)), ((), ())), preferred_element_type=jnp.float32
    )


def matmul_right(left, right):
    return lax.dot_general(
        left, right, (((1,), (1,)), ((), ())), preferred_element_type=jnp.float32
    )


def norm_rows(values):
    center = values - jnp.mean(values, axis=-1, keepdims=True)
    spread = jnp.mean(center * center, axis=-1, keepdims=True)
    return center * lax.rsqrt(spread + EPS_NORM)


def rotary(values, places):
    half_width = values.shape[-1] // 2
    quarter = half_width // 2
    frequency = jnp.exp(-math.log(10000.0) * jnp.arange(quarter).astype(jnp.float32) / quarter)
    pieces = []
    for member in range(2):
        block = values[..., member * half_width : (member + 1) * half_width]
        angles = places[member].astype(jnp.float32)[:, None] * frequency[None, :]
        cosine = jnp.cos(angles)[:, None, :]
        sine = jnp.sin(angles)[:, None, :]
        former = block[..., :quarter]
        latter = block[..., quarter:]
        pieces.append(former * cosine - latter * sine)
        pieces.append(latter * cosine + former * sine)
    return jnp.concatenate(pieces, axis=-1)


def time_embed(step_value, model_width):
    half_width = model_width // 2
    frequency = jnp.exp(
        -math.log(10000.0) * jnp.arange(half_width).astype(jnp.float32) / half_width
    )
    angles = step_value.astype(jnp.float32) * frequency
    return jnp.concatenate([jnp.cos(angles), jnp.sin(angles)])


def skip_norm(joined, gain_skip):
    return norm_rows(joined) * gain_skip


def modulated(stream, gain_row, shift_row):
    return norm_rows(stream) * gain_row + shift_row


def gained(stream, gain_row):
    return norm_rows(stream) * gain_row


def head_prep(linear, places, head_count):
    row_count = linear.shape[0]
    shaped = linear.reshape(row_count, head_count, -1)
    return rotary(norm_rows(shaped), places).reshape(row_count, -1)


def head_norm(linear, head_count):
    row_count = linear.shape[0]
    return norm_rows(linear.reshape(row_count, head_count, -1)).reshape(row_count, -1)


def gelu_tanh(values):
    return jax.nn.gelu(values, approximate=True)


def attend_scores(queries, key_rows, valid_keys, head_count):
    query_count = queries.shape[0]
    head_size = queries.shape[1] // head_count
    shaped_query = queries.reshape(query_count, head_count, head_size)
    shaped_keys = key_rows.reshape(key_rows.shape[0], head_count, head_size)
    score_scale = 1.0 / math.sqrt(head_size)
    scores = (
        jnp.einsum("qhd,khd->hqk", shaped_query, shaped_keys, preferred_element_type=jnp.float32)
        * score_scale
    )
    if valid_keys is not None:
        scores = jnp.where(valid_keys[None, None, :], scores, -1e30)
    return (scores, shaped_query, shaped_keys, score_scale)


def attend_forward(queries, key_rows, value_rows, valid_keys, head_count):
    query_count = queries.shape[0]
    scores, shaped_query, shaped_keys, score_scale = attend_scores(
        queries, key_rows, valid_keys, head_count
    )
    shaped_values = value_rows.reshape(value_rows.shape[0], head_count, -1)
    row_top = jnp.max(scores, axis=-1, keepdims=True)
    logsum = row_top + jnp.log(jnp.sum(jnp.exp(scores - row_top), axis=-1, keepdims=True))
    weights_soft = jnp.exp(scores - logsum).astype(jnp.bfloat16)
    mixture = jnp.einsum(
        "hqk,khd->qhd", weights_soft, shaped_values, preferred_element_type=jnp.float32
    )
    return (mixture.reshape(query_count, -1).astype(jnp.bfloat16), logsum)


def attend_backward(queries, key_rows, value_rows, valid_keys, logsum, grad_mixture, head_count):
    query_count = queries.shape[0]
    scores, shaped_query, shaped_keys, score_scale = attend_scores(
        queries, key_rows, valid_keys, head_count
    )
    shaped_values = value_rows.reshape(value_rows.shape[0], head_count, -1)
    shaped_grad = grad_mixture.reshape(query_count, head_count, -1)
    weights_full = jnp.exp(scores - logsum)
    weights_soft = weights_full.astype(jnp.bfloat16)
    grad_weights = jnp.einsum(
        "qhd,khd->hqk", shaped_grad, shaped_values, preferred_element_type=jnp.float32
    )
    grad_values = jnp.einsum(
        "hqk,qhd->khd", weights_soft, shaped_grad, preferred_element_type=jnp.float32
    )
    row_delta = jnp.sum(weights_full * grad_weights, axis=-1, keepdims=True)
    grad_scores = (weights_full * (grad_weights - row_delta)).astype(jnp.bfloat16)
    grad_queries = (
        jnp.einsum("hqk,khd->qhd", grad_scores, shaped_keys, preferred_element_type=jnp.float32)
        * score_scale
    )
    grad_keys = (
        jnp.einsum("hqk,qhd->khd", grad_scores, shaped_query, preferred_element_type=jnp.float32)
        * score_scale
    )
    key_count = key_rows.shape[0]
    return (
        grad_queries.reshape(query_count, -1),
        grad_keys.reshape(key_count, -1),
        grad_values.reshape(key_count, -1),
    )


def gather_weights(masters):
    parts = [matrix.astype(jnp.bfloat16) for matrix in masters]
    wider = (
        lax.all_gather(parts[0], "fsdp", axis=1, tiled=True),
        lax.all_gather(parts[1], "fsdp", axis=2, tiled=True),
        lax.all_gather(parts[2], "fsdp", axis=1, tiled=True),
        lax.all_gather(parts[3], "fsdp", axis=2, tiled=True),
        lax.all_gather(parts[4], "fsdp", axis=1, tiled=True),
        lax.all_gather(parts[5], "fsdp", axis=1, tiled=True),
        lax.all_gather(parts[6], "fsdp", axis=1, tiled=True),
    )
    return (
        lax.all_gather(wider[0], "dp", axis=0, tiled=True),
        lax.all_gather(wider[1], "dp", axis=1, tiled=True),
        lax.all_gather(wider[2], "dp", axis=0, tiled=True),
        lax.all_gather(wider[3], "dp", axis=1, tiled=True),
        lax.all_gather(wider[4], "dp", axis=0, tiled=True),
        lax.all_gather(wider[5], "dp", axis=0, tiled=True),
        lax.all_gather(wider[6], "dp", axis=0, tiled=True),
    )


def project(lowered, weight):
    result = matmul(lowered, weight)
    return (result, lowered)


def project_back(saved_rows, grad_low, weight, want_input):
    weight_term = matmul_left(saved_rows, grad_low)
    input_grad = matmul_right(grad_low, weight) if want_input else None
    return (input_grad, weight_term)


def shift_forward(embed_low, weight):
    shift_row = matmul(embed_low[None, :], weight)
    return shift_row


def shift_backward(embed_low, grad_shift):
    flat_grad = grad_shift.reshape(-1)
    return embed_low.astype(jnp.float32)[:, None] * flat_grad[None, :]


def accumulate(total, term):
    return term if total is None else total + term


def flatten_all(arrays):
    return jnp.concatenate([matrix.reshape(-1) for matrix in arrays])


def split_all(vector, shapes):
    pieces = []
    offset = 0
    for shape_now in shapes:
        count_now = math.prod(shape_now)
        pieces.append(vector[offset : offset + count_now].reshape(shape_now))
        offset = offset + count_now
    return pieces


def shards(
    latents,
    skip_input,
    text_tokens,
    cotangent,
    timesteps,
    text_lengths,
    positions,
    skip_weight,
    skip_rows,
    skip_columns,
    square_weight,
    square_rows,
    square_columns,
    self_weight,
    self_rows,
    self_columns,
    output_weight,
    output_rows,
    output_columns,
    text_weight,
    text_rows,
    text_columns,
    up_weight,
    up_rows,
    up_columns,
    down_weight,
    down_rows,
    down_columns,
    norm_gains,
    gain_state,
):
    bf16 = jnp.bfloat16
    masters = (
        skip_weight,
        square_weight,
        self_weight,
        output_weight,
        text_weight,
        up_weight,
        down_weight,
    )
    model_width = D
    head_count = HEADS
    total_skip = None
    total_modulate = None
    total_cross_query = None
    total_self = None
    total_self_out = None
    total_cross_out = None
    total_text = None
    total_up = None
    total_down = None
    total_gains = jnp.zeros((5, D), jnp.float32)
    block_rows = []
    input_grad_rows = []
    skip_grad_rows = []
    for latent_index in range(latents.shape[0]):
        current = gather_weights(masters)
        skip_full, square_full, self_full, output_full, text_full, up_full, down_full = current
        joined = jnp.concatenate([latents[latent_index], skip_input[latent_index]], axis=-1).astype(
            jnp.float32
        )
        normed_skip, pull_skip = jax.vjp(skip_norm, joined, norm_gains[0:2].reshape(-1))
        lowered_skip = normed_skip.astype(bf16)
        stream, saved_skip = project(lowered_skip, skip_full)
        embed_low = jax.nn.silu(time_embed(timesteps[latent_index], model_width)).astype(bf16)
        shift_row = shift_forward(embed_low, square_full[0])
        normed_self, pull_self_norm = jax.vjp(modulated, stream, norm_gains[2], shift_row)
        lowered_self = normed_self.astype(bf16)
        joint, saved_self = project(lowered_self, self_full)
        places = positions[latent_index]

        def prepare(linear):
            return head_prep(linear, places, head_count)

        def text_prepare(linear):
            return head_norm(linear, head_count)

        query_rows, pull_query = jax.vjp(prepare, joint[:, :model_width])
        key_local, pull_key = jax.vjp(prepare, joint[:, model_width : 2 * model_width])
        text_local = text_tokens[latent_index]
        text_joint, saved_text = project(text_local, text_full)
        text_key_local, pull_text_key = jax.vjp(text_prepare, text_joint[:, :model_width])
        queries = query_rows.astype(bf16)
        key_all, value_all, text_key_all, text_value_all = (
            lax.all_gather(key_local.astype(bf16), "fsdp", axis=0, tiled=True),
            lax.all_gather(joint[:, 2 * model_width :].astype(bf16), "fsdp", axis=0, tiled=True),
            lax.all_gather(text_key_local.astype(bf16), "fsdp", axis=0, tiled=True),
            lax.all_gather(text_joint[:, model_width:].astype(bf16), "fsdp", axis=0, tiled=True),
        )
        attended, self_logsum = attend_forward(queries, key_all, value_all, None, head_count)
        self_branch, saved_attended = project(attended, output_full[0])
        self_stream = stream + self_branch
        normed_cross, pull_cross_norm = jax.vjp(gained, self_stream, norm_gains[3])
        lowered_cross = normed_cross.astype(bf16)
        cross_linear, saved_cross = project(lowered_cross, square_full[1])
        cross_query_rows, pull_cross_query = jax.vjp(prepare, cross_linear)
        cross_queries = cross_query_rows.astype(bf16)
        valid_keys = jnp.arange(text_key_all.shape[0]) < text_lengths[latent_index]
        cross_attended, cross_logsum = attend_forward(
            cross_queries, text_key_all, text_value_all, valid_keys, head_count
        )
        cross_branch, saved_cross_att = project(cross_attended, output_full[1])
        cross_stream = self_stream + cross_branch
        normed_mlp, pull_mlp_norm = jax.vjp(gained, cross_stream, norm_gains[4])
        lowered_mlp = normed_mlp.astype(bf16)
        hidden_pre, saved_mlp = project(lowered_mlp, up_full)
        hidden_rows, pull_gelu = jax.vjp(gelu_tanh, hidden_pre)
        hidden_low = hidden_rows.astype(bf16)
        down_branch, saved_hidden = project(hidden_low, down_full)
        block_rows.append((cross_stream + down_branch).astype(bf16))
        back = gather_weights(masters)
        back_skip, back_square, back_self, back_output, back_text, back_up, back_down = back
        upstream = cotangent[latent_index]
        grad_hidden, term_down = project_back(saved_hidden, upstream, back_down, True)
        total_down = accumulate(total_down, term_down)
        grad_pre = pull_gelu(grad_hidden)[0].astype(bf16)
        grad_mlp_in, term_up = project_back(saved_mlp, grad_pre, back_up, True)
        total_up = accumulate(total_up, term_up)
        grad_cross_part, grad_gain_mlp = pull_mlp_norm(grad_mlp_in)
        grad_cross_stream = upstream.astype(jnp.float32) + grad_cross_part
        cross_low = grad_cross_stream.astype(bf16)
        grad_cross_att_full, term_cross_out = project_back(
            saved_cross_att, cross_low, back_output[1], True
        )
        total_cross_out = accumulate(total_cross_out, term_cross_out)
        grad_cross_att = grad_cross_att_full.astype(bf16)
        grad_cross_q, grad_text_key, grad_text_value = attend_backward(
            cross_queries,
            text_key_all,
            text_value_all,
            valid_keys,
            cross_logsum,
            grad_cross_att,
            head_count,
        )
        grad_cross_linear = pull_cross_query(grad_cross_q)[0].astype(bf16)
        grad_cross_in, term_cross_query = project_back(
            saved_cross, grad_cross_linear, back_square[1], True
        )
        total_cross_query = accumulate(total_cross_query, term_cross_query)
        grad_self_part, grad_gain_cross = pull_cross_norm(grad_cross_in)
        grad_self_stream = grad_cross_stream + grad_self_part
        self_low = grad_self_stream.astype(bf16)
        grad_self_att_full, term_self_out = project_back(
            saved_attended, self_low, back_output[0], True
        )
        total_self_out = accumulate(total_self_out, term_self_out)
        grad_self_att = grad_self_att_full.astype(bf16)
        grad_query, grad_key_all, grad_value_all = attend_backward(
            queries, key_all, value_all, None, self_logsum, grad_self_att, head_count
        )
        grad_key_local, grad_value_local, grad_text_key_local, grad_text_value_local = (
            lax.psum_scatter(
                grad_key_all.astype(jnp.bfloat16), "fsdp", scatter_dimension=0, tiled=True
            ).astype(jnp.float32),
            lax.psum_scatter(
                grad_value_all.astype(jnp.bfloat16), "fsdp", scatter_dimension=0, tiled=True
            ).astype(jnp.float32),
            lax.psum_scatter(
                grad_text_key.astype(jnp.bfloat16), "fsdp", scatter_dimension=0, tiled=True
            ).astype(jnp.float32),
            lax.psum_scatter(
                grad_text_value.astype(jnp.bfloat16), "fsdp", scatter_dimension=0, tiled=True
            ).astype(jnp.float32),
        )
        grad_joint = jnp.concatenate(
            [pull_query(grad_query)[0], pull_key(grad_key_local)[0], grad_value_local], axis=-1
        ).astype(bf16)
        grad_self_in, term_self = project_back(saved_self, grad_joint, back_self, True)
        total_self = accumulate(total_self, term_self)
        grad_stream_part, grad_gain_self, grad_shift = pull_self_norm(grad_self_in)
        total_modulate = accumulate(total_modulate, shift_backward(embed_low, grad_shift))
        grad_stream = grad_self_stream + grad_stream_part
        stream_low = grad_stream.astype(bf16)
        grad_skip_in, term_skip = project_back(saved_skip, stream_low, back_skip, True)
        total_skip = accumulate(total_skip, term_skip)
        grad_joined, grad_gain_skip = pull_skip(grad_skip_in)
        input_grad_rows.append(grad_joined[:, :model_width].astype(bf16))
        skip_grad_rows.append(grad_joined[:, model_width:].astype(bf16))
        text_grad_joint = jnp.concatenate(
            [pull_text_key(grad_text_key_local)[0], grad_text_value_local], axis=-1
        ).astype(bf16)
        unused_grad, term_text = project_back(saved_text, text_grad_joint, back_text, False)
        total_text = accumulate(total_text, term_text)
        total_gains = total_gains + jnp.concatenate(
            [
                grad_gain_skip.reshape(2, -1),
                grad_gain_self[None],
                grad_gain_cross[None],
                grad_gain_mlp[None],
            ],
            axis=0,
        )
    square_total = jnp.stack([total_modulate, total_cross_query])
    output_total = jnp.stack([total_self_out, total_cross_out])
    part_fsdp = (
        lax.psum_scatter(
            total_skip.astype(jnp.bfloat16), "fsdp", scatter_dimension=1, tiled=True
        ).astype(jnp.float32),
        lax.psum_scatter(
            square_total.astype(jnp.bfloat16), "fsdp", scatter_dimension=2, tiled=True
        ).astype(jnp.float32),
        lax.psum_scatter(
            total_self.astype(jnp.bfloat16), "fsdp", scatter_dimension=1, tiled=True
        ).astype(jnp.float32),
        lax.psum_scatter(
            output_total.astype(jnp.bfloat16), "fsdp", scatter_dimension=2, tiled=True
        ).astype(jnp.float32),
        lax.psum_scatter(
            total_text.astype(jnp.bfloat16), "fsdp", scatter_dimension=1, tiled=True
        ).astype(jnp.float32),
        lax.psum_scatter(
            total_up.astype(jnp.bfloat16), "fsdp", scatter_dimension=1, tiled=True
        ).astype(jnp.float32),
        lax.psum_scatter(
            total_down.astype(jnp.bfloat16), "fsdp", scatter_dimension=1, tiled=True
        ).astype(jnp.float32),
    )
    grads = (
        lax.psum_scatter(part_fsdp[0], "dp", scatter_dimension=0, tiled=True),
        lax.psum_scatter(part_fsdp[1], "dp", scatter_dimension=1, tiled=True),
        lax.psum_scatter(part_fsdp[2], "dp", scatter_dimension=0, tiled=True),
        lax.psum_scatter(part_fsdp[3], "dp", scatter_dimension=1, tiled=True),
        lax.psum_scatter(part_fsdp[4], "dp", scatter_dimension=0, tiled=True),
        lax.psum_scatter(part_fsdp[5], "dp", scatter_dimension=0, tiled=True),
        lax.psum_scatter(part_fsdp[6], "dp", scatter_dimension=0, tiled=True),
    )
    dp_count = lax.axis_size("dp")
    fsdp_count = lax.axis_size("fsdp")
    master_slabs = [
        skip_weight[None],
        square_weight,
        self_weight[None],
        output_weight,
        text_weight[None],
        up_weight[None],
        down_weight[None],
    ]
    grad_slabs = [
        grads[0][None],
        grads[1],
        grads[2][None],
        grads[3],
        grads[4][None],
        grads[5][None],
        grads[6][None],
    ]
    row_slabs = [
        skip_rows[None],
        square_rows,
        self_rows[None],
        output_rows,
        text_rows[None],
        up_rows[None],
        down_rows[None],
    ]
    column_slabs = [
        skip_columns[None],
        square_columns,
        self_columns[None],
        output_columns,
        text_columns[None],
        up_columns[None],
        down_columns[None],
    ]
    squares = [gradient * gradient + EPS_SQUARE for gradient in grad_slabs]
    row_parts = [jnp.sum(square_block, axis=2) for square_block in squares]
    column_parts = [jnp.sum(square_block, axis=1) for square_block in squares]
    row_total = [part_now.shape[1] * dp_count for part_now in row_parts]
    column_total = [part_now.shape[1] * fsdp_count for part_now in column_parts]
    row_index = lax.axis_index("dp")
    column_index = lax.axis_index("fsdp")
    row_placed = [
        lax.dynamic_update_slice_in_dim(
            jnp.zeros((part_now.shape[0], height), jnp.float32),
            part_now,
            row_index * part_now.shape[1],
            1,
        )
        for part_now, height in zip(row_parts, row_total)
    ]
    column_placed = [
        lax.dynamic_update_slice_in_dim(
            jnp.zeros((part_now.shape[0], breadth), jnp.float32),
            part_now,
            column_index * part_now.shape[1],
            1,
        )
        for part_now, breadth in zip(column_parts, column_total)
    ]
    old_sums = jnp.concatenate([jnp.sum(state_now, axis=1) for state_now in row_slabs]) / fsdp_count
    joined_rows, joined_columns, gain_total, old_total = lax.psum(
        (flatten_all(row_placed), flatten_all(column_placed), total_gains, old_sums), ("dp", "fsdp")
    )
    row_full = split_all(joined_rows, [placed.shape for placed in row_placed])
    column_full = split_all(joined_columns, [placed.shape for placed in column_placed])
    rows_new = [
        DECAY * old_state
        + (1.0 - DECAY)
        * lax.dynamic_slice_in_dim(full_now, row_index * old_state.shape[1], old_state.shape[1], 1)
        / breadth
        for old_state, full_now, breadth in zip(row_slabs, row_full, column_total)
    ]
    column_sums = [
        lax.dynamic_slice_in_dim(full_now, column_index * old_state.shape[1], old_state.shape[1], 1)
        for full_now, old_state in zip(column_full, column_slabs)
    ]
    old_parts = split_all(old_total, [(state_now.shape[0],) for state_now in row_slabs])
    row_means = [
        (DECAY * old_part + (1.0 - DECAY) * jnp.sum(full_now, axis=1) / breadth) / height
        for old_part, full_now, breadth, height in zip(old_parts, row_full, column_total, row_total)
    ]
    columns_new = [
        DECAY * old_state + (1.0 - DECAY) * summed / height
        for old_state, summed, height in zip(column_slabs, column_sums, row_total)
    ]
    updates = [
        gradient
        * lax.rsqrt(state_row[:, :, None] * state_column[:, None, :] / mean_now[:, None, None])
        for gradient, state_row, state_column, mean_now in zip(
            grad_slabs, rows_new, columns_new, row_means
        )
    ]
    update_squares = jnp.concatenate([jnp.sum(update * update, axis=(1, 2)) for update in updates])
    master_squares = jnp.concatenate(
        [jnp.sum(master * master, axis=(1, 2)) for master in master_slabs]
    )
    update_all, master_all = lax.psum((update_squares, master_squares), ("dp", "fsdp"))
    slab_shapes = [(master.shape[0],) for master in master_slabs]
    update_split = split_all(update_all, slab_shapes)
    master_split = split_all(master_all, slab_shapes)
    new_masters = []
    for master, update, update_sum, master_sum, height, breadth in zip(
        master_slabs, updates, update_split, master_split, row_total, column_total
    ):
        entries = height * breadth
        ratio = jnp.sqrt(update_sum / entries) / CLIP
        step_scale = jnp.maximum(EPS_SCALE, jnp.sqrt(master_sum / entries))
        new_masters.append(
            master - (RATE * step_scale / jnp.maximum(1.0, ratio))[:, None, None] * update
        )
    gain_state_new = DECAY * gain_state + (1.0 - DECAY) * (gain_total * gain_total + EPS_SQUARE)
    gain_update = gain_total * lax.rsqrt(gain_state_new)
    gain_ratio = jnp.sqrt(jnp.mean(gain_update * gain_update)) / CLIP
    gain_scale = jnp.maximum(EPS_SCALE, jnp.sqrt(jnp.mean(norm_gains * norm_gains)))
    gains_new = norm_gains - RATE * gain_scale * gain_update / jnp.maximum(1.0, gain_ratio)
    return (
        jnp.stack(block_rows),
        jnp.stack(input_grad_rows),
        jnp.stack(skip_grad_rows),
        new_masters[0][0],
        rows_new[0][0],
        columns_new[0][0],
        grads[0],
        new_masters[1],
        rows_new[1],
        columns_new[1],
        grads[1],
        new_masters[2][0],
        rows_new[2][0],
        columns_new[2][0],
        grads[2],
        new_masters[3],
        rows_new[3],
        columns_new[3],
        grads[3],
        new_masters[4][0],
        rows_new[4][0],
        columns_new[4][0],
        grads[4],
        new_masters[5][0],
        rows_new[5][0],
        columns_new[5][0],
        grads[5],
        new_masters[6][0],
        rows_new[6][0],
        columns_new[6][0],
        grads[6],
        gains_new,
        gain_state_new,
        gain_total,
    )


def solution(mesh):
    return jax.shard_map(
        shards,
        mesh=mesh,
        in_specs=(
            P("dp", "fsdp", None),
            P("dp", "fsdp", None),
            P("dp", "fsdp", None),
            P("dp", "fsdp", None),
            P("dp"),
            P("dp"),
            P("dp", None, "fsdp"),
            P("dp", "fsdp"),
            P("dp"),
            P("fsdp"),
            P(None, "dp", "fsdp"),
            P(None, "dp"),
            P(None, "fsdp"),
            P("dp", "fsdp"),
            P("dp"),
            P("fsdp"),
            P(None, "dp", "fsdp"),
            P(None, "dp"),
            P(None, "fsdp"),
            P("dp", "fsdp"),
            P("dp"),
            P("fsdp"),
            P("dp", "fsdp"),
            P("dp"),
            P("fsdp"),
            P("dp", "fsdp"),
            P("dp"),
            P("fsdp"),
            P(),
            P(),
        ),
        out_specs=(
            P("dp", "fsdp", None),
            P("dp", "fsdp", None),
            P("dp", "fsdp", None),
            P("dp", "fsdp"),
            P("dp"),
            P("fsdp"),
            P("dp", "fsdp"),
            P(None, "dp", "fsdp"),
            P(None, "dp"),
            P(None, "fsdp"),
            P(None, "dp", "fsdp"),
            P("dp", "fsdp"),
            P("dp"),
            P("fsdp"),
            P("dp", "fsdp"),
            P(None, "dp", "fsdp"),
            P(None, "dp"),
            P(None, "fsdp"),
            P(None, "dp", "fsdp"),
            P("dp", "fsdp"),
            P("dp"),
            P("fsdp"),
            P("dp", "fsdp"),
            P("dp", "fsdp"),
            P("dp"),
            P("fsdp"),
            P("dp", "fsdp"),
            P("dp", "fsdp"),
            P("dp"),
            P("fsdp"),
            P("dp", "fsdp"),
            P(),
            P(),
            P(),
        ),
        check_vma=False,
    )
```

profile of v0, /device:TPU:0, one launch (start us, length us, event | category | flops | bytes accessed | tf_op | source)
XLA Modules:
  0.0 3744.7 jit_solution(17011898406879993042)
XLA Ops:
  11.6 11.8 all_gather.44
  26.8 13.4 all_gather.46
  51.8 8.8 all_gather.54
  67.4 88.1 %all-gather.20.cloned.1.call-done = bf16[2816,1408]{1,0:T(8,128)(2,1)} async-done(((bf16[352,1408]{1,0:T(8,128)(2,1)}), bf16[2816,1408]{1,0:T(8,128)(2,1)}) %all-gather.20.cloned.1.call-update) | async-done | bytes 7929872 | tf_op jit(solution)/shard_map/all_gather | solution.py:170
  161.1 114.7 %all-gather.22.cloned.1.call-done = bf16[2,1408,1408]{2,1,0:T(8,128)(2,1)} async-done(((bf16[2,176,1408]{2,1,0:T(8,128)(2,1)}), bf16[2,1408,1408]{2,1,0:T(8,128)(2,1)}) %all-gather.22.cloned.1.call-update) | async-done | bytes 7929872 | tf_op jit(solution)/shard_map/all_gather | solution.py:171
  278.6 165.5 %all-gather.24.cloned.1.call-done = bf16[1408,4224]{1,0:T(8,128)(2,1)} async-done(((bf16[176,4224]{1,0:T(8,128)(2,1)}), bf16[1408,4224]{1,0:T(8,128)(2,1)}) %all-gather.24.cloned.1.call-update) | async-done | bytes 11894800 | tf_op jit(solution)/shard_map/all_gather | solution.py:172
  474.9 20.3 all_gather.52
  509.5 83.9 %all-gather.32.cloned.1.call-done = bf16[1024,2816]{0,1:T(8,128)(2,1)} async-done(((bf16[128,2816]{0,1:T(8,128)(2,1)}), bf16[1024,2816]{0,1:T(8,128)(2,1)}) %all-gather.32.cloned.1.call-update) | async-done | bytes 5767184 | tf_op jit(solution)/shard_map/all_gather | solution.py:174
  598.9 16.0 all-gather.3
  630.1 11.6 all-gather.4
  652.9 15.0 all-gather.1
  683.0 10.3 all-gather.2
  725.2 64.6 %all-gather.30.cloned.1.call-done = bf16[2,1408,1408]{2,1,0:T(8,128)(2,1)} async-done(((bf16[2,176,1408]{2,1,0:T(8,128)(2,1)}), bf16[2,1408,1408]{2,1,0:T(8,128)(2,1)}) %all-gather.30.cloned.1.call-update) | async-done | bytes 7929872 | tf_op jit(solution)/shard_map/all_gather | solution.py:173
  796.0 13.0 all-gather.28.cloned.1.call-done
  833.5 310.1 %all-gather.36.cloned.1.call-done = bf16[1408,6144]{1,0:T(8,128)(2,1)} async-done(((bf16[176,6144]{1,0:T(8,128)(2,1)}), bf16[1408,6144]{1,0:T(8,128)(2,1)}) %all-gather.36.cloned.1.call-update) | async-done | bytes 17301520 | tf_op jit(solution)/shard_map/all_gather | solution.py:175
  1143.6 10.8 fusion.211
  1161.1 316.9 %all-gather.40.cloned.1.call-done = bf16[6144,1408]{0,1:T(8,128)(2,1)} async-done(((bf16[768,1408]{0,1:T(8,128)(2,1)}), bf16[6144,1408]{0,1:T(8,128)(2,1)}) %all-gather.40.cloned.1.call-update) | async-done | bytes 17301520 | tf_op jit(solution)/shard_map/all_gather | solution.py:176
  1478.0 13.3 fusion.30
  1491.3 12.9 fusion.251
  1504.2 13.0 fusion.23
  1517.2 14.2 multiply_reduce_fusion.15
  1635.4 50.1 %fusion.218 = (bf16[96,1408]{1,0:T(8,128)(2,1)}, bf16[96,1408]{1,0:T(8,128)(2,1)}, bf16[96,1408]{1,0:T(8,128)(2,1)S(1)}, bf16[96,1408]{1,0:T(8,128)(2,1)}) fusion(bf16[336,1408]{1,0:T(8,128)(2,1)S(1)} %copy-done.108, bf16[336,1408]{1,0:T(8,128)(2,1)S(1)} %copy-done.109, bf16[336,1408]{1,0:T(8,128)(2,1)} %copy.427, bf16[336,1408]{1,0:T(8,128)(2,1)} %copy.426), kind=kCustom, calls=%all-reduce-scatter.4 | all-reduce-scatter fusion | flops 2162689 | bytes 4866560
  1758.3 23.1 copy.419
  1803.7 9.5 fusion.112
  1829.3 21.9 copy.412
  1862.8 11.1 add_convert_fusion.3
  1874.6 12.6 fusion.113
  1887.3 15.0 add_convert_fusion.2
  1904.3 14.4 fusion.209
  1918.6 19.8 add_convert_fusion.1
  1939.6 18.5 fusion.120
  1958.1 19.7 add_convert_fusion
  1982.1 143.6 %all-reduce.61.cloned.1.call-done = (bf16[2,1408,1408]{1,0,2:T(2,128)(2,1)}, bf16[2,1408,1408]{1,0,2:T(2,128)(2,1)}) async-done(((bf16[2,1408,1408]{1,0,2:T(2,128)(2,1)}, bf16[2,1408,1408]{1,0,2:T(2,128)(2,1)}), (bf16[2,1408,1408]{1,0,2:T(2,128)(2,1)}, bf16[2,1408,1408]{1,0,2:T(2,128)(2,1)})) %all-reduce.61.cloned.1.call-update) | async-done | bytes 15859728
  2152.2 45.1 %reduce-scatter.35.cloned.1.call-done = bf16[2816,352]{0,1:T(8,128)(2,1)} async-done(((bf16[2816,1408]{0,1:T(8,128)(2,1)}), bf16[2816,352]{0,1:T(8,128)(2,1)}) %reduce-scatter.35.cloned.1.call-update) | async-done | bytes 1982480 | tf_op jit(solution)/shard_map/reduce_scatter | solution.py:417
  2201.7 92.8 %reduce-scatter.37.cloned.1.call-done = bf16[1408,1056]{0,1:T(8,128)(2,1)} async-done(((bf16[1408,4224]{0,1:T(8,128)(2,1)}), bf16[1408,1056]{0,1:T(8,128)(2,1)}) %reduce-scatter.37.cloned.1.call-update) | async-done | bytes 2973712 | tf_op jit(solution)/shard_map/reduce_scatter | solution.py:423
  2300.2 126.2 %reduce-scatter.43.cloned.1.call-done = bf16[1408,1536]{1,0:T(8,128)(2,1)} async-done(((bf16[1408,6144]{1,0:T(8,128)(2,1)}), bf16[1408,1536]{1,0:T(8,128)(2,1)}) %reduce-scatter.43.cloned.1.call-update) | async-done | bytes 4325392 | tf_op jit(solution)/shard_map/reduce_scatter | solution.py:432
  2433.3 125.1 %reduce-scatter.47.cloned.1.call-done = bf16[6144,352]{0,1:T(8,128)(2,1)} async-done(((bf16[6144,1408]{0,1:T(8,128)(2,1)}), bf16[6144,352]{0,1:T(8,128)(2,1)}) %reduce-scatter.47.cloned.1.call-update) | async-done | bytes 4325392 | tf_op jit(solution)/shard_map/reduce_scatter | solution.py:435
  2577.2 12.2 fusion.53
  2589.4 12.3 fusion.54
  2623.0 11.9 reduce-scatter.41.cloned.1.call-done
  2636.6 278.8 %all-reduce.59.cloned.1.call-done = (f32[2,1408,352]{2,0,1:T(2,128)}, f32[2,1408,352]{2,0,1:T(2,128)}) async-done(((f32[2,1408,352]{2,0,1:T(2,128)}, f32[2,1408,352]{2,0,1:T(2,128)}), (f32[2,1408,352]{2,0,1:T(2,128)}, f32[2,1408,352]{2,0,1:T(2,128)})) %all-reduce.59.cloned.1.call-update) | async-done | bytes 7929872
  2920.3 88.5 %reduce-scatter.59.cloned.1.call-done = f32[352,352]{1,0:T(8,128)} async-done(((f32[2816,352]{1,0:T(8,128)}), f32[352,352]{1,0:T(8,128)}) %reduce-scatter.59.cloned.1.call-update) | async-done | bytes 495632
  3011.0 123.0 %reduce-scatter.61.cloned.1.call-done = f32[176,1056]{1,0:T(8,128)} async-done(((f32[1408,1056]{1,0:T(8,128)}), f32[176,1056]{1,0:T(8,128)}) %reduce-scatter.61.cloned.1.call-update) | async-done | bytes 743440
  3136.5 154.8 %reduce-scatter.45.cloned.1.call-done = f32[176,1536]{1,0:T(8,128)} async-done(((f32[1408,1536]{1,0:T(8,128)}), f32[176,1536]{1,0:T(8,128)}) %reduce-scatter.45.cloned.1.call-update) | async-done | bytes 1081360 | tf_op jit(solution)/shard_map/reduce_scatter | solution.py:445
  3293.1 154.8 %reduce-scatter.49.cloned.1.call-done = f32[768,352]{0,1:T(8,128)} async-done(((f32[6144,352]{0,1:T(8,128)}), f32[768,352]{0,1:T(8,128)}) %reduce-scatter.49.cloned.1.call-update) | async-done | bytes 1081360 | tf_op jit(solution)/shard_map/reduce_scatter | solution.py:446
  3451.1 126.0 %all-reduce.57.cloned.1.call-done = (f32[18432]{0:T(1024)}, f32[21632]{0:T(1024)}) async-done(((f32[18432]{0:T(1024)}, f32[21632]{0:T(1024)}), (f32[18432]{0:T(1024)}, f32[21632]{0:T(1024)})) %all-reduce.57.cloned.1.call-update) | async-done | bytes 160272 | tf_op jit(solution)/shard_map/psum | solution.py:512
  3595.9 42.3 %psum.45 = f32[9]{0:T(128)S(1)} all-reduce(f32[9]{0:T(128)S(1)} %broadcast_multiply_fusion.8), channel_id=1, replica_groups=mesh['dp'=8,'fsdp'=4] {'dp','fsdp'}, use_global_device_ids=true, to_apply=%region_131.132 | all-reduce | flops 9 | bytes 72 | tf_op jit(solution)/shard_map/psum | solution.py:512
  3668.6 40.5 %all-reduce.48 = (f32[9]{0:T(128)S(1)}, f32[9]{0:T(128)S(1)}, f32[5,1408]{1,0:T(8,128)S(1)}) all-reduce(f32[9]{0:T(128)S(1)} %copy-done.344, f32[9]{0:T(128)S(1)} %concatenate.109, f32[5,1408]{1,0:T(8,128)S(1)} %maximum_add_fusion), channel_id=1, replica_groups=mesh['dp'=8,'fsdp'=4] {'dp','fsdp'}, use_global_device_ids=true, to_apply=%region_83.84 | all-reduce | flops 7058 | bytes 56464 | tf_op jit(solution)/shard_map/psum | solution.py:548
  (1341 shorter events, 584.0 us)
Async XLA Ops:
  7.2 36.1 all-gather.46.cloned.1.call-start
  10.2 145.3 %all-gather.20.cloned.1.call-start = ((), (), s32[]{:S(2)}) async-start(), calls=%async_computation.14 | async-start | bytes 8921088 | tf_op jit(solution)/shard_map/all_gather | solution.py:170
  25.3 250.5 %all-gather.22.cloned.1.call-start = ((), (), s32[]{:S(2)}) async-start(), calls=%async_computation.15 | async-start | bytes 8921088 | tf_op jit(solution)/shard_map/all_gather | solution.py:171
  43.3 400.8 %all-gather.24.cloned.1.call-start = ((), (), s32[]{:S(2)}) async-start(), calls=%async_computation.16 | async-start | bytes 13381632 | tf_op jit(solution)/shard_map/all_gather | solution.py:172
  47.7 456.3 %all-gather.34.cloned.1.call-start = ((), (), s32[]{:S(2)}) async-start(), calls=%async_computation.21 | async-start | bytes 2703360 | tf_op jit(solution)/shard_map/all_gather | solution.py:166
  49.4 455.4 %all-gather.38.cloned.1.call-start = ((), (), s32[]{:S(2)}) async-start(), calls=%async_computation.23 | async-start | bytes 2703360 | tf_op jit(solution)/shard_map/all_gather | solution.py:167
  51.1 542.3 %all-gather.32.cloned.1.call-start = ((), (), s32[]{:S(2)}) async-start(), calls=%async_computation.20 | async-start | bytes 6488064 | tf_op jit(solution)/shard_map/all_gather | solution.py:174
  60.7 653.5 %all-gather.42.cloned.1.call-start = ((), (), s32[]{:S(2)}) async-start(), calls=%async_computation.25 | async-start | bytes 1802240 | tf_op jit(solution)/shard_map/all_gather | solution.py:306
  66.6 1466.2 %copy-start.153 = (f32[1408]{0:T(1024)}, f32[1408]{0:T(1024)S(1)}, u32[]{:S(2)}) copy-start(f32[1408]{0:T(1024)S(1)} %get-tuple-element.340) | copy-start | bytes 16900
  160.3 629.5 %copy-start.34 = (f32[128,1408]{1,0:T(8,128)}, f32[128,1408]{1,0:T(8,128)S(1)}, u32[]{:S(2)}) copy-start(f32[128,1408]{1,0:T(8,128)S(1)} %get-tuple-element.592) | copy-start | bytes 2162692
  452.7 263.3 %all-gather.26.cloned.1.call-start = ((), (), s32[]{:S(2)}) async-start(), calls=%async_computation.17 | async-start | bytes 1802240 | tf_op jit(solution)/shard_map/all_gather | solution.py:306
  469.9 249.3 %all-gather.44.cloned.1.call-start = ((), (), s32[]{:S(2)}) async-start(), calls=%async_computation.26 | async-start | bytes 1802240 | tf_op jit(solution)/shard_map/all_gather | solution.py:305
  474.1 315.6 %all-gather.30.cloned.1.call-start = ((), (), s32[]{:S(2)}) async-start(), calls=%async_computation.19 | async-start | bytes 8921088 | tf_op jit(solution)/shard_map/all_gather | solution.py:173
  500.0 309.0 %all-gather.28.cloned.1.call-start = ((), (), s32[]{:S(2)}) async-start(), calls=%async_computation.18 | async-start | bytes 1802240 | tf_op jit(solution)/shard_map/all_gather | solution.py:305
  503.9 639.6 %all-gather.36.cloned.1.call-start = ((), (), s32[]{:S(2)}) async-start(), calls=%async_computation.22 | async-start | bytes 19464192 | tf_op jit(solution)/shard_map/all_gather | solution.py:175
  504.7 973.2 %all-gather.40.cloned.1.call-start = ((), (), s32[]{:S(2)}) async-start(), calls=%async_computation.24 | async-start | bytes 19464192 | tf_op jit(solution)/shard_map/all_gather | solution.py:176
  505.3 1289.6 %reduce-scatter.55.cloned.1.call-start = ((), (), s32[]{:S(2)}) async-start(), calls=%async_computation.38 | async-start | bytes 1802240
  1585.6 210.6 %reduce-scatter.51.cloned.1.call-start = ((), (), s32[]{:S(2)}) async-start(), calls=%async_computation.36 | async-start | bytes 1802240
  1603.7 193.9 %reduce-scatter.57.cloned.1.call-start = ((), (), s32[]{:S(2)}) async-start(), calls=%async_computation.39 | async-start | bytes 1802240
  1635.3 164.1 %reduce-scatter.53.cloned.1.call-start = ((), (), s32[]{:S(2)}) async-start(), calls=%async_computation.37 | async-start | bytes 1802240
  1686.5 25.6 collective-permute-start.2
  1702.5 27.6 collective-permute-start.3
  1706.3 28.6 collective-permute-start.1
  1709.8 7.8 collective-permute-start
  1711.9 266.0 %reduce-scatter.39.cloned.1.call-start = ((), (), s32[]{:S(2)}) async-start(), calls=%async_computation.29 | async-start | bytes 7208960 | tf_op jit(solution)/shard_map/reduce_scatter | solution.py:429
  1750.1 375.6 %all-reduce.61.cloned.1.call-start = ((), (), s32[]{:S(2)}) async-start(), calls=%async_computation.44 | async-start | bytes 31719424
  1851.3 346.0 %reduce-scatter.35.cloned.1.call-start = ((), (), s32[]{:S(2)}) async-start(), calls=%async_computation.27 | async-start | bytes 9912320 | tf_op jit(solution)/shard_map/reduce_scatter | solution.py:417
  1874.0 420.5 %reduce-scatter.37.cloned.1.call-start = ((), (), s32[]{:S(2)}) async-start(), calls=%async_computation.28 | async-start | bytes 14868480 | tf_op jit(solution)/shard_map/reduce_scatter | solution.py:423
  1902.4 524.1 %reduce-scatter.43.cloned.1.call-start = ((), (), s32[]{:S(2)}) async-start(), calls=%async_computation.31 | async-start | bytes 21626880 | tf_op jit(solution)/shard_map/reduce_scatter | solution.py:432
  1938.5 619.9 %reduce-scatter.47.cloned.1.call-start = ((), (), s32[]{:S(2)}) async-start(), calls=%async_computation.33 | async-start | bytes 21626880 | tf_op jit(solution)/shard_map/reduce_scatter | solution.py:435
  1977.8 657.0 %reduce-scatter.41.cloned.1.call-start = ((), (), s32[]{:S(2)}) async-start(), calls=%async_computation.30 | async-start | bytes 3244032 | tf_op jit(solution)/shard_map/reduce_scatter | solution.py:444
  1981.2 934.1 %all-reduce.59.cloned.1.call-start = ((), (), s32[]{:S(2)}) async-start(), calls=%async_computation.43 | async-start | bytes 17301504
  2152.2 856.6 %reduce-scatter.59.cloned.1.call-start = ((), (), s32[]{:S(2)}) async-start(), calls=%async_computation.40 | async-start | bytes 4866048
  2201.6 932.4 %reduce-scatter.61.cloned.1.call-start = ((), (), s32[]{:S(2)}) async-start(), calls=%async_computation.41 | async-start | bytes 7299072
  2300.1 991.1 %reduce-scatter.45.cloned.1.call-start = ((), (), s32[]{:S(2)}) async-start(), calls=%async_computation.32 | async-start | bytes 9732096 | tf_op jit(solution)/shard_map/reduce_scatter | solution.py:445
  2433.2 1014.7 %reduce-scatter.49.cloned.1.call-start = ((), (), s32[]{:S(2)}) async-start(), calls=%async_computation.34 | async-start | bytes 9732096 | tf_op jit(solution)/shard_map/reduce_scatter | solution.py:446
  2565.2 1011.9 %all-reduce.57.cloned.1.call-start = ((), (), s32[]{:S(2)}) async-start(), calls=%async_computation.42 | async-start | bytes 327680 | tf_op jit(solution)/shard_map/psum | solution.py:512
  3010.9 574.5 %copy-start.345 = (f32[352]{0:T(512)S(1)}, f32[352]{0:T(512)}, u32[]{:S(2)}) copy-start(f32[352]{0:T(512)} %param.38) | copy-start | bytes 4228
  3010.9 575.7 %copy-start.346 = (f32[2,176]{1,0:T(2,128)S(1)}, f32[2,176]{1,0:T(2,128)}, u32[]{:S(2)}) copy-start(f32[2,176]{1,0:T(2,128)} %param.41) | copy-start | bytes 4228
  3010.9 575.8 %copy-start.356 = (f32[176]{0:T(256)S(1)}, f32[176]{0:T(256)}, u32[]{:S(2)}) copy-start(f32[176]{0:T(256)} %param.44) | copy-start | bytes 2116
  3010.9 577.1 %copy-start.347 = (f32[2,176]{1,0:T(2,128)S(1)}, f32[2,176]{1,0:T(2,128)}, u32[]{:S(2)}) copy-start(f32[2,176]{1,0:T(2,128)} %param.47) | copy-start | bytes 4228
  3011.0 577.2 %copy-start.358 = (f32[128]{0:T(128)S(1)}, f32[128]{0:T(128)}, u32[]{:S(2)}) copy-start(f32[128]{0:T(128)} %param.50) | copy-start | bytes 1540
  3011.0 578.4 %copy-start.357 = (f32[176]{0:T(256)S(1)}, f32[176]{0:T(256)}, u32[]{:S(2)}) copy-start(f32[176]{0:T(256)} %param.53) | copy-start | bytes 2116
  3011.0 579.6 %copy-start.335 = (f32[768]{0:T(1024)S(1)}, f32[768]{0:T(1024)}, u32[]{:S(2)}) copy-start(f32[768]{0:T(1024)} %param.56) | copy-start | bytes 9220
  3135.5 511.0 %copy-start.336 = (f32[2,352]{1,0:T(2,128)S(1)}, f32[2,352]{1,0:T(2,128)}, u32[]{:S(2)}) copy-start(f32[2,352]{1,0:T(2,128)} %param.42) | copy-start | bytes 8452
  3135.5 511.6 %copy-start.308 = (f32[1056]{0:T(1024)S(1)}, f32[1056]{0:T(1024)}, u32[]{:S(2)}) copy-start(f32[1056]{0:T(1024)} %param.45) | copy-start | bytes 12676
  3135.5 511.7 %copy-start.337 = (f32[2,352]{1,0:T(2,128)S(1)}, f32[2,352]{1,0:T(2,128)}, u32[]{:S(2)}) copy-start(f32[2,352]{1,0:T(2,128)} %param.48) | copy-start | bytes 8452
  3135.5 513.1 %copy-start.334 = (f32[704]{0:T(1024)S(1)}, f32[704]{0:T(1024)}, u32[]{:S(2)}) copy-start(f32[704]{0:T(1024)} %param.51) | copy-start | bytes 8452
  (375 other events, 11040.3 us)
Sparse Core Ops, SparseCore 0:
  10.3 23.4 all-gather.45
  36.6 118.8 all-gather.19
  158.4 117.3 all-gather.21
  277.8 166.2 all-gather.23
  446.1 21.1 all-gather.33
  469.2 29.9 all-gather.37
  501.2 92.1 all-gather.31
  595.5 21.9 all-gather.41
  619.6 18.1 all-gather.25
  639.8 27.6 all-gather.43
  669.8 119.8 all-gather.29
  791.7 17.2 all-gather.27
  810.6 332.9 all-gather.35
  1145.0 332.9 all-gather.39
  1585.8 27.3 reduce-scatter.54
  1615.7 28.4 reduce-scatter.50
  1646.7 32.1 reduce-scatter.56
  1712.0 27.4 reduce-scatter.52
  1750.2 54.9 reduce-scatter.38
  1851.4 274.2 all-reduce.60
  2128.3 68.9 reduce-scatter.34
  2199.9 94.5 reduce-scatter.36
  2297.1 129.2 reduce-scatter.42
  2429.1 129.2 reduce-scatter.46
  2562.5 72.3 reduce-scatter.40
  2638.7 276.5 all-reduce.58
  2919.8 88.9 reduce-scatter.58
  3013.0 120.9 reduce-scatter.60
  3138.6 152.6 reduce-scatter.44
  3295.3 152.4 reduce-scatter.48
  3455.6 121.4 all-reduce.56
where the time goes:
time: 3760 us; the launch traced here: 3740 us
  waiting for transfers between devices  2630 us (70%)
  matrix products  379 us (10%)
  local copies, waits for them, and re-layouts  299 us (8%)
  blocking collectives  240 us (6%)
  other arithmetic  147 us (4%)
  between operations  38.8 us (1%)
    unnamed x43, waiting for transfers between devices  636 us
    all_gather x1, waiting for transfers between devices, gather_weights(): lax.all_gather(wider[6], 'dp', axis=0, tiled=True)  317 us
    all_gather x1, waiting for transfers between devices, gather_weights(): lax.all_gather(wider[5], 'dp', axis=0, tiled=True)  310 us
    all_gather x1, waiting for transfers between devices, gather_weights(): lax.all_gather(wider[2], 'dp', axis=0, tiled=True)  166 us
    reduce_scatter x1, waiting for transfers between devices, shards(): lax.psum_scatter(part_fsdp[5], 'dp', scatter_dimension=0, tiled=True)  155 us
    reduce_scatter x1, waiting for transfers between devices, shards(): lax.psum_scatter(part_fsdp[6], 'dp', scatter_dimension=0, tiled=True)  155 us
    dot_general x16, matrix products, matmul_left(): lax.dot_general(left, right, (((0,), (0,)), ((), ())), preferred_element_...  140 us
    reduce_scatter x1, waiting for transfers between devices, shards(): lax.psum_scatter(total_up.astype(jnp.bfloat16), 'fsdp', scatter_dimension...  126 us
  transfers between devices with their start and end apart: 35, of which 20 were waited for; matrix products, arithmetic and copies ran while one was open for 18% of the time, Pallas kernels for 0%

commit v1 on v0

v1 whole, which is shorter than its diff:
```python
import functools
import math

import jax
import jax.numpy as jnp
from jax import lax
from jax.experimental import pallas as pl
from jax.experimental.pallas import tpu as pltpu
from jax.sharding import PartitionSpec as P

D = 1408
HEADS = 16

EPS_NORM = 1e-06
EPS_SQUARE = 1e-30
EPS_SCALE = 0.001
DECAY = 0.5
CLIP = 1.0
RATE = 0.5

BF16 = jnp.bfloat16
F32 = jnp.float32


def matmul(left, right):
    return jnp.dot(left, right, preferred_element_type=F32)


def matmul_left(left, right):
    return lax.dot_general(left, right, (((0,), (0,)), ((), ())), preferred_element_type=F32)


def matmul_right(left, right):
    return lax.dot_general(left, right, (((1,), (1,)), ((), ())), preferred_element_type=F32)


def norm_rows(values):
    center = values - jnp.mean(values, axis=-1, keepdims=True)
    spread = jnp.mean(center * center, axis=-1, keepdims=True)
    return center * lax.rsqrt(spread + EPS_NORM)


def rotary(values, places):
    half_width = values.shape[-1] // 2
    quarter = half_width // 2
    frequency = jnp.exp(-math.log(10000.0) * jnp.arange(quarter).astype(F32) / quarter)
    pieces = []
    for member in range(2):
        block = values[..., member * half_width : (member + 1) * half_width]
        angles = places[member].astype(F32)[:, None] * frequency[None, :]
        cosine = jnp.cos(angles)[:, None, :]
        sine = jnp.sin(angles)[:, None, :]
        former = block[..., :quarter]
        latter = block[..., quarter:]
        pieces.append(former * cosine - latter * sine)
        pieces.append(latter * cosine + former * sine)
    return jnp.concatenate(pieces, axis=-1)


def time_embed(steps, model_width):
    half_width = model_width // 2
    frequency = jnp.exp(-math.log(10000.0) * jnp.arange(half_width).astype(F32) / half_width)
    angles = steps.astype(F32)[:, None] * frequency[None, :]
    return jnp.concatenate([jnp.cos(angles), jnp.sin(angles)], axis=-1)


def skip_norm(joined, gain_skip):
    return norm_rows(joined) * gain_skip


def modulated(stream, gain_row, shift_row):
    return norm_rows(stream) * gain_row + shift_row


def gained(stream, gain_row):
    return norm_rows(stream) * gain_row


def head_prep(linear, places):
    row_count = linear.shape[0]
    shaped = linear.reshape(row_count, HEADS, -1)
    return rotary(norm_rows(shaped), places).reshape(row_count, -1)


def head_norm(linear):
    row_count = linear.shape[0]
    return norm_rows(linear.reshape(row_count, HEADS, -1)).reshape(row_count, -1)


def gelu_tanh(values):
    return jax.nn.gelu(values, approximate=True)


def attend_scores(queries, key_rows, valid_keys):
    query_count = queries.shape[0]
    head_size = queries.shape[1] // HEADS
    shaped_query = queries.reshape(query_count, HEADS, head_size)
    shaped_keys = key_rows.reshape(key_rows.shape[0], HEADS, head_size)
    score_scale = 1.0 / math.sqrt(head_size)
    scores = jnp.einsum("qhd,khd->hqk", shaped_query, shaped_keys, preferred_element_type=F32) * score_scale
    if valid_keys is not None:
        scores = jnp.where(valid_keys[None, None, :], scores, -1e30)
    return scores, shaped_query, shaped_keys, score_scale


def attend_forward(queries, key_rows, value_rows, valid_keys):
    query_count = queries.shape[0]
    scores, _, _, _ = attend_scores(queries, key_rows, valid_keys)
    shaped_values = value_rows.reshape(value_rows.shape[0], HEADS, -1)
    row_top = jnp.max(scores, axis=-1, keepdims=True)
    logsum = row_top + jnp.log(jnp.sum(jnp.exp(scores - row_top), axis=-1, keepdims=True))
    weights_soft = jnp.exp(scores - logsum).astype(BF16)
    mixture = jnp.einsum("hqk,khd->qhd", weights_soft, shaped_values, preferred_element_type=F32)
    return mixture.reshape(query_count, -1).astype(BF16), logsum


def attend_backward(queries, key_rows, value_rows, valid_keys, logsum, grad_mixture):
    query_count = queries.shape[0]
    scores, shaped_query, shaped_keys, score_scale = attend_scores(queries, key_rows, valid_keys)
    shaped_values = value_rows.reshape(value_rows.shape[0], HEADS, -1)
    shaped_grad = grad_mixture.reshape(query_count, HEADS, -1)
    weights_full = jnp.exp(scores - logsum)
    weights_soft = weights_full.astype(BF16)
    grad_weights = jnp.einsum("qhd,khd->hqk", shaped_grad, shaped_values, preferred_element_type=F32)
    grad_values = jnp.einsum("hqk,qhd->khd", weights_soft, shaped_grad, preferred_element_type=F32)
    row_delta = jnp.sum(weights_full * grad_weights, axis=-1, keepdims=True)
    grad_scores = (weights_full * (grad_weights - row_delta)).astype(BF16)
    grad_queries = (
        jnp.einsum("hqk,khd->qhd", grad_scores, shaped_keys, preferred_element_type=F32) * score_scale
    )
    grad_keys = (
        jnp.einsum("hqk,qhd->khd", grad_scores, shaped_query, preferred_element_type=F32) * score_scale
    )
    key_count = key_rows.shape[0]
    return (
        grad_queries.reshape(query_count, -1),
        grad_keys.reshape(key_count, -1),
        grad_values.reshape(key_count, -1),
    )


def swap(value, axis, mask):
    size = lax.axis_size(axis)
    return lax.ppermute(value, axis, [(i, i ^ mask) for i in range(size)])


def masks_of(axis):
    size = lax.axis_size(axis)
    return [1 << b for b in range(size.bit_length() - 1)]


def butterfly(value, axis):
    for mask in masks_of(axis):
        value = value + swap(value, axis, mask)
    return value


CORE = ("fsdp", 1)
YAX = ("fsdp", 2)


class Slots:
    def __init__(self, rows):
        self.rows = rows
        self.size = -(-rows // 64) * 16
        self.offset = rows - 2 * self.size
        self.overlap = 4 * self.size - rows

    def start(self, index):
        return (index % 2) * self.offset + (index // 2) * self.size


def to_slot(block, slots):
    pieces = jnp.stack(
        [lax.slice_in_dim(block, slots.start(f), slots.start(f) + slots.size, axis=1) for f in range(4)]
    )
    got = lax.all_to_all(pieces, "fsdp", 0, 0, tiled=False)
    count, breadth = block.shape[0], block.shape[2]
    return jnp.transpose(got, (1, 2, 0, 3)).reshape(count, slots.size, 4 * breadth)


def from_slot(rows, slots):
    count, size, breadth = rows.shape
    pieces = jnp.transpose(rows.reshape(count, size, 4, breadth // 4), (2, 0, 1, 3))
    got = lax.all_to_all(pieces, "fsdp", 0, 0, tiled=False)
    return jnp.concatenate([got[0], got[2], got[1][:, slots.overlap :], got[3]], axis=1)


def staged(pairs, hold_ref, in_sems, out_sems):
    arrivals = [
        pltpu.make_async_copy(source, hold_ref.at[k], in_sems.at[k]) for k, (source, _, _) in enumerate(pairs)
    ]
    for copy in arrivals:
        copy.start()
    departures = []
    for k, (_, rows, target) in enumerate(pairs):
        arrivals[k].wait()
        held = hold_ref.at[k] if rows is None else hold_ref.at[k, :, rows, :]
        copy = pltpu.make_async_copy(held, target, out_sems.at[k])
        copy.start()
        departures.append(copy)
    for copy in departures:
        copy.wait()


def assemble_kernel(stages, slots, index_ref, own_ref, far_ref, out_ref, hold_ref, in_sems, out_sems):
    here_dp = index_ref[0]
    here_f = index_ref[1]
    half = 1 << len(stages)

    def pairs(f):
        made = []
        for side, ref in ((0, own_ref), (1, far_ref)):
            for k in range(half):
                dp_bits, f_bits = 0, side
                for j, (axis, mask) in enumerate(stages):
                    if (k >> j) & 1:
                        if axis == "dp":
                            dp_bits |= mask
                        else:
                            f_bits |= mask
                source_f = f ^ f_bits
                skip = slots.overlap if source_f == 1 else 0
                row = (here_dp ^ dp_bits) * slots.rows + slots.start(source_f) + skip
                row = pl.multiple_of(row, 16)
                size = slots.size - skip
                made.append((ref.at[k], pl.ds(skip, size), out_ref.at[:, pl.ds(row, size), :]))
        return made

    for f in range(4):

        @pl.when(here_f == f)
        def _():
            staged(pairs(f), hold_ref, in_sems, out_sems)


def assemble(index, own, far, stages, slots):
    half, count, size, breadth = own.shape
    total = lax.axis_size("dp") * slots.rows
    bytes_now = 2 * count * total * breadth
    return pl.pallas_call(
        functools.partial(assemble_kernel, stages, slots),
        out_shape=jax.ShapeDtypeStruct((count, total, breadth), own.dtype),
        in_specs=[
            pl.BlockSpec(memory_space=pltpu.SMEM),
            pl.BlockSpec(memory_space=pl.ANY),
            pl.BlockSpec(memory_space=pl.ANY),
        ],
        out_specs=pl.BlockSpec(memory_space=pl.ANY),
        scratch_shapes=[
            pltpu.VMEM((2 * half, count, size, breadth), own.dtype),
            pltpu.SemaphoreType.DMA((2 * half,)),
            pltpu.SemaphoreType.DMA((2 * half,)),
        ],
        compiler_params=pltpu.CompilerParams(vmem_limit_bytes=24 << 20),
        cost_estimate=pl.CostEstimate(flops=0, bytes_accessed=2 * bytes_now, transcendentals=0),
    )(index, own, far)


def place_kernel(stages, index_ref, own_ref, far_ref, out_ref, hold_ref, in_sems, out_sems):
    here_dp = index_ref[0]
    half = own_ref.shape[0]
    made = []
    for side, ref in ((0, own_ref), (1, far_ref)):
        for k in range(half):
            bits = 0
            for j, (_, mask) in enumerate(stages):
                if ((k + side * half) >> j) & 1:
                    bits |= mask
            made.append((ref.at[k], None, out_ref.at[here_dp ^ bits]))
    staged(made, hold_ref, in_sems, out_sems)


def place(index, own, far, stages):
    half, rows, breadth = own.shape
    return pl.pallas_call(
        functools.partial(place_kernel, stages),
        out_shape=jax.ShapeDtypeStruct((2 * half, rows, breadth), own.dtype),
        in_specs=[
            pl.BlockSpec(memory_space=pltpu.SMEM),
            pl.BlockSpec(memory_space=pl.ANY),
            pl.BlockSpec(memory_space=pl.ANY),
        ],
        out_specs=pl.BlockSpec(memory_space=pl.ANY),
        scratch_shapes=[
            pltpu.VMEM((2 * half, rows, breadth), own.dtype),
            pltpu.SemaphoreType.DMA((2 * half,)),
            pltpu.SemaphoreType.DMA((2 * half,)),
        ],
        compiler_params=pltpu.CompilerParams(vmem_limit_bytes=24 << 20),
        cost_estimate=pl.CostEstimate(flops=0, bytes_accessed=8 * half * rows * breadth, transcendentals=0),
    )(index, own, far)


def double(buffer, stages):
    for axis, mask in stages:
        buffer = jnp.concatenate([buffer, swap(buffer, axis, mask)], axis=0)
    return buffer


def gather_full(index, blocks, stages):
    block = blocks.astype(BF16)
    if not fits(block.shape[1]):
        wide = lax.all_gather(block, "fsdp", axis=2, tiled=True)
        return lax.all_gather(wide, "dp", axis=1, tiled=True)
    slots = Slots(block.shape[1])
    own = double(to_slot(block, slots)[None], stages)
    far = swap(own, *CORE)
    return assemble(index, own, far, stages, slots)


def fits(rows):
    return rows % 16 == 0 and rows >= 64


def gather_dp(index, block, stages):
    if not fits(block.shape[0]):
        return lax.all_gather(block, "dp", axis=0, tiled=False)
    own = double(block[None], stages[:-1])
    far = swap(own, *stages[-1])
    return place(index, own, far, stages)


def total_of(parts):
    value = parts[0].astype(F32)
    for part in parts[1:]:
        value = value + part.astype(F32)
    return value


def halve(parts, axis, mask, choose):
    bit = (lax.axis_index(axis) // mask) % 2
    send = total_of([choose(part, 1 - bit) for part in parts]).astype(BF16)
    received = swap(send, axis, mask)
    return [choose(part, bit) for part in parts] + [received]


def dp_dims(size):
    return (2,) * (size.bit_length() - 1)


def reduce_dp_step(parts, dims_left, mask):
    place_now = dims_left.index(mask)

    def choose(part, bit):
        return lax.dynamic_index_in_dim(part, bit, axis=place_now, keepdims=False)

    left = [other for other in dims_left if other != mask]
    return halve(parts, "dp", mask, choose), left


def reduce_full(gradient, stages):
    count, height, breadth = gradient.shape
    dp = lax.axis_size("dp")
    rows = height // dp
    if not fits(rows):
        low = gradient.astype(BF16)
        thin = lax.psum_scatter(low, "fsdp", scatter_dimension=2, tiled=True)
        return lax.psum_scatter(thin.astype(F32), "dp", scatter_dimension=1, tiled=True)
    slots = Slots(rows)
    dims_left = masks_of("dp")[::-1]
    shaped = gradient.reshape((count,) + dp_dims(dp) + (rows, breadth))
    shaped = jnp.moveaxis(shaped, 0, -3)
    parts = [shaped]

    for axis, mask in stages:
        if axis == "dp":
            parts, dims_left = reduce_dp_step(parts, dims_left, mask)
        else:
            step, size = (slots.offset, 2 * slots.size) if mask == 1 else (slots.size, slots.size)

            def choose(part, bit):
                return lax.dynamic_slice_in_dim(part, bit * step, size, axis=part.ndim - 2)

            parts = halve(parts, axis, mask, choose)
    return from_slot(total_of(parts).astype(BF16), slots).astype(F32)


def reduce_dp(gradient, stages):
    dp, rows, breadth = gradient.shape
    if not fits(rows):
        return lax.psum_scatter(gradient.astype(F32), "dp", scatter_dimension=0, tiled=False)
    dims_left = masks_of("dp")[::-1]
    parts = [gradient.reshape(dp_dims(dp) + (rows, breadth))]
    for _, mask in stages:
        parts, dims_left = reduce_dp_step(parts, dims_left, mask)
    return total_of(parts)


def spread_tokens(rows):
    pair = jnp.concatenate([rows, swap(rows, *YAX)], axis=0)
    return jnp.concatenate([pair, swap(pair, *CORE)], axis=0)


def collect_tokens(partial):
    half = partial.shape[0] // 2
    pair = partial[:half] + swap(partial[half:].astype(BF16), *CORE).astype(F32)
    quarter = half // 2
    return pair[:quarter] + swap(pair[quarter:].astype(BF16), *YAX).astype(F32)


def pick(pair, bit):
    return lax.dynamic_index_in_dim(pair, bit, axis=0, keepdims=False)


def to_latent(pair, y):
    return jnp.concatenate([pick(pair, y), swap(pick(pair, 1 - y), *YAX)], axis=0)


def from_latent(rows, y):
    half = rows.shape[0] // 2
    own = rows[:half]
    other = swap(rows[half:], *YAX)
    return jnp.where(y == 0, jnp.stack([own, other]), jnp.stack([other, own]))


def flatten_all(arrays):
    return jnp.concatenate([matrix.reshape(-1) for matrix in arrays])


def split_all(vector, shapes):
    pieces = []
    offset = 0
    for shape_now in shapes:
        count_now = math.prod(shape_now)
        pieces.append(vector[offset : offset + count_now].reshape(shape_now))
        offset = offset + count_now
    return pieces


def shards(
    latents,
    skip_input,
    text_tokens,
    cotangent,
    timesteps,
    text_lengths,
    positions,
    skip_weight,
    skip_rows,
    skip_columns,
    square_weight,
    square_rows,
    square_columns,
    self_weight,
    self_rows,
    self_columns,
    output_weight,
    output_rows,
    output_columns,
    text_weight,
    text_rows,
    text_columns,
    up_weight,
    up_rows,
    up_columns,
    down_weight,
    down_rows,
    down_columns,
    norm_gains,
    gain_state,
):
    dp = lax.axis_size("dp")
    d_at = lax.axis_index("dp")
    f_at = lax.axis_index("fsdp")
    y_at = f_at // 2
    c_at = f_at % 2
    index = jnp.stack([d_at, f_at]).astype(jnp.int32)

    dp_masks = masks_of("dp")
    high = [("dp", mask) for mask in dp_masks if mask > 1]
    low = ("dp", 1)
    order_a = high + [YAX, low]
    order_b = high + [low, YAX]
    order_m = high + [low]
    back_a = [CORE] + order_a[::-1]
    back_b = [CORE] + order_b[::-1]
    back_m = order_m[::-1]

    joined = jnp.concatenate([to_latent(latents, y_at), to_latent(skip_input, y_at)], axis=-1).astype(F32)
    upstream = to_latent(cotangent, y_at)
    text_local = to_latent(text_tokens, y_at)
    places = to_latent(jnp.swapaxes(positions, 1, 2), y_at).T
    text_count = pick(text_lengths, y_at)

    skip_full = gather_full(index, skip_weight[None], order_a)[0]
    self_full = gather_full(index, self_weight[None], order_b)[0]
    text_full = gather_full(index, text_weight[None], order_a)[0]
    cross_full = gather_full(
        index, jnp.stack([output_weight[0], square_weight[1], output_weight[1]]), order_b
    )
    out_self, square_cross, out_cross = cross_full[0], cross_full[1], cross_full[2]
    rows_d = up_weight.shape[0]
    chunk = down_weight.shape[0] // 4
    per_f = up_weight.shape[1] // (4 * chunk)
    up_pieces = jnp.transpose(up_weight.astype(BF16).reshape(rows_d, per_f, 4, chunk), (2, 0, 1, 3))
    up_got = lax.all_to_all(up_pieces, "fsdp", 0, 0, tiled=False)
    up_block = jnp.transpose(up_got, (1, 0, 2, 3)).reshape(rows_d, 4 * per_f * chunk)
    up_full = gather_dp(index, up_block, order_m).reshape(dp * rows_d, -1)
    down_got = lax.all_to_all(
        down_weight.astype(BF16).reshape(4, chunk, -1), "fsdp", 0, 0, tiled=False
    )
    down_block = jnp.transpose(down_got, (1, 0, 2)).reshape(chunk, D)
    down_full = gather_dp(index, down_block, order_m).reshape(dp * chunk, D)

    steps = double(timesteps[None], [("dp", mask) for mask in dp_masks])
    embed_all = jax.nn.silu(time_embed(steps.reshape(-1), D)).astype(BF16)
    rows_q = square_weight.shape[1]
    columns_q = square_weight.shape[2]
    embed_part = lax.dynamic_slice_in_dim(embed_all, d_at * rows_q, rows_q, axis=1)
    shift_parts = matmul(embed_part, square_weight[0].astype(BF16)).reshape(dp, 2, columns_q)
    for mask in dp_masks[::-1]:
        shift_parts = shift_parts[:mask] + swap(shift_parts[mask:], "dp", mask)
    shift_mine = shift_parts[0]
    shift_four = double(shift_mine[None], [CORE, YAX])
    shift_four = jnp.stack([pick(shift_four, f_at ^ f) for f in range(4)])
    shift_row = pick(jnp.swapaxes(shift_four, 0, 1), y_at).reshape(1, D)

    normed_skip, pull_skip = jax.vjp(skip_norm, joined, norm_gains[0:2].reshape(-1))
    lowered_skip = normed_skip.astype(BF16)
    stream = matmul(lowered_skip, skip_full)
    normed_self, pull_self_norm = jax.vjp(modulated, stream, norm_gains[2], shift_row)
    lowered_self = normed_self.astype(BF16)
    joint = matmul(lowered_self, self_full)

    def prepare(linear):
        return head_prep(linear, places)

    query_rows, pull_query = jax.vjp(prepare, joint[:, :D])
    key_local, pull_key = jax.vjp(prepare, joint[:, D : 2 * D])
    queries = query_rows.astype(BF16)
    key_value = jnp.stack([key_local.astype(BF16), joint[:, 2 * D :].astype(BF16)])
    key_value = jnp.concatenate([key_value, swap(key_value, *CORE)], axis=1)
    key_all, value_all = key_value[0], key_value[1]

    text_joint = matmul(text_local, text_full)
    text_key_local, pull_text_key = jax.vjp(head_norm, text_joint[:, :D])
    text_kv = jnp.stack([text_key_local.astype(BF16), text_joint[:, D:].astype(BF16)])
    text_kv = jnp.concatenate([text_kv, swap(text_kv, *CORE)], axis=1)
    text_key_all, text_value_all = text_kv[0], text_kv[1]

    attended, self_logsum = attend_forward(queries, key_all, value_all, None)
    self_stream = stream + matmul(attended, out_self)
    normed_cross, pull_cross_norm = jax.vjp(gained, self_stream, norm_gains[3])
    lowered_cross = normed_cross.astype(BF16)
    cross_linear = matmul(lowered_cross, square_cross)
    cross_query_rows, pull_cross_query = jax.vjp(prepare, cross_linear)
    cross_queries = cross_query_rows.astype(BF16)
    own_text = text_tokens.shape[1]
    text_slots = jnp.concatenate(
        [(f_at ^ mask) * own_text + jnp.arange(own_text) for mask in (0, 2, 1, 3)]
    )
    valid_keys = text_slots < text_count
    cross_attended, cross_logsum = attend_forward(cross_queries, text_key_all, text_value_all, valid_keys)
    cross_stream = self_stream + matmul(cross_attended, out_cross)
    normed_mlp, pull_mlp_norm = jax.vjp(gained, cross_stream, norm_gains[4])
    lowered_mlp = spread_tokens(normed_mlp.astype(BF16))
    hidden_pre = matmul(lowered_mlp, up_full)
    hidden_rows, pull_gelu = jax.vjp(gelu_tanh, hidden_pre)
    hidden_low = hidden_rows.astype(BF16)
    block_rows = (cross_stream + collect_tokens(matmul(hidden_low, down_full))).astype(BF16)
    block_output = from_latent(block_rows, y_at)

    upstream_all = spread_tokens(upstream)
    grad_hidden = matmul_right(upstream_all, down_full)
    grad_pre = pull_gelu(grad_hidden)[0].astype(BF16)
    grad_mlp_in = collect_tokens(matmul_right(grad_pre, up_full))
    term_down = matmul_left(hidden_low, upstream_all).astype(BF16)
    term_up = matmul_left(lowered_mlp, grad_pre).astype(BF16)
    down_rows_sum = reduce_dp(term_down.reshape(dp, chunk, D), back_m)
    up_rows_sum = reduce_dp(term_up.reshape(dp, rows_d, -1), back_m)

    grad_cross_part, grad_gain_mlp = pull_mlp_norm(grad_mlp_in)
    grad_cross_stream = upstream.astype(F32) + grad_cross_part
    cross_low = grad_cross_stream.astype(BF16)
    grad_cross_att = matmul_right(cross_low, out_cross).astype(BF16)
    term_cross_out = matmul_left(cross_attended, cross_low).astype(BF16)
    grad_cross_q, grad_text_key, grad_text_value = attend_backward(
        cross_queries, text_key_all, text_value_all, valid_keys, cross_logsum, grad_cross_att
    )
    grad_text_kv = jnp.stack([grad_text_key, grad_text_value])
    text_half = grad_text_kv.shape[1] // 2
    grad_text_local = grad_text_kv[:, :text_half] + swap(
        grad_text_kv[:, text_half:].astype(BF16), *CORE
    ).astype(F32)
    grad_cross_linear = pull_cross_query(grad_cross_q)[0].astype(BF16)
    grad_cross_in = matmul_right(grad_cross_linear, square_cross)
    term_cross_query = matmul_left(lowered_cross, grad_cross_linear).astype(BF16)
    grad_self_part, grad_gain_cross = pull_cross_norm(grad_cross_in)
    grad_self_stream = grad_cross_stream + grad_self_part
    self_low = grad_self_stream.astype(BF16)
    grad_self_att = matmul_right(self_low, out_self).astype(BF16)
    term_self_out = matmul_left(attended, self_low).astype(BF16)
    cross_sum = reduce_full(jnp.stack([term_self_out, term_cross_query, term_cross_out]), back_b)
    text_grad_joint = jnp.concatenate(
        [pull_text_key(grad_text_local[0])[0], grad_text_local[1]], axis=-1
    ).astype(BF16)
    text_sum = reduce_full(matmul_left(text_local, text_grad_joint).astype(BF16)[None], back_a)

    grad_query, grad_key_all, grad_value_all = attend_backward(
        queries, key_all, value_all, None, self_logsum, grad_self_att
    )
    grad_kv = jnp.stack([grad_key_all, grad_value_all])
    token_half = grad_kv.shape[1] // 2
    grad_kv_local = grad_kv[:, :token_half] + swap(grad_kv[:, token_half:].astype(BF16), *CORE).astype(F32)
    grad_joint = jnp.concatenate(
        [pull_query(grad_query)[0], pull_key(grad_kv_local[0])[0], grad_kv_local[1]], axis=-1
    ).astype(BF16)
    self_sum = reduce_full(matmul_left(lowered_self, grad_joint).astype(BF16)[None], back_b)
    grad_self_in = matmul_right(grad_joint, self_full)
    grad_stream_part, grad_gain_self, grad_shift = pull_self_norm(grad_self_in)
    grad_stream = grad_self_stream + grad_stream_part
    stream_low = grad_stream.astype(BF16)
    skip_sum = reduce_full(matmul_left(lowered_skip, stream_low).astype(BF16)[None], back_a)
    grad_joined, grad_gain_skip = pull_skip(matmul_right(stream_low, skip_full))
    latents_grad = from_latent(grad_joined[:, :D].astype(BF16), y_at)
    skip_input_grad = from_latent(grad_joined[:, D:].astype(BF16), y_at)

    grad_shift = grad_shift.reshape(1, D)
    grad_shift = grad_shift + swap(grad_shift, *CORE)
    other_shift = swap(grad_shift, *YAX)
    shift_pair = jnp.where(
        y_at == 0,
        jnp.concatenate([grad_shift, other_shift]),
        jnp.concatenate([other_shift, grad_shift]),
    )
    shift_pair = lax.dynamic_slice_in_dim(shift_pair, f_at * columns_q, columns_q, axis=1)
    shift_grads = double(shift_pair[None], [("dp", mask) for mask in dp_masks]).reshape(-1, columns_q)
    modulate_sum = lax.dot_general(
        embed_part.astype(F32),
        shift_grads,
        (((0,), (0,)), ((), ())),
        precision=lax.Precision.HIGHEST,
        preferred_element_type=F32,
    )

    up_back = jnp.transpose(
        up_rows_sum.astype(BF16).reshape(rows_d, 4, per_f, chunk), (1, 0, 2, 3)
    )
    up_back = lax.all_to_all(up_back, "fsdp", 0, 0, tiled=False)
    up_sum = jnp.transpose(up_back, (1, 2, 0, 3)).reshape(up_weight.shape).astype(F32)
    down_back = jnp.transpose(down_rows_sum.astype(BF16).reshape(chunk, 4, -1), (1, 0, 2))
    down_back = lax.all_to_all(down_back, "fsdp", 0, 0, tiled=False)
    down_sum = down_back.reshape(down_weight.shape).astype(F32)

    fsdp = lax.axis_size("fsdp")
    master_slabs = [
        skip_weight[None],
        square_weight,
        self_weight[None],
        output_weight,
        text_weight[None],
        up_weight[None],
        down_weight[None],
    ]
    grad_slabs = [
        skip_sum,
        jnp.stack([modulate_sum, cross_sum[1]]),
        self_sum,
        jnp.stack([cross_sum[0], cross_sum[2]]),
        text_sum,
        up_sum[None],
        down_sum[None],
    ]
    row_slabs = [
        skip_rows[None],
        square_rows,
        self_rows[None],
        output_rows,
        text_rows[None],
        up_rows[None],
        down_rows[None],
    ]
    column_slabs = [
        skip_columns[None],
        square_columns,
        self_columns[None],
        output_columns,
        text_columns[None],
        up_columns[None],
        down_columns[None],
    ]
    squares = [gradient * gradient + EPS_SQUARE for gradient in grad_slabs]
    row_parts = [jnp.sum(square_block, axis=2) for square_block in squares]
    column_parts = [jnp.sum(square_block, axis=1) for square_block in squares]
    heights = [part.shape[1] * dp for part in row_parts]
    breadths = [part.shape[1] * fsdp for part in column_parts]
    gains_part = jnp.concatenate(
        [grad_gain_skip.reshape(2, -1), grad_gain_self[None], grad_gain_cross[None], grad_gain_mlp[None]],
        axis=0,
    )
    old_sums = jnp.concatenate([jnp.sum(state, axis=1) for state in row_slabs])
    master_squares = jnp.concatenate([jnp.sum(master * master, axis=(1, 2)) for master in master_slabs])
    early = butterfly(jnp.concatenate([old_sums / fsdp, master_squares]), "fsdp")
    early = butterfly(early, "dp")
    matrix_count = old_sums.shape[0]
    old_total, master_all = early[:matrix_count], early[matrix_count:]

    rows_vector = butterfly(flatten_all(row_parts), "fsdp")
    row_sums = split_all(rows_vector, [part.shape for part in row_parts])
    square_sums = jnp.concatenate([jnp.sum(part, axis=1) for part in row_sums])
    column_shapes = [part.shape for part in column_parts]
    columns_vector = butterfly(
        flatten_all(column_parts + [square_sums, gains_part]), "dp"
    )
    column_all = split_all(columns_vector, column_shapes + [square_sums.shape, gains_part.shape])
    column_sums, square_total, gain_half = column_all[:-2], column_all[-2], column_all[-1]
    gain_total = butterfly(gain_half, "fsdp")

    slab_counts = [(part.shape[0],) for part in row_parts]
    rows_new = [
        DECAY * old_state + (1.0 - DECAY) * summed / breadth
        for old_state, summed, breadth in zip(row_slabs, row_sums, breadths)
    ]
    columns_new = [
        DECAY * old_state + (1.0 - DECAY) * summed / height
        for old_state, summed, height in zip(column_slabs, column_sums, heights)
    ]
    row_means = [
        (DECAY * old_part + (1.0 - DECAY) * square_part / breadth) / height
        for old_part, square_part, breadth, height in zip(
            split_all(old_total, slab_counts), split_all(square_total, slab_counts), breadths, heights
        )
    ]
    updates = [
        gradient * lax.rsqrt(state_row[:, :, None] * state_column[:, None, :] / mean_now[:, None, None])
        for gradient, state_row, state_column, mean_now in zip(grad_slabs, rows_new, columns_new, row_means)
    ]
    update_squares = jnp.concatenate([jnp.sum(update * update, axis=(1, 2)) for update in updates])
    update_all = butterfly(butterfly(update_squares, "fsdp"), "dp")
    new_masters = []
    for master, update, update_sum, master_sum, height, breadth in zip(
        master_slabs,
        updates,
        split_all(update_all, slab_counts),
        split_all(master_all, slab_counts),
        heights,
        breadths,
    ):
        entries = height * breadth
        ratio = jnp.sqrt(update_sum / entries) / CLIP
        step_scale = jnp.maximum(EPS_SCALE, jnp.sqrt(master_sum / entries))
        new_masters.append(
            master - (RATE * step_scale / jnp.maximum(1.0, ratio))[:, None, None] * update
        )
    gain_state_new = DECAY * gain_state + (1.0 - DECAY) * (gain_total * gain_total + EPS_SQUARE)
    gain_update = gain_total * lax.rsqrt(gain_state_new)
    gain_ratio = jnp.sqrt(jnp.mean(gain_update * gain_update)) / CLIP
    gain_scale = jnp.maximum(EPS_SCALE, jnp.sqrt(jnp.mean(norm_gains * norm_gains)))
    gains_new = norm_gains - RATE * gain_scale * gain_update / jnp.maximum(1.0, gain_ratio)
    results = [block_output, latents_grad, skip_input_grad]
    for which in range(7):
        group = [new_masters[which], rows_new[which], columns_new[which], grad_slabs[which]]
        if which in (1, 3):
            results.extend(group)
        else:
            results.extend(item[0] for item in group)
    return tuple(results) + (gains_new, gain_state_new, gain_total)


def solution(mesh):
    matrix, row, column = P("dp", "fsdp"), P("dp"), P("fsdp")
    pair, pair_row, pair_column = P(None, "dp", "fsdp"), P(None, "dp"), P(None, "fsdp")
    tokens = P("dp", "fsdp", None)
    kinds = (False, True, False, True, False, False, False)
    in_specs = [tokens] * 4 + [P("dp"), P("dp"), P("dp", None, "fsdp")]
    out_specs = [tokens] * 3
    for paired in kinds:
        if paired:
            in_specs += [pair, pair_row, pair_column]
            out_specs += [pair, pair_row, pair_column, pair]
        else:
            in_specs += [matrix, row, column]
            out_specs += [matrix, row, column, matrix]
    return jax.shard_map(
        shards,
        mesh=mesh,
        in_specs=tuple(in_specs + [P(), P()]),
        out_specs=tuple(out_specs + [P(), P(), P()]),
        check_vma=False,
    )
```

time: 3760 us -> 1410 us (0.38)
  waiting for transfers between devices: 2630 us -> 574 us
  blocking collectives: 240 us -> 0 us
  matrix products: 379 us -> 148 us
  starting transfers between devices: 11.2 us -> 137 us
  other arithmetic: 147 us -> 238 us
  local copies, waits for them, and re-layouts: 299 us -> 237 us
  Pallas kernels: 0 us -> 42.5 us
    all_gather x14 -> x0, waiting for transfers between devices: 1160 us -> none  [the longest x1 317 us: gather_weights(): lax.all_gather(wider[6], 'dp', axis=0, tiled=True)]
    reduce_scatter x8 -> x0, waiting for transfers between devices: 711 us -> none  [the longest x1 155 us: shards(): lax.psum_scatter(part_fsdp[5], 'dp', scatter_dimension=0, tiled=True)]
    unnamed x43 -> x0, waiting for transfers between devices: 636 us -> none
    ppermute x0 -> x102, waiting for transfers between devices: none -> 540 us  [swap(): return lax.ppermute(value, axis, [(i, i ^ mask) for i in range(size)])]
    psum x1 -> x0, waiting for transfers between devices: 126 us -> none  [shards(): lax.psum((flatten_all(row_placed), flatten_all(column_placed), total_gain...]
    all_gather x8 -> x0, blocking collectives: 107 us -> none  [the longest x2 31 us: shards(): lax.all_gather(text_joint[:, model_width:].astype(bf16), 'fsdp', axis=0,...]
    dot_general x16 -> x8, matrix products: 140 us -> 41.4 us  [matmul_left(): lax.dot_general(left, right, (((0,), (0,)), ((), ())), preferred_element_...]
    ppermute x0 -> x102, starting transfers between devices: none -> 92.9 us  [swap(): return lax.ppermute(value, axis, [(i, i ^ mask) for i in range(size)])]
  transfers between devices with their start and end apart: 35 -> 114, of which waited for: 20 -> 49; matrix products, arithmetic and copies ran while one was open for 18% -> 40% of each run, Pallas kernels for 0% -> 3%
where the time goes in v1:
time: 1410 us; the launch traced here: 1400 us
  waiting for transfers between devices  574 us (41%)
  other arithmetic  238 us (17%)
  local copies, waits for them, and re-layouts  237 us (17%)
  matrix products  148 us (10%)
  starting transfers between devices  137 us (10%)
  Pallas kernels  42.5 us (3%)
  between operations  19.8 us (1%)
    ppermute x102, waiting for transfers between devices, swap(): return lax.ppermute(value, axis, [(i, i ^ mask) for i in range(size)])  540 us
    ppermute x102, starting transfers between devices, swap(): return lax.ppermute(value, axis, [(i, i ^ mask) for i in range(size)])  92.9 us
    unnamed x552, local copies, waits for them, and re-layouts  77.8 us
    convert_element_type x20, other arithmetic, halve(): send = total_of([choose(part, 1 - bit) for part in parts]).astype(BF16)  65.4 us
    dot_general x8, matrix products, matmul_left(): lax.dot_general(left, right, (((0,), (0,)), ((), ())), preferred_element_...  41.4 us
    dot_general x7, matrix products, matmul_right(): lax.dot_general(left, right, (((1,), (1,)), ((), ())), preferred_element_...  39.5 us
    pallas_call x4, Pallas kernels, assemble(): pl.pallas_call(functools.partial(assemble_kernel, stages, slots), out_sha...  37.1 us
    dot_general x9, matrix products, matmul(): return jnp.dot(left, right, preferred_element_type=F32)  32.4 us
  transfers between devices with their start and end apart: 114, of which 49 were waited for; matrix products, arithmetic and copies ran while one was open for 40% of the time, Pallas kernels for 3%

profile of v1, /device:TPU:0, one launch (start us, length us, event | category | flops | bytes accessed | tf_op | source)
XLA Modules:
  0.0 1397.6 jit_solution(10880750618990149693)
XLA Ops:
  67.2 4.6 all-to-all-done
  90.2 5.2 all-to-all-done.1
  118.9 7.6 all-to-all-done.4
  143.4 44.2 %collective-permute-done.16 = bf16[2,1,48,4224]{3,2,1,0:T(8,128)(2,1)S(1)} collective-permute-done((bf16[2,1,48,4224]{3,2,1,0:T(8,128)(2,1)S(1)}, bf16[2,1,48,4224]{3,2,1,0:T(8,128)(2,1)S(1)}, u32[]{:S(2)}, u32[]{:S(2)}) %collective-permute-start.16) | collective-permute-done | bytes 811040 | tf_op jit(solution)/shard_map/ppermute | solution.py:144
  195.6 20.9 %collective-permute-done.3 = bf16[2,1,96,1408]{3,2,1,0:T(8,128)(2,1)S(1)} collective-permute-done((bf16[2,1,96,1408]{3,2,1,0:T(8,128)(2,1)S(1)}, bf16[2,1,96,1408]{3,2,1,0:T(8,128)(2,1)S(1)}, u32[]{:S(2)}, u32[]{:S(2)}) %collective-permute-start.3) | collective-permute-done | bytes 540704 | tf_op jit(solution)/shard_map/ppermute | solution.py:144
  219.8 7.3 collective-permute-done.17
  235.1 22.8 %collective-permute-done.31 = bf16[8,1,32,2816]{3,2,1,0:T(8,128)(2,1)S(1)} collective-permute-done((bf16[8,1,32,2816]{3,2,1,0:T(8,128)(2,1)S(1)}, bf16[8,1,32,2816]{3,2,1,0:T(8,128)(2,1)S(1)}, u32[]{:S(2)}, u32[]{:S(2)}) %collective-permute-start.31) | collective-permute-done | bytes 1441824 | tf_op jit(solution)/shard_map/ppermute | solution.py:144
  261.0 31.8 %collective-permute-done.24 = bf16[4,3,48,1408]{3,2,1,0:T(8,128)(2,1)S(1)} collective-permute-done((bf16[4,3,48,1408]{3,2,1,0:T(8,128)(2,1)S(1)}, bf16[4,3,48,1408]{3,2,1,0:T(8,128)(2,1)S(1)}, u32[]{:S(2)}, u32[]{:S(2)}) %collective-permute-start.24) | collective-permute-done | bytes 1622048 | tf_op jit(solution)/shard_map/ppermute | solution.py:144
  297.4 16.7 %collective-permute-done.18 = bf16[8,1,48,4224]{3,2,1,0:T(8,128)(2,1)S(1)} collective-permute-done((bf16[8,1,48,4224]{3,2,1,0:T(8,128)(2,1)S(1)}, bf16[8,1,48,4224]{3,2,1,0:T(8,128)(2,1)S(1)}, u32[]{:S(2)}, u32[]{:S(2)}) %collective-permute-start.18) | collective-permute-done | bytes 3244064 | tf_op jit(solution)/shard_map/ppermute | solution.py:144
  318.3 16.8 %collective-permute-done.5 = bf16[8,1,96,1408]{3,2,1,0:T(8,128)(2,1)S(1)} collective-permute-done((bf16[8,1,96,1408]{3,2,1,0:T(8,128)(2,1)S(1)}, bf16[8,1,96,1408]{3,2,1,0:T(8,128)(2,1)S(1)}, u32[]{:S(2)}, u32[]{:S(2)}) %collective-permute-start.5) | collective-permute-done | bytes 2162720 | tf_op jit(solution)/shard_map/ppermute | solution.py:144
  336.6 16.3 %shard_map.552 = bf16[1,1024,2816]{2,1,0:T(8,128)(2,1)S(1)} custom-call(s32[2]{0:T(128)S(1)} %pad_add_fusion.11.index_ref, bf16[16,1,32,2816]{3,2,1,0:T(8,128)(2,1)S(1)} %constant_dynamic-update-slice_fusion.15.own_ref, bf16[16,1,32,2816]{3,2,1,0:T(8,128)(2,1)S(1)} %collective-permute-done.32.far_ref), custom_call_target="tpu_custom_call" | custom-call | bytes 11534336 | tf_op jit(solution)/shard_map/pallas_call | solution.py:241
  395.6 5.9 shard_map.549
  406.8 7.4 shard_map.550
  436.8 7.5 shard_map.551
  455.3 6.2 copy.631
  480.8 5.7 convolution_convert_fusion.9
  512.1 11.0 collective-permute-done.34
  524.3 6.0 collective-permute-done.45
  538.1 11.4 collective-permute-done.46
  550.9 6.8 collective-permute-done.38.far_ref
  560.7 42.7 %collective-permute-done.41.far_ref = bf16[4,192,1408]{2,1,0:T(8,128)(2,1)} collective-permute-done((bf16[4,192,1408]{2,1,0:T(8,128)(2,1)S(1)}, bf16[4,192,1408]{2,1,0:T(8,128)(2,1)}, u32[]{:S(2)}, u32[]{:S(2)}) %collective-permute-start.41) | collective-permute-done | bytes 2162720 | tf_op jit(solution)/shard_map/ppermute | solution.py:144
  605.9 6.4 fusion.66
  612.3 5.4 fusion.187
  619.0 12.5 fusion.15
  631.5 6.9 fusion.205
  641.5 9.2 convolution_convert_fusion.2
  654.5 7.5 convolution_convert_fusion.3
  667.7 13.8 collective-permute-done.49
  682.0 13.9 collective-permute-done.43
  702.4 5.2 multiply_reduce_fusion.2
  725.2 6.8 multiply_reduce_fusion
  777.5 5.9 pad_maximum_fusion
  819.3 22.0 %collective-permute-done.85 = bf16[2,176,1536]{2,1,0:T(8,128)(2,1)} collective-permute-done((bf16[2,176,1536]{2,1,0:T(8,128)(2,1)}, bf16[2,176,1536]{2,1,0:T(8,128)(2,1)}, u32[]{:S(2)}, u32[]{:S(2)}) %collective-permute-start.85) | collective-permute-done | bytes 1081376 | tf_op jit(solution)/shard_map/ppermute | solution.py:144
  852.1 8.4 multiply_reduce_fusion.6
  860.5 8.2 convolution_convert_fusion
  868.7 6.1 constant_dynamic-slice_fusion.3
  923.6 6.4 fusion.8
  931.2 6.0 add_convert_fusion
  937.2 11.5 collective-permute-done.80
  964.9 123.4 %collective-permute-done.81 = bf16[2,2,1,32,2816]{4,3,2,1,0:T(8,128)(2,1)S(1)} collective-permute-done((bf16[2,2,1,32,2816]{4,3,2,1,0:T(8,128)(2,1)}, bf16[2,2,1,32,2816]{4,3,2,1,0:T(8,128)(2,1)S(1)}, u32[]{:S(2)}, u32[]{:S(2)}) %collective-permute-start.81) | collective-permute-done | bytes 720928 | tf_op jit(solution)/shard_map/ppermute | solution.py:144
  1111.5 5.2 fusion.55
  1118.0 13.9 collective-permute-done.60
  1143.6 9.3 collective-permute-done.61
  1178.4 18.2 %collective-permute-done.71 = bf16[2,3,48,1408]{3,2,1,0:T(8,128)(2,1)} collective-permute-done((bf16[2,3,48,1408]{3,2,1,0:T(8,128)(2,1)}, bf16[2,3,48,1408]{3,2,1,0:T(8,128)(2,1)}, u32[]{:S(2)}, u32[]{:S(2)}) %collective-permute-start.71) | collective-permute-done | bytes 811040 | tf_op jit(solution)/shard_map/ppermute | solution.py:144
  1207.4 7.6 collective-permute-done.72
  1221.7 19.1 %collective-permute-done.76 = bf16[2,1,48,4224]{3,2,1,0:T(8,128)(2,1)} collective-permute-done((bf16[2,1,48,4224]{3,2,1,0:T(8,128)(2,1)}, bf16[2,1,48,4224]{3,2,1,0:T(8,128)(2,1)}, u32[]{:S(2)}, u32[]{:S(2)}) %collective-permute-start.76) | collective-permute-done | bytes 811040 | tf_op jit(solution)/shard_map/ppermute | solution.py:144
  1243.6 8.6 collective-permute-done.77
  1291.7 4.7 concatenate.368
  (1172 shorter events, 700.9 us)
Async XLA Ops:
  2.7 101.2 %collective-permute-start = (bf16[128,1408]{1,0:T(8,128)(2,1)}, bf16[128,1408]{1,0:T(8,128)(2,1)}, u32[]{:S(2)}, u32[]{:S(2)}) collective-permute-start(bf16[128,1408]{1,0:T(8,128)(2,1)} %get-tuple-element.410), channel_id=1, source_target_pairs={{0,2},{1,3},{2,0},{3,1},{4,6},{5,7},{6,4},{7,5},{8,10},{9,11},{10,... | collective-permute-start | bytes 1081352 | tf_op jit(solution)/shard_map/ppermute | solution.py:144
  7.6 97.9 %collective-permute-start.1 = (bf16[128,1408]{1,0:T(8,128)(2,1)}, bf16[128,1408]{1,0:T(8,128)(2,1)}, u32[]{:S(2)}, u32[]{:S(2)}) collective-permute-start(bf16[128,1408]{1,0:T(8,128)(2,1)} %get-tuple-element.412), channel_id=1, source_target_pairs={{0,2},{1,3},{2,0},{3,1},{4,6},{5,7},{6,4},{7,5},{8,10},{9,11},{10,... | collective-permute-start | bytes 1081352 | tf_op jit(solution)/shard_map/ppermute | solution.py:144
  10.1 48.5 %collective-permute-start.20 = (s32[128,2]{0,1:T(2,128)}, s32[128,2]{0,1:T(2,128)}, u32[]{:S(2)}, u32[]{:S(2)}) collective-permute-start(s32[128,2]{0,1:T(2,128)} %get-tuple-element.512), channel_id=1, source_target_pairs={{0,2},{1,3},{2,0},{3,1},{4,6},{5,7},{6,4},{7,5},{8,10},{9,11},{10,... | collective-permute-start | bytes 3080 | tf_op jit(solution)/shard_map/ppermute | solution.py:144
  13.8 339.1 %collective-permute-start.27 = (bf16[84,1024]{1,0:T(8,128)(2,1)}, bf16[84,1024]{1,0:T(8,128)(2,1)}, u32[]{:S(2)}, u32[]{:S(2)}) collective-permute-start(bf16[84,1024]{1,0:T(8,128)(2,1)} %bitcast.613), channel_id=1, source_target_pairs={{0,2},{1,3},{2,0},{3,1},{4,6},{5,7},{6,4},{7,5},{8,10},{9,11},{10,... | collective-permute-start | bytes 516104 | tf_op jit(solution)/shard_map/ppermute | solution.py:144
  15.3 46.4 %all-to-all-start.3 = ((bf16[4,1,32,704]{3,2,1,0:T(8,128)(2,1)}), bf16[4,1,32,704]{3,2,1,0:T(8,128)(2,1)}, u32[]{:S(2)}, u32[]{:S(2)}) async-start(bf16[4,1,32,704]{3,2,1,0:T(8,128)(2,1)} %pad_maximum_fusion.49), calls=%async_computation.3 | async-start | bytes 393216 | tf_op jit(solution)/shard_map/all_to_all | solution.py:177
  88.5 45.6 %collective-permute-start.2 = (bf16[1,1,96,1408]{3,2,1,0:T(8,128)(2,1)S(1)}, bf16[1,1,96,1408]{3,2,1,0:T(8,128)(2,1)}, u32[]{:S(2)}, u32[]{:S(2)}) collective-permute-start(bf16[1,1,96,1408]{3,2,1,0:T(8,128)(2,1)S(1)} %broadcast_in_dim_reshape.19), channel_id=1, source_target_pairs={{0,8},{4,12},{8,0},{12,4},{16,24},{20,28},{24,16},{28,20},{1,9},{5... | collective-permute-start | bytes 811016 | tf_op jit(solution)/shard_map/ppermute | solution.py:144
  102.0 89.2 %collective-permute-start.22 = (bf16[1,3,48,1408]{3,2,1,0:T(8,128)(2,1)S(1)}, bf16[1,3,48,1408]{3,2,1,0:T(8,128)(2,1)}, u32[]{:S(2)}, u32[]{:S(2)}) collective-permute-start(bf16[1,3,48,1408]{3,2,1,0:T(8,128)(2,1)S(1)} %broadcast_in_dim_reshape.21), channel_id=1, source_target_pairs={{0,8},{4,12},{8,0},{12,4},{16,24},{20,28},{24,16},{28,20},{1,9},{5... | collective-permute-start | bytes 1216520 | tf_op jit(solution)/shard_map/ppermute | solution.py:144
  134.1 60.3 %collective-permute-start.36 = (bf16[1,176,1536]{2,1,0:T(8,128)(2,1)}, bf16[1,176,1536]{2,1,0:T(8,128)(2,1)S(1)}, u32[]{:S(2)}, u32[]{:S(2)}) collective-permute-start(bf16[1,176,1536]{2,1,0:T(8,128)(2,1)} %broadcast_in_dim_reshape.23), channel_id=1, source_target_pairs={{0,8},{4,12},{8,0},{12,4},{16,24},{20,28},{24,16},{28,20},{1,9},{5... | collective-permute-start | bytes 1622024 | tf_op jit(solution)/shard_map/ppermute | solution.py:144
  136.7 50.9 %collective-permute-start.16 = (bf16[2,1,48,4224]{3,2,1,0:T(8,128)(2,1)S(1)}, bf16[2,1,48,4224]{3,2,1,0:T(8,128)(2,1)S(1)}, u32[]{:S(2)}, u32[]{:S(2)}) collective-permute-start(bf16[2,1,48,4224]{3,2,1,0:T(8,128)(2,1)S(1)} %pad_maximum_fusion.25), channel_id=1, source_target_pairs={{0,16},{4,20},{8,24},{12,28},{16,0},{20,4},{24,8},{28,12},{1,17},{... | collective-permute-start | bytes 2433032 | tf_op jit(solution)/shard_map/ppermute | solution.py:144
  138.7 77.8 %collective-permute-start.3 = (bf16[2,1,96,1408]{3,2,1,0:T(8,128)(2,1)S(1)}, bf16[2,1,96,1408]{3,2,1,0:T(8,128)(2,1)S(1)}, u32[]{:S(2)}, u32[]{:S(2)}) collective-permute-start(bf16[2,1,96,1408]{3,2,1,0:T(8,128)(2,1)S(1)} %pad_maximum_fusion.32), channel_id=1, source_target_pairs={{0,16},{4,20},{8,24},{12,28},{16,0},{20,4},{24,8},{28,12},{1,17},{... | collective-permute-start | bytes 1622024 | tf_op jit(solution)/shard_map/ppermute | solution.py:144
  217.7 41.5 %collective-permute-start.4 = (bf16[4,1,96,1408]{3,2,1,0:T(8,128)(2,1)S(1)}, bf16[4,1,96,1408]{3,2,1,0:T(8,128)(2,1)S(1)}, u32[]{:S(2)}, u32[]{:S(2)}) collective-permute-start(bf16[4,1,96,1408]{3,2,1,0:T(8,128)(2,1)S(1)} %pad_maximum_fusion.19), channel_id=1, source_target_pairs={{0,2},{1,3},{2,0},{3,1},{4,6},{5,7},{6,4},{7,5},{8,10},{9,11},{10,... | collective-permute-start | bytes 3244040 | tf_op jit(solution)/shard_map/ppermute | solution.py:144
  219.2 38.8 %collective-permute-start.31 = (bf16[8,1,32,2816]{3,2,1,0:T(8,128)(2,1)S(1)}, bf16[8,1,32,2816]{3,2,1,0:T(8,128)(2,1)S(1)}, u32[]{:S(2)}, u32[]{:S(2)}) collective-permute-start(bf16[8,1,32,2816]{3,2,1,0:T(8,128)(2,1)S(1)} %pad_maximum_fusion.14), channel_id=1, source_target_pairs={{0,4},{4,0},{8,12},{12,8},{16,20},{20,16},{24,28},{28,24},{1,5},{5... | collective-permute-start | bytes 4325384 | tf_op jit(solution)/shard_map/ppermute | solution.py:144
  228.5 85.6 %collective-permute-start.18 = (bf16[8,1,48,4224]{3,2,1,0:T(8,128)(2,1)S(1)}, bf16[8,1,48,4224]{3,2,1,0:T(8,128)(2,1)S(1)}, u32[]{:S(2)}, u32[]{:S(2)}) collective-permute-start(bf16[8,1,48,4224]{3,2,1,0:T(8,128)(2,1)S(1)} %pad_maximum_fusion.1), channel_id=1, source_target_pairs={{0,2},{1,3},{2,0},{3,1},{4,6},{5,7},{6,4},{7,5},{8,10},{9,11},{10,... | collective-permute-start | bytes 9732104 | tf_op jit(solution)/shard_map/ppermute | solution.py:144
  233.5 59.2 %collective-permute-start.24 = (bf16[4,3,48,1408]{3,2,1,0:T(8,128)(2,1)S(1)}, bf16[4,3,48,1408]{3,2,1,0:T(8,128)(2,1)S(1)}, u32[]{:S(2)}, u32[]{:S(2)}) collective-permute-start(bf16[4,3,48,1408]{3,2,1,0:T(8,128)(2,1)S(1)} %pad_maximum_fusion.12), channel_id=1, source_target_pairs={{0,4},{4,0},{8,12},{12,8},{16,20},{20,16},{24,28},{28,24},{1,5},{5... | collective-permute-start | bytes 4866056 | tf_op jit(solution)/shard_map/ppermute | solution.py:144
  258.1 78.5 %collective-permute-start.32 = (bf16[16,1,32,2816]{3,2,1,0:T(8,128)(2,1)S(1)}, bf16[16,1,32,2816]{3,2,1,0:T(8,128)(2,1)S(1)}, u32[]{:S(2)}, u32[]{:S(2)}) collective-permute-start(bf16[16,1,32,2816]{3,2,1,0:T(8,128)(2,1)S(1)} %constant_dynamic-update-slice_fusion.15.own_ref), channel_id=1, source_target_pairs={{0,1},{1,0},{2,3},{3,2},{4,5},{5,4},{6,7},{7,6},{8,9},{9,8},{10,11... | collective-permute-start | bytes 8650760 | tf_op jit(solution)/shard_map/ppermute | solution.py:144
  260.4 74.7 %collective-permute-start.5 = (bf16[8,1,96,1408]{3,2,1,0:T(8,128)(2,1)S(1)}, bf16[8,1,96,1408]{3,2,1,0:T(8,128)(2,1)S(1)}, u32[]{:S(2)}, u32[]{:S(2)}) collective-permute-start(bf16[8,1,96,1408]{3,2,1,0:T(8,128)(2,1)S(1)} %pad_maximum_fusion.7), channel_id=1, source_target_pairs={{0,4},{4,0},{8,12},{12,8},{16,20},{20,16},{24,28},{28,24},{1,5},{5... | collective-permute-start | bytes 6488072 | tf_op jit(solution)/shard_map/ppermute | solution.py:144
  295.6 83.9 %collective-permute-start.25 = (bf16[8,3,48,1408]{3,2,1,0:T(8,128)(2,1)}, bf16[8,3,48,1408]{3,2,1,0:T(8,128)(2,1)}, u32[]{:S(2)}, u32[]{:S(2)}) collective-permute-start(bf16[8,3,48,1408]{3,2,1,0:T(8,128)(2,1)} %pad_maximum_fusion.2), channel_id=1, source_target_pairs={{0,2},{1,3},{2,0},{3,1},{4,6},{5,7},{6,4},{7,5},{8,10},{9,11},{10,... | collective-permute-start | bytes 9732104 | tf_op jit(solution)/shard_map/ppermute | solution.py:144
  315.9 90.9 %collective-permute-start.19 = (bf16[16,1,48,4224]{3,2,1,0:T(8,128)(2,1)}, bf16[16,1,48,4224]{3,2,1,0:T(8,128)(2,1)}, u32[]{:S(2)}, u32[]{:S(2)}) collective-permute-start(bf16[16,1,48,4224]{3,2,1,0:T(8,128)(2,1)} %constant_dynamic-update-slice_fusion.5.own_ref), channel_id=1, source_target_pairs={{0,1},{1,0},{2,3},{3,2},{4,5},{5,4},{6,7},{7,6},{8,9},{9,8},{10,11... | collective-permute-start | bytes 19464200 | tf_op jit(solution)/shard_map/ppermute | solution.py:144
  335.1 49.2 %collective-permute-start.39 = (bf16[1,192,1408]{2,1,0:T(8,128)(2,1)}, bf16[1,192,1408]{2,1,0:T(8,128)(2,1)}, u32[]{:S(2)}, u32[]{:S(2)}) collective-permute-start(bf16[1,192,1408]{2,1,0:T(8,128)(2,1)} %broadcast_in_dim_reshape.24), channel_id=1, source_target_pairs={{0,8},{4,12},{8,0},{12,4},{16,24},{20,28},{24,16},{28,20},{1,9},{5... | collective-permute-start | bytes 1622024 | tf_op jit(solution)/shard_map/ppermute | solution.py:144
  336.6 59.0 %collective-permute-start.6 = (bf16[16,1,96,1408]{3,2,1,0:T(8,128)(2,1)}, bf16[16,1,96,1408]{3,2,1,0:T(8,128)(2,1)}, u32[]{:S(2)}, u32[]{:S(2)}) collective-permute-start(bf16[16,1,96,1408]{3,2,1,0:T(8,128)(2,1)} %constant_dynamic-update-slice_fusion.own_ref), channel_id=1, source_target_pairs={{0,1},{1,0},{2,3},{3,2},{4,5},{5,4},{6,7},{7,6},{8,9},{9,8},{10,11... | collective-permute-start | bytes 12976136 | tf_op jit(solution)/shard_map/ppermute | solution.py:144
  383.4 50.5 %collective-permute-start.26 = (bf16[16,3,48,1408]{3,2,1,0:T(8,128)(2,1)}, bf16[16,3,48,1408]{3,2,1,0:T(8,128)(2,1)}, u32[]{:S(2)}, u32[]{:S(2)}) collective-permute-start(bf16[16,3,48,1408]{3,2,1,0:T(8,128)(2,1)} %constant_dynamic-update-slice_fusion.10.own_ref), channel_id=1, source_target_pairs={{0,1},{1,0},{2,3},{3,2},{4,5},{5,4},{6,7},{7,6},{8,9},{9,8},{10,11... | collective-permute-start | bytes 19464200 | tf_op jit(solution)/shard_map/ppermute | solution.py:144
  384.3 121.0 %collective-permute-start.37 = (bf16[2,176,1536]{2,1,0:T(8,128)(2,1)}, bf16[2,176,1536]{2,1,0:T(8,128)(2,1)}, u32[]{:S(2)}, u32[]{:S(2)}) collective-permute-start(bf16[2,176,1536]{2,1,0:T(8,128)(2,1)} %pad_maximum_fusion.20), channel_id=1, source_target_pairs={{0,16},{4,20},{8,24},{12,28},{16,0},{20,4},{24,8},{28,12},{1,17},{... | collective-permute-start | bytes 3244040 | tf_op jit(solution)/shard_map/ppermute | solution.py:144
  388.0 120.1 %collective-permute-start.40 = (bf16[2,192,1408]{2,1,0:T(8,128)(2,1)}, bf16[2,192,1408]{2,1,0:T(8,128)(2,1)}, u32[]{:S(2)}, u32[]{:S(2)}) collective-permute-start(bf16[2,192,1408]{2,1,0:T(8,128)(2,1)} %pad_maximum_fusion.21), channel_id=1, source_target_pairs={{0,16},{4,20},{8,24},{12,28},{16,0},{20,4},{24,8},{28,12},{1,17},{... | collective-permute-start | bytes 3244040 | tf_op jit(solution)/shard_map/ppermute | solution.py:144
  507.5 50.2 %collective-permute-start.38 = (bf16[4,176,1536]{2,1,0:T(8,128)(2,1)}, bf16[4,176,1536]{2,1,0:T(8,128)(2,1)}, u32[]{:S(2)}, u32[]{:S(2)}) collective-permute-start(bf16[4,176,1536]{2,1,0:T(8,128)(2,1)} %constant_dynamic-update-slice_fusion.20.own_ref), channel_id=1, source_target_pairs={{0,4},{4,0},{8,12},{12,8},{16,20},{20,16},{24,28},{28,24},{1,5},{5... | collective-permute-start | bytes 6488072 | tf_op jit(solution)/shard_map/ppermute | solution.py:144
  509.5 93.9 %collective-permute-start.41 = (bf16[4,192,1408]{2,1,0:T(8,128)(2,1)S(1)}, bf16[4,192,1408]{2,1,0:T(8,128)(2,1)}, u32[]{:S(2)}, u32[]{:S(2)}) collective-permute-start(bf16[4,192,1408]{2,1,0:T(8,128)(2,1)S(1)} %constant_dynamic-update-slice_fusion.23.own_ref), channel_id=1, source_target_pairs={{0,4},{4,0},{8,12},{12,8},{16,20},{20,16},{24,28},{28,24},{1,5},{5... | collective-permute-start | bytes 6488072 | tf_op jit(solution)/shard_map/ppermute | solution.py:144
  524.3 81.5 %collective-permute-start.35 = (bf16[512,1408]{1,0:T(8,128)(2,1)}, bf16[512,1408]{1,0:T(8,128)(2,1)}, u32[]{:S(2)}, u32[]{:S(2)}) collective-permute-start(bf16[512,1408]{1,0:T(8,128)(2,1)} %pad_maximum_fusion.15), channel_id=1, source_target_pairs={{0,1},{1,0},{2,3},{3,2},{4,5},{5,4},{6,7},{7,6},{8,9},{9,8},{10,11... | collective-permute-start | bytes 4325384 | tf_op jit(solution)/shard_map/ppermute | solution.py:144
  550.8 68.2 %collective-permute-start.47 = (bf16[512,1408]{1,0:T(8,128)(2,1)S(1)}, bf16[512,1408]{1,0:T(8,128)(2,1)}, u32[]{:S(2)}, u32[]{:S(2)}) collective-permute-start(bf16[512,1408]{1,0:T(8,128)(2,1)S(1)} %pad_maximum_fusion.16), channel_id=1, source_target_pairs={{0,1},{1,0},{2,3},{3,2},{4,5},{5,4},{6,7},{7,6},{8,9},{9,8},{10,11... | collective-permute-start | bytes 4325384 | tf_op jit(solution)/shard_map/ppermute | solution.py:144
  619.0 44.5 %collective-permute-start.42 = (bf16[512,1408]{1,0:T(8,128)(2,1)}, bf16[512,1408]{1,0:T(8,128)(2,1)S(1)}, u32[]{:S(2)}, u32[]{:S(2)}) collective-permute-start(bf16[512,1408]{1,0:T(8,128)(2,1)} %slice.965), channel_id=1, source_target_pairs={{0,1},{1,0},{2,3},{3,2},{4,5},{5,4},{6,7},{7,6},{8,9},{9,8},{10,11... | collective-permute-start | bytes 4325384 | tf_op jit(solution)/shard_map/ppermute | solution.py:144
  654.0 88.0 %collective-permute-start.87 = (bf16[2,2,192,1408]{3,2,1,0:T(8,128)(2,1)}, bf16[2,2,192,1408]{3,2,1,0:T(8,128)(2,1)}, u32[]{:S(2)}, u32[]{:S(2)}) collective-permute-start(bf16[2,2,192,1408]{3,2,1,0:T(8,128)(2,1)} %dynamic-slice_bitcast_fusion.1), channel_id=1, source_target_pairs={{0,4},{4,0},{8,12},{12,8},{16,20},{20,16},{24,28},{28,24},{1,5},{5... | collective-permute-start | bytes 6488072 | tf_op jit(solution)/shard_map/ppermute | solution.py:144
  666.5 96.4 %collective-permute-start.84 = (bf16[2,2,176,1536]{3,2,1,0:T(8,128)(2,1)}, bf16[2,2,176,1536]{3,2,1,0:T(8,128)(2,1)}, u32[]{:S(2)}, u32[]{:S(2)}) collective-permute-start(bf16[2,2,176,1536]{3,2,1,0:T(8,128)(2,1)} %dynamic-slice_bitcast_fusion.2), channel_id=1, source_target_pairs={{0,4},{4,0},{8,12},{12,8},{16,20},{20,16},{24,28},{28,24},{1,5},{5... | collective-permute-start | bytes 6488072 | tf_op jit(solution)/shard_map/ppermute | solution.py:144
  739.9 106.1 %collective-permute-start.50 = (bf16[2,256,1408]{1,2,0:T(8,128)(2,1)}, bf16[2,256,1408]{1,2,0:T(8,128)(2,1)}, u32[]{:S(2)}, u32[]{:S(2)}) collective-permute-start(bf16[2,256,1408]{1,2,0:T(8,128)(2,1)} %fusion.42), channel_id=1, source_target_pairs={{0,1},{1,0},{2,3},{3,2},{4,5},{5,4},{6,7},{7,6},{8,9},{9,8},{10,11... | collective-permute-start | bytes 4325384 | tf_op jit(solution)/shard_map/ppermute | solution.py:144
  744.8 98.9 %collective-permute-start.88 = (bf16[2,192,1408]{2,1,0:T(8,128)(2,1)}, bf16[2,192,1408]{2,1,0:T(8,128)(2,1)}, u32[]{:S(2)}, u32[]{:S(2)}) collective-permute-start(bf16[2,192,1408]{2,1,0:T(8,128)(2,1)} %fusion.48), channel_id=1, source_target_pairs={{0,16},{4,20},{8,24},{12,28},{16,0},{20,4},{24,8},{28,12},{1,17},{... | collective-permute-start | bytes 3244040 | tf_op jit(solution)/shard_map/ppermute | solution.py:144
  765.7 75.6 %collective-permute-start.85 = (bf16[2,176,1536]{2,1,0:T(8,128)(2,1)}, bf16[2,176,1536]{2,1,0:T(8,128)(2,1)}, u32[]{:S(2)}, u32[]{:S(2)}) collective-permute-start(bf16[2,176,1536]{2,1,0:T(8,128)(2,1)} %fusion.49), channel_id=1, source_target_pairs={{0,16},{4,20},{8,24},{12,28},{16,0},{20,4},{24,8},{28,12},{1,17},{... | collective-permute-start | bytes 3244040 | tf_op jit(solution)/shard_map/ppermute | solution.py:144
  791.7 131.2 %collective-permute-start.68 = (bf16[2,2,2,3,96,1408]{5,4,3,2,1,0:T(8,128)(2,1)}, bf16[2,2,2,3,96,1408]{5,4,3,2,1,0:T(8,128)(2,1)}, u32[]{:S(2)}, u32[]{:S(2)}) collective-permute-start(bf16[2,2,2,3,96,1408]{5,4,3,2,1,0:T(8,128)(2,1)} %dynamic-slice_bitcast_fusion), channel_id=1, source_target_pairs={{0,1},{1,0},{2,3},{3,2},{4,5},{5,4},{6,7},{7,6},{8,9},{9,8},{10,11... | collective-permute-start | bytes 19464200 | tf_op jit(solution)/shard_map/ppermute | solution.py:144
  819.0 85.4 %collective-permute-start.79 = (bf16[2,2,2,1,64,2816]{5,4,1,3,2,0:T(8,128)(2,1)}, bf16[2,2,2,1,64,2816]{5,4,1,3,2,0:T(8,128)(2,1)S(1)}, u32[]{:S(2)}, u32[]{:S(2)}) collective-permute-start(bf16[2,2,2,1,64,2816]{5,4,1,3,2,0:T(8,128)(2,1)} %copy.702), channel_id=1, source_target_pairs={{0,1},{1,0},{2,3},{3,2},{4,5},{5,4},{6,7},{7,6},{8,9},{9,8},{10,11... | collective-permute-start | bytes 8650760 | tf_op jit(solution)/shard_map/ppermute | solution.py:144
  875.3 54.7 %collective-permute-start.73 = (bf16[2,2,2,1,96,4224]{5,4,3,2,1,0:T(8,128)(2,1)}, bf16[2,2,2,1,96,4224]{5,4,3,2,1,0:T(8,128)(2,1)}, u32[]{:S(2)}, u32[]{:S(2)}) collective-permute-start(bf16[2,2,2,1,96,4224]{5,4,3,2,1,0:T(8,128)(2,1)} %constant_dynamic-slice_fusion.3), channel_id=1, source_target_pairs={{0,1},{1,0},{2,3},{3,2},{4,5},{5,4},{6,7},{7,6},{8,9},{9,8},{10,11... | collective-permute-start | bytes 19464200 | tf_op jit(solution)/shard_map/ppermute | solution.py:144
  904.4 47.9 %collective-permute-start.89 = (bf16[192,1408]{1,0:T(8,128)(2,1)}, bf16[192,1408]{1,0:T(8,128)(2,1)}, u32[]{:S(2)}, u32[]{:S(2)}) collective-permute-start(bf16[192,1408]{1,0:T(8,128)(2,1)} %fusion.68), channel_id=1, source_target_pairs={{0,8},{4,12},{8,0},{12,4},{16,24},{20,28},{24,16},{28,20},{1,9},{5... | collective-permute-start | bytes 1622024 | tf_op jit(solution)/shard_map/ppermute | solution.py:144
  916.1 40.6 %collective-permute-start.86 = (bf16[176,1536]{1,0:T(8,128)(2,1)}, bf16[176,1536]{1,0:T(8,128)(2,1)}, u32[]{:S(2)}, u32[]{:S(2)}) collective-permute-start(bf16[176,1536]{1,0:T(8,128)(2,1)} %fusion.71), channel_id=1, source_target_pairs={{0,8},{4,12},{8,0},{12,4},{16,24},{20,28},{24,16},{28,20},{1,9},{5... | collective-permute-start | bytes 1622024 | tf_op jit(solution)/shard_map/ppermute | solution.py:144
  922.9 169.0 %collective-permute-start.59 = (bf16[2,2,1,192,1408]{4,3,2,1,0:T(8,128)(2,1)}, bf16[2,2,1,192,1408]{4,3,2,1,0:T(8,128)(2,1)}, u32[]{:S(2)}, u32[]{:S(2)}) collective-permute-start(bf16[2,2,1,192,1408]{4,3,2,1,0:T(8,128)(2,1)} %fusion.47), channel_id=1, source_target_pairs={{0,4},{4,0},{8,12},{12,8},{16,20},{20,16},{24,28},{28,24},{1,5},{5... | collective-permute-start | bytes 6488072 | tf_op jit(solution)/shard_map/ppermute | solution.py:144
  930.0 181.5 %collective-permute-start.69 = (bf16[2,2,2,3,48,1408]{5,4,3,2,1,0:T(8,128)(2,1)}, bf16[2,2,2,3,48,1408]{5,4,3,2,1,0:T(8,128)(2,1)}, u32[]{:S(2)}, u32[]{:S(2)}) collective-permute-start(bf16[2,2,2,3,48,1408]{5,4,3,2,1,0:T(8,128)(2,1)} %fusion.8), channel_id=1, source_target_pairs={{0,2},{1,3},{2,0},{3,1},{4,6},{5,7},{6,4},{7,5},{8,10},{9,11},{10,... | collective-permute-start | bytes 9732104 | tf_op jit(solution)/shard_map/ppermute | solution.py:144
  948.7 187.8 %collective-permute-start.74 = (bf16[2,2,2,1,48,4224]{5,4,3,2,1,0:T(8,128)(2,1)}, bf16[2,2,2,1,48,4224]{5,4,3,2,1,0:T(8,128)(2,1)}, u32[]{:S(2)}, u32[]{:S(2)}) collective-permute-start(bf16[2,2,2,1,48,4224]{5,4,3,2,1,0:T(8,128)(2,1)} %add_convert_fusion), channel_id=1, source_target_pairs={{0,2},{1,3},{2,0},{3,1},{4,6},{5,7},{6,4},{7,5},{8,10},{9,11},{10,... | collective-permute-start | bytes 9732104 | tf_op jit(solution)/shard_map/ppermute | solution.py:144
  952.3 136.0 %collective-permute-start.81 = (bf16[2,2,1,32,2816]{4,3,2,1,0:T(8,128)(2,1)}, bf16[2,2,1,32,2816]{4,3,2,1,0:T(8,128)(2,1)S(1)}, u32[]{:S(2)}, u32[]{:S(2)}) collective-permute-start(bf16[2,2,1,32,2816]{4,3,2,1,0:T(8,128)(2,1)} %fusion.97), channel_id=1, source_target_pairs={{0,2},{1,3},{2,0},{3,1},{4,6},{5,7},{6,4},{7,5},{8,10},{9,11},{10,... | collective-permute-start | bytes 2162696 | tf_op jit(solution)/shard_map/ppermute | solution.py:144
  956.7 139.8 %collective-permute-start.52 = (bf16[128,1408]{1,0:T(8,128)(2,1)S(1)}, bf16[128,1408]{1,0:T(8,128)(2,1)}, u32[]{:S(2)}, u32[]{:S(2)}) collective-permute-start(bf16[128,1408]{1,0:T(8,128)(2,1)S(1)} %copy-done.172), channel_id=1, source_target_pairs={{0,2},{1,3},{2,0},{3,1},{4,6},{5,7},{6,4},{7,5},{8,10},{9,11},{10,... | collective-permute-start | bytes 1081352 | tf_op jit(solution)/shard_map/ppermute | solution.py:144
  961.4 142.4 %all-to-all-start.10 = ((bf16[4,176,2,192]{3,2,1,0:T(2,128)(2,1)}), bf16[4,176,2,192]{3,2,1,0:T(2,128)(2,1)S(1)}, u32[]{:S(2)}, u32[]{:S(2)}) async-start(bf16[4,176,2,192]{3,2,1,0:T(2,128)(2,1)} %copy.679), calls=%async_computation.10 | async-start | bytes 1441792 | tf_op jit(solution)/shard_map/all_to_all | solution.py:640
  1088.3 180.9 %collective-permute-start.51 = (bf16[128,1408]{1,0:T(8,128)(2,1)}, bf16[128,1408]{1,0:T(8,128)(2,1)}, u32[]{:S(2)}, u32[]{:S(2)}) collective-permute-start(bf16[128,1408]{1,0:T(8,128)(2,1)} %get-tuple-element.383), channel_id=1, source_target_pairs={{0,2},{1,3},{2,0},{3,1},{4,6},{5,7},{6,4},{7,5},{8,10},{9,11},{10,... | collective-permute-start | bytes 1081352 | tf_op jit(solution)/shard_map/ppermute | solution.py:144
  1103.8 58.2 %all-to-all-start.11 = ((bf16[4,192,352]{2,1,0:T(8,128)(2,1)}), bf16[4,192,352]{2,1,0:T(8,128)(2,1)S(1)}, u32[]{:S(2)}, u32[]{:S(2)}) async-start(bf16[4,192,352]{2,1,0:T(8,128)(2,1)} %copy.680), calls=%async_computation.11 | async-start | bytes 1179648 | tf_op jit(solution)/shard_map/all_to_all | solution.py:643
  1140.1 59.2 %collective-permute-start.75 = (bf16[2,2,1,48,4224]{4,3,2,1,0:T(8,128)(2,1)S(1)}, bf16[2,2,1,48,4224]{4,3,2,1,0:T(8,128)(2,1)}, u32[]{:S(2)}, u32[]{:S(2)}) collective-permute-start(bf16[2,2,1,48,4224]{4,3,2,1,0:T(8,128)(2,1)S(1)} %fusion.54), channel_id=1, source_target_pairs={{0,4},{4,0},{8,12},{12,8},{16,20},{20,16},{24,28},{28,24},{1,5},{5... | collective-permute-start | bytes 4866056 | tf_op jit(solution)/shard_map/ppermute | solution.py:144
  1335.5 54.9 %collective-permute-start.100 = (f32[5,1408]{1,0:T(8,128)}, f32[5,1408]{1,0:T(8,128)}, u32[]{:S(2)}, u32[]{:S(2)}) collective-permute-start(f32[5,1408]{1,0:T(8,128)} %reshape.2597), channel_id=1, source_target_pairs={{0,1},{1,0},{2,3},{3,2},{4,5},{5,4},{6,7},{7,6},{8,9},{9,8},{10,11... | collective-permute-start | bytes 84488 | tf_op jit(solution)/shard_map/ppermute | solution.py:144
  (328 other events, 4387.8 us)

commit v2 on v1

v2 whole, which is shorter than its diff:
```python
import functools
import math

import jax
import jax.numpy as jnp
from jax import lax
from jax.experimental import pallas as pl
from jax.experimental.pallas import tpu as pltpu
from jax.sharding import PartitionSpec as P

D = 1408
HEADS = 16

EPS_NORM = 1e-06
EPS_SQUARE = 1e-30
EPS_SCALE = 0.001
DECAY = 0.5
CLIP = 1.0
RATE = 0.5

BF16 = jnp.bfloat16
F32 = jnp.float32


def matmul(left, right):
    return jnp.dot(left, right, preferred_element_type=F32)


def matmul_left(left, right):
    return lax.dot_general(left, right, (((0,), (0,)), ((), ())), preferred_element_type=F32)


def matmul_right(left, right):
    return lax.dot_general(left, right, (((1,), (1,)), ((), ())), preferred_element_type=F32)


def norm_rows(values):
    center = values - jnp.mean(values, axis=-1, keepdims=True)
    spread = jnp.mean(center * center, axis=-1, keepdims=True)
    return center * lax.rsqrt(spread + EPS_NORM)


def rotary(values, places):
    half_width = values.shape[-1] // 2
    quarter = half_width // 2
    frequency = jnp.exp(-math.log(10000.0) * jnp.arange(quarter).astype(F32) / quarter)
    pieces = []
    for member in range(2):
        block = values[..., member * half_width : (member + 1) * half_width]
        angles = places[member].astype(F32)[:, None] * frequency[None, :]
        cosine = jnp.cos(angles)[:, None, :]
        sine = jnp.sin(angles)[:, None, :]
        former = block[..., :quarter]
        latter = block[..., quarter:]
        pieces.append(former * cosine - latter * sine)
        pieces.append(latter * cosine + former * sine)
    return jnp.concatenate(pieces, axis=-1)


def time_embed(steps, model_width):
    half_width = model_width // 2
    frequency = jnp.exp(-math.log(10000.0) * jnp.arange(half_width).astype(F32) / half_width)
    angles = steps.astype(F32)[:, None] * frequency[None, :]
    return jnp.concatenate([jnp.cos(angles), jnp.sin(angles)], axis=-1)


def skip_norm(joined, gain_skip):
    return norm_rows(joined) * gain_skip


def modulated(stream, gain_row, shift_row):
    return norm_rows(stream) * gain_row + shift_row


def gained(stream, gain_row):
    return norm_rows(stream) * gain_row


def head_prep(linear, places):
    row_count = linear.shape[0]
    shaped = linear.reshape(row_count, HEADS, -1)
    return rotary(norm_rows(shaped), places).reshape(row_count, -1)


def head_norm(linear):
    row_count = linear.shape[0]
    return norm_rows(linear.reshape(row_count, HEADS, -1)).reshape(row_count, -1)


def gelu_tanh(values):
    return jax.nn.gelu(values, approximate=True)


def attend_scores(queries, key_rows, valid_keys):
    query_count = queries.shape[0]
    head_size = queries.shape[1] // HEADS
    shaped_query = queries.reshape(query_count, HEADS, head_size)
    shaped_keys = key_rows.reshape(key_rows.shape[0], HEADS, head_size)
    score_scale = 1.0 / math.sqrt(head_size)
    scores = jnp.einsum("qhd,khd->hqk", shaped_query, shaped_keys, preferred_element_type=F32) * score_scale
    if valid_keys is not None:
        scores = jnp.where(valid_keys[None, None, :], scores, -1e30)
    return scores, shaped_query, shaped_keys, score_scale


def attend_forward(queries, key_rows, value_rows, valid_keys):
    query_count = queries.shape[0]
    scores, _, _, _ = attend_scores(queries, key_rows, valid_keys)
    shaped_values = value_rows.reshape(value_rows.shape[0], HEADS, -1)
    row_top = jnp.max(scores, axis=-1, keepdims=True)
    logsum = row_top + jnp.log(jnp.sum(jnp.exp(scores - row_top), axis=-1, keepdims=True))
    weights_soft = jnp.exp(scores - logsum).astype(BF16)
    mixture = jnp.einsum("hqk,khd->qhd", weights_soft, shaped_values, preferred_element_type=F32)
    return mixture.reshape(query_count, -1).astype(BF16), logsum


def attend_backward(queries, key_rows, value_rows, valid_keys, logsum, grad_mixture):
    query_count = queries.shape[0]
    scores, shaped_query, shaped_keys, score_scale = attend_scores(queries, key_rows, valid_keys)
    shaped_values = value_rows.reshape(value_rows.shape[0], HEADS, -1)
    shaped_grad = grad_mixture.reshape(query_count, HEADS, -1)
    weights_full = jnp.exp(scores - logsum)
    weights_soft = weights_full.astype(BF16)
    grad_weights = jnp.einsum("qhd,khd->hqk", shaped_grad, shaped_values, preferred_element_type=F32)
    grad_values = jnp.einsum("hqk,qhd->khd", weights_soft, shaped_grad, preferred_element_type=F32)
    row_delta = jnp.sum(weights_full * grad_weights, axis=-1, keepdims=True)
    grad_scores = (weights_full * (grad_weights - row_delta)).astype(BF16)
    grad_queries = (
        jnp.einsum("hqk,khd->qhd", grad_scores, shaped_keys, preferred_element_type=F32) * score_scale
    )
    grad_keys = (
        jnp.einsum("hqk,qhd->khd", grad_scores, shaped_query, preferred_element_type=F32) * score_scale
    )
    key_count = key_rows.shape[0]
    return (
        grad_queries.reshape(query_count, -1),
        grad_keys.reshape(key_count, -1),
        grad_values.reshape(key_count, -1),
    )


def swap(value, axis, mask):
    size = lax.axis_size(axis)
    return lax.ppermute(value, axis, [(i, i ^ mask) for i in range(size)])


def masks_of(axis):
    size = lax.axis_size(axis)
    return [1 << b for b in range(size.bit_length() - 1)]


def butterfly(value, axis):
    for mask in masks_of(axis):
        value = value + swap(value, axis, mask)
    return value


def after(value, *others):
    others = [other for other in others if other is not None]
    if not others:
        return value
    return lax.optimization_barrier((value, *others))[0]


class Links:
    def __init__(self, depth=2):
        self.depth = depth
        self.sent = {}
        self.gate = None

    def hold(self, value, link):
        queue = self.sent.setdefault(link, [])
        earlier = queue[-self.depth] if len(queue) >= self.depth else None
        return after(value, earlier, self.gate)

    def send(self, value, axis, pairs, link):
        got = lax.ppermute(value, axis, pairs)
        self.sent.setdefault(link, []).append(got)
        return got

    def move(self, value, axis, pairs, link):
        return self.send(self.hold(value, link), axis, pairs, link)

    def swap(self, value, axis, mask):
        return self.move(value, axis, xor_pairs(axis, mask), (axis, mask))


def xor_pairs(axis, mask):
    return [(i, i ^ mask) for i in range(lax.axis_size(axis))]


class Flow:
    def __init__(self, stages):
        self.stages = stages
        self.pending = []
        self.result = None

    def step(self, main=None):
        if self.result is not None:
            return main
        if main is not None:
            main = after(main, *self.pending)
        try:
            self.pending = next(self.stages)
        except StopIteration as end:
            self.pending = []
            self.result = end.value
        return main

    def finish(self):
        while self.result is None:
            self.step()
        return self.result


MIDDLE = [(2, 4), (3, 5), (4, 2), (5, 3)]
OUTWARD = [(2, 0), (3, 1), (4, 6), (5, 7)]
INWARD = [(0, 2), (1, 3), (6, 4), (7, 5)]


CORE = ("fsdp", 1)
YAX = ("fsdp", 2)


class Slots:
    def __init__(self, rows, plain=False, size=None):
        self.rows = rows
        self.plain = plain
        self.size = rows // 4 if plain else size or -(-rows // 64) * 16
        self.offset = rows - 2 * self.size
        self.overlap = 4 * self.size - rows

    def skip(self, index):
        if self.plain or index % 2 == 0:
            return 0
        return min(self.size, max(0, 2 * self.size - self.start(index)))

    def start(self, index):
        if self.plain:
            return index * self.size
        return (index % 2) * self.offset + (index // 2) * self.size


def exchange(pieces, gate=None):
    widest = max(piece.shape[2] for piece in pieces)
    joined = jnp.concatenate(
        [jnp.pad(piece, ((0, 0), (0, 0), (0, widest - piece.shape[2]))) for piece in pieces], axis=1
    )
    got = lax.all_to_all(after(joined, gate), "fsdp", 0, 0, tiled=False)
    made = []
    offset = 0
    for piece in pieces:
        made.append(got[:, offset : offset + piece.shape[1], : piece.shape[2]])
        offset += piece.shape[1]
    return made


def slot_pieces(block, slots):
    count, _, breadth = block.shape
    chunk = D // 4
    cuts = jnp.stack(
        [lax.slice_in_dim(block, slots.start(f), slots.start(f) + slots.size, axis=1) for f in range(4)]
    )
    cuts = cuts.reshape(4, count, slots.size, breadth // chunk, chunk)
    return jnp.swapaxes(cuts, 2, 3).reshape(4, -1, chunk)


def slot_rows(got, slots, count):
    chunk = got.shape[2]
    shaped = got.reshape(4, count, -1, slots.size, chunk)
    return jnp.transpose(shaped, (1, 3, 0, 2, 4)).reshape(count, slots.size, -1)


def back_pieces(rows):
    count, size, breadth = rows.shape
    chunk = D // 4
    shaped = rows.reshape(count, size, 4, breadth // (4 * chunk), chunk)
    return jnp.transpose(shaped, (2, 0, 3, 1, 4)).reshape(4, -1, chunk)


def back_block(got, slots, count):
    chunk = got.shape[2]
    shaped = jnp.swapaxes(got.reshape(4, count, -1, slots.size, chunk), 2, 3)
    shaped = shaped.reshape(4, count, slots.size, -1)
    if slots.plain:
        return jnp.swapaxes(shaped, 0, 1).reshape(count, slots.rows, -1)
    return jnp.concatenate(
        [shaped[0], shaped[2], shaped[1][:, slots.overlap :], shaped[3]], axis=1
    )


def staged(pairs, in_sems, out_sems):
    arrivals = [
        pltpu.make_async_copy(source, hold, in_sems.at[k]) for k, (source, hold, _, _) in enumerate(pairs)
    ]
    for copy in arrivals:
        copy.start()
    departures = []
    for k, (_, _, held, target) in enumerate(pairs):
        arrivals[k].wait()
        copy = pltpu.make_async_copy(held, target, out_sems.at[k])
        copy.start()
        departures.append(copy)
    for copy in departures:
        copy.wait()


def z_sources(z_at):
    return [z_at, z_at ^ 1, jnp.where(z_at < 2, 2, 1), jnp.where(z_at < 2, 3, 0)]


def assemble_kernel(groups, index_ref, *refs):
    here_z = index_ref[0] // 2
    here_x = index_ref[0] % 2
    here_f = index_ref[1]
    out_refs = refs[8 : 8 + len(groups)]
    hold_ref, in_sems, out_sems = refs[8 + len(groups) :]
    sources = z_sources(here_z)

    def copies(f):
        arrivals, departures = [], []
        for side in range(8):
            source_f = f ^ (side // 4) ^ (side & 2)
            for k in range(4):
                source_dp = 2 * sources[k] + (here_x ^ (side & 1))
                at = side * 4 + k
                arrivals.append(pltpu.make_async_copy(refs[side].at[k], hold_ref.at[at], in_sems.at[at]))
                leaving = []
                for which, (first, count, slots) in enumerate(groups):
                    skip = slots.skip(source_f)
                    if skip == slots.size:
                        continue
                    row = source_dp * slots.rows + slots.start(source_f) + skip
                    row = pl.multiple_of(row, 16)
                    size = slots.size - skip
                    leaving.append(
                        pltpu.make_async_copy(
                            hold_ref.at[at, pl.ds(first, count), pl.ds(skip, size), :],
                            out_refs[which].at[:, pl.ds(row, size), :],
                            out_sems.at[at * len(groups) + which],
                        )
                    )
                departures.append(leaving)
        return arrivals, departures

    for f in range(4):

        @pl.when(here_f == f)
        def _():
            arrivals, departures = copies(f)
            for copy in arrivals:
                copy.start()
            for copy, leaving in zip(arrivals, departures):
                copy.wait()
                for onward in leaving:
                    onward.start()
            for leaving in departures:
                for onward in leaving:
                    onward.wait()


def assemble(index, parts, groups):
    _, total, size, breadth = parts[0].shape
    return pl.pallas_call(
        functools.partial(assemble_kernel, groups),
        out_shape=[
            jax.ShapeDtypeStruct((count, 8 * slots.rows, breadth), BF16) for _, count, slots in groups
        ],
        in_specs=[pl.BlockSpec(memory_space=pltpu.SMEM)] + [pl.BlockSpec(memory_space=pl.ANY)] * 8,
        out_specs=[pl.BlockSpec(memory_space=pl.ANY)] * len(groups),
        scratch_shapes=[
            pltpu.VMEM((32, total, size, breadth), BF16),
            pltpu.SemaphoreType.DMA((32,)),
            pltpu.SemaphoreType.DMA((32 * len(groups),)),
        ],
        compiler_params=pltpu.CompilerParams(vmem_limit_bytes=32 << 20),
        cost_estimate=pl.CostEstimate(
            flops=0, bytes_accessed=128 * total * size * breadth, transcendentals=0
        ),
    )(index, *parts)


def assemble_halves_kernel(orders, slots, index_ref, *refs):
    here_z = index_ref[0] // 2
    here_x = index_ref[0] % 2
    here_f = index_ref[1]
    count = len(orders)
    part_refs, out_ref = refs[: 4 * count], refs[4 * count]
    holds, (in_sems, out_sems) = refs[4 * count + 1 : 5 * count + 1], refs[5 * count + 1 :]
    sources = z_sources(here_z)

    def pairs(f):
        made = []
        left = 0
        for which, y_first in enumerate(orders):
            width = part_refs[4 * which].shape[-1]
            for side in range(4):
                ref = part_refs[4 * which + side]
                for k in range(8):
                    bits = (k // 4, side % 2)
                    y_bit, x_bit = bits if y_first else bits[::-1]
                    source_f = f ^ (side // 2) ^ (2 * y_bit)
                    source_dp = 2 * sources[k % 4] + (here_x ^ x_bit)
                    skip = slots.skip(source_f)
                    row = source_dp * slots.rows + slots.start(source_f) + skip
                    row = pl.multiple_of(row, 16)
                    size = slots.size - skip
                    hold = holds[which].at[side * 8 + k]
                    made.append(
                        (
                            ref.at[k],
                            hold,
                            holds[which].at[side * 8 + k, :, pl.ds(skip, size), :],
                            out_ref.at[:, pl.ds(row, size), pl.ds(left, width)],
                        )
                    )
            left += width
        return made

    for f in range(4):

        @pl.when(here_f == f)
        def _():
            staged(pairs(f), in_sems, out_sems)


def assemble_halves(index, parts, orders, slots):
    count, size = parts[0].shape[1:3]
    total = lax.axis_size("dp") * slots.rows
    breadth = sum(part.shape[-1] for part in parts[::4])
    bytes_now = 2 * count * total * breadth
    copies = 32 * len(orders)
    return pl.pallas_call(
        functools.partial(assemble_halves_kernel, orders, slots),
        out_shape=jax.ShapeDtypeStruct((count, total, breadth), BF16),
        in_specs=[pl.BlockSpec(memory_space=pltpu.SMEM)] + [pl.BlockSpec(memory_space=pl.ANY)] * len(parts),
        out_specs=pl.BlockSpec(memory_space=pl.ANY),
        scratch_shapes=[pltpu.VMEM((32, count, size, part.shape[-1]), BF16) for part in parts[::4]]
        + [pltpu.SemaphoreType.DMA((copies,)), pltpu.SemaphoreType.DMA((copies,))],
        compiler_params=pltpu.CompilerParams(vmem_limit_bytes=24 << 20),
        cost_estimate=pl.CostEstimate(flops=0, bytes_accessed=2 * bytes_now, transcendentals=0),
    )(index, *parts)


def place_kernel(index_ref, *refs):
    parts, (out_ref, hold_ref, in_sems, out_sems) = refs[:-4], refs[-4:]
    sources = z_sources(index_ref[0] // 2)
    here_x = index_ref[0] % 2
    made = []
    for side in range(2):
        for k in range(4):
            hold = hold_ref.at[k + side * 4]
            source = parts[side].at[k] if len(parts) == 2 else parts[0].at[k, side]
            made.append((source, hold, hold, out_ref.at[2 * sources[k] + (here_x ^ side)]))
    staged(made, in_sems, out_sems)


def place(index, *parts):
    rows, breadth = parts[0].shape[-2:]
    return pl.pallas_call(
        place_kernel,
        out_shape=jax.ShapeDtypeStruct((8, rows, breadth), BF16),
        in_specs=[pl.BlockSpec(memory_space=pltpu.SMEM)] + [pl.BlockSpec(memory_space=pl.ANY)] * len(parts),
        out_specs=pl.BlockSpec(memory_space=pl.ANY),
        scratch_shapes=[
            pltpu.VMEM((8, rows, breadth), BF16),
            pltpu.SemaphoreType.DMA((8,)),
            pltpu.SemaphoreType.DMA((8,)),
        ],
        compiler_params=pltpu.CompilerParams(vmem_limit_bytes=24 << 20),
        cost_estimate=pl.CostEstimate(flops=0, bytes_accessed=32 * rows * breadth, transcendentals=0),
    )(index, *parts)


def double(buffer, stages):
    for axis, mask in stages:
        buffer = jnp.concatenate([buffer, swap(buffer, axis, mask)], axis=0)
    return buffer


def fits(rows):
    return lax.axis_size("dp") == 8 and rows % 16 == 0 and rows >= 64


def along_z(links, buffer):
    got = links.swap(buffer, "dp", 2)
    yield [got]
    pair = jnp.stack([buffer, got])
    middle = links.move(pair, "dp", MIDDLE, "middle")
    yield [middle]
    outer = links.move(middle, "dp", OUTWARD, ("dp", 2))
    yield [outer]
    z_at = lax.axis_index("dp") // 2
    inner = (z_at == 1) | (z_at == 2)

    def columns(first, last):
        far = jnp.where(inner, middle[..., first:last], outer[..., first:last])
        return jnp.concatenate([pair[..., first:last], far], axis=0)

    return columns


def cut_of(breadth):
    return (breadth // 128 + 1) // 2 * 128


def across(links, value):
    pairs = [(i, i ^ 6) for i in range(4 * lax.axis_size("dp"))]
    got_x, got_y = links.swap(value, "dp", 1), links.swap(value, *YAX)
    return got_x, got_y, links.move(value, ("dp", "fsdp"), pairs, "both")


def gather_full(links, index, slot, groups):
    columns = yield from along_z(links, slot)
    rows = columns(0, slot.shape[-1])
    got = across(links, rows)
    far = [links.swap(rows, *CORE)]
    yield list(got)
    far += [links.swap(part, *CORE) for part in got]
    yield far
    return assemble(index, [rows, *got, *far], groups)


def gather_halves(links, index, slot, slots):
    columns = yield from along_z(links, slot)
    breadth = slot.shape[-1]
    cut = cut_of(breadth)
    first, second = columns(0, cut), columns(cut, breadth)
    got_first, got_second = links.swap(first, *YAX), links.swap(second, "dp", 1)
    yield [got_first, got_second]
    first = jnp.concatenate([first, got_first], axis=0)
    second = jnp.concatenate([second, got_second], axis=0)
    got_first, got_second = links.swap(first, "dp", 1), links.swap(second, *YAX)
    far_own = [links.swap(first, *CORE), links.swap(second, *CORE)]
    yield [got_first, got_second]
    far_got = [links.swap(got_first, *CORE), links.swap(got_second, *CORE)]
    yield far_own + far_got
    parts = [first, got_first, far_own[0], far_got[0], second, got_second, far_own[1], far_got[1]]
    return assemble_halves(index, parts, [True, False], slots)


def gather_wide(block):
    wide = lax.all_gather(block, "fsdp", axis=2, tiled=True)
    return lax.all_gather(wide, "dp", axis=1, tiled=True)


def gather_dp(links, index, block, z_first):
    if z_first:
        columns = yield from along_z(links, block)
        own = columns(0, block.shape[-1])
        far = links.swap(own, "dp", 1)
        yield [far]
        return place(index, own, far)
    far = links.swap(block, "dp", 1)
    yield [far]
    columns = yield from along_z(links, jnp.stack([block, far]))
    return place(index, columns(0, block.shape[-1]))


class View:
    def __init__(self, base, starts=None, sizes=None):
        self.base = base
        self.starts = starts or [0] * base.ndim
        self.sizes = sizes or list(base.shape)

    def narrow(self, axis, start, size):
        starts, sizes = list(self.starts), list(self.sizes)
        starts[axis] = starts[axis] + start
        sizes[axis] = size
        return View(self.base, starts, sizes)

    def read(self):
        if self.sizes == list(self.base.shape):
            return self.base
        if all(isinstance(start, int) for start in self.starts):
            ends = [start + size for start, size in zip(self.starts, self.sizes)]
            return lax.slice(self.base, self.starts, ends)
        return lax.dynamic_slice(self.base, self.starts, self.sizes)


def total_of(views):
    value = views[0].read().astype(F32)
    for view in views[1:]:
        value = value + view.read().astype(F32)
    return value


def split_on(axis_at):
    return lambda view, bit: view.narrow(axis_at, bit, 1)


def split_rows(axis_at, step, size):
    return lambda view, bit: view.narrow(axis_at, bit * step, size)


def send_half(links, views, axis, mask, choose):
    bit = (lax.axis_index(axis) // mask) % 2
    away = links.hold(1 - bit, (axis, mask))
    send = total_of([choose(view, away) for view in views]).astype(BF16)
    received = links.send(send, axis, xor_pairs(axis, mask), (axis, mask))
    return [choose(view, bit) for view in views], received


def halve(links, views, axis, mask, choose):
    kept, received = send_half(links, views, axis, mask, choose)
    yield [received]
    return kept + [View(received)]


def halve_z(links, views, choose_far, choose_near):
    bit = lax.axis_index("dp") // 4
    away = links.hold(1 - bit, ("dp", 2))
    send = total_of([choose_far(view, away) for view in views]).astype(BF16)
    inward = links.send(send, "dp", INWARD, ("dp", 2))
    yield [inward]
    away = links.hold(1 - bit, "middle")
    send = total_of([choose_far(view, away) for view in views] + [View(inward)]).astype(BF16)
    middle = links.send(send, "dp", MIDDLE, "middle")
    yield [middle]
    views = [choose_far(view, bit) for view in views] + [View(middle)]
    return (yield from halve(links, views, "dp", 2, choose_near))


def reduce_full(links, gradient):
    count, height, breadth = gradient.shape
    rows = height // 8
    slots = Slots(rows)
    by_core = split_rows(4, slots.offset, 2 * slots.size)
    by_y = split_rows(4, slots.size, slots.size)
    by_x = split_on(3)
    views = [View(gradient.reshape(count, 2, 2, 2, rows, breadth))]
    views = yield from halve(links, views, "fsdp", 1, by_core)
    cut = cut_of(breadth)
    first = [view.narrow(5, 0, cut) for view in views]
    second = [view.narrow(5, cut, breadth - cut) for view in views]
    first, got_first = send_half(links, first, "dp", 1, by_x)
    second, got_second = send_half(links, second, "fsdp", 2, by_y)
    yield [got_first, got_second]
    first, second = first + [View(got_first)], second + [View(got_second)]
    first, got_first = send_half(links, first, "fsdp", 2, by_y)
    second, got_second = send_half(links, second, "dp", 1, by_x)
    yield [got_first, got_second]
    first, second = first + [View(got_first)], second + [View(got_second)]
    joined = jnp.concatenate([total_of(first), total_of(second)], axis=-1).astype(BF16)
    views = yield from halve_z(links, [View(joined)], split_on(1), split_on(2))
    return total_of(views).astype(BF16).reshape(count, slots.size, breadth)


def reduce_wide(gradient):
    thin = lax.psum_scatter(gradient.astype(BF16), "fsdp", scatter_dimension=2, tiled=True)
    return lax.psum_scatter(thin.astype(F32), "dp", scatter_dimension=1, tiled=True)


def spread_tokens(rows):
    pair = jnp.concatenate([rows, swap(rows, *YAX)], axis=0)
    return jnp.concatenate([pair, swap(pair, *CORE)], axis=0)


def collect_tokens(partial):
    half = partial.shape[0] // 2
    pair = partial[:half] + swap(partial[half:].astype(BF16), *CORE).astype(F32)
    quarter = half // 2
    return pair[:quarter] + swap(pair[quarter:].astype(BF16), *YAX).astype(F32)


def pick(pair, bit):
    return lax.dynamic_index_in_dim(pair, bit, axis=0, keepdims=False)


def to_latent(pair, y):
    return jnp.concatenate([pick(pair, y), swap(pick(pair, 1 - y), *YAX)], axis=0)


def from_latent(rows, y):
    half = rows.shape[0] // 2
    own = rows[:half]
    other = swap(rows[half:], *YAX)
    return jnp.where(y == 0, jnp.stack([own, other]), jnp.stack([other, own]))


def flatten_all(arrays):
    return jnp.concatenate([matrix.reshape(-1) for matrix in arrays])


def split_all(vector, shapes):
    pieces = []
    offset = 0
    for shape_now in shapes:
        count_now = math.prod(shape_now)
        pieces.append(vector[offset : offset + count_now].reshape(shape_now))
        offset = offset + count_now
    return pieces


def statistics(group, extra, late):
    dp, fsdp = lax.axis_size("dp"), lax.axis_size("fsdp")
    old_sums = jnp.concatenate([jnp.sum(rows, axis=1) for _, _, rows, _ in group])
    master_squares = jnp.concatenate(
        [jnp.sum(after(master, late) ** 2, axis=(1, 2)) for master, _, _, _ in group]
    )
    squares = [gradient * gradient + EPS_SQUARE for _, gradient, _, _ in group]
    row_parts = [jnp.sum(square_block, axis=2) for square_block in squares]
    column_parts = [jnp.sum(square_block, axis=1) for square_block in squares]
    row_sums = split_all(butterfly(flatten_all(row_parts), "fsdp"), [part.shape for part in row_parts])
    over_dp = column_parts + [old_sums / fsdp, master_squares] + ([] if extra is None else [extra])
    over_dp = split_all(butterfly(flatten_all(over_dp), "dp"), [part.shape for part in over_dp])
    column_sums = over_dp[: len(group)]
    totals = [jnp.concatenate([jnp.sum(part, axis=1) for part in column_sums])] + over_dp[len(group) :]
    totals = split_all(butterfly(flatten_all(totals), "fsdp"), [part.shape for part in totals])
    counts = [(part.shape[0],) for part in row_parts]
    square_split, old_split, master_split = [split_all(total, counts) for total in totals[:3]]
    states = []
    for (_, gradient, rows, columns), row_sum, column_sum, square_total, old_total, master_sum in zip(
        group, row_sums, column_sums, square_split, old_split, master_split
    ):
        height, breadth = gradient.shape[1] * dp, gradient.shape[2] * fsdp
        rows_new = DECAY * rows + (1.0 - DECAY) * row_sum / breadth
        columns_new = DECAY * columns + (1.0 - DECAY) * column_sum / height
        mean = (DECAY * old_total + (1.0 - DECAY) * square_total / breadth) / height
        update = gradient * lax.rsqrt(rows_new[:, :, None] * columns_new[:, None, :] / mean[:, None, None])
        states.append((rows_new, columns_new, update, jnp.sum(update * update, axis=(1, 2)), master_sum))
    return states, totals[3] if extra is not None else None


WIDE = 768
MEMBERS = 9


def members_of(arrays):
    return [(at, one, slab.shape[1], slab.shape[2]) for at, slab in enumerate(arrays) for one in range(slab.shape[0])]


def pack_rows(states):
    rows = [jnp.pad(state, ((0, 0), (0, WIDE - state.shape[1]))) for state in states]
    return jnp.pad(jnp.concatenate(rows, axis=0), ((0, 16 - MEMBERS), (0, 0)))


def pack_columns(states):
    rows = [
        jnp.pad(state, ((0, 0), (0, 2 * WIDE - state.shape[1]))).reshape(-1, WIDE) for state in states
    ]
    return jnp.pad(jnp.concatenate(rows, axis=0), ((0, 32 - 2 * MEMBERS), (0, 0)))


def lane_is(index, shape):
    return lax.broadcasted_iota(jnp.int32, shape, 1) == index


def sums_kernel(count, *refs):
    grads, (extra_ref, rows_ref, columns_ref, turn_ref) = refs[:count], refs[count:]
    columns_ref[...] = jnp.zeros(columns_ref.shape, F32)
    turn_ref[...] = jnp.zeros(turn_ref.shape, F32)
    rows_ref[...] = jnp.zeros(rows_ref.shape, F32)
    totals = jnp.zeros((1, WIDE), F32)
    for at, (slab, one, height, breadth) in enumerate(members_of(grads)):
        gradient = grads[slab][one]
        square = gradient * gradient + EPS_SQUARE
        in_row = jnp.sum(square, axis=1, keepdims=True)
        turn_ref[:height, :] += jnp.where(lane_is(at, (height, 128)), in_row, 0.0)
        in_column = jnp.sum(square, axis=0, keepdims=True)
        columns_ref[2 * at : 2 * at + 1, : min(breadth, WIDE)] = in_column[:, :WIDE]
        if breadth > WIDE:
            columns_ref[2 * at + 1 : 2 * at + 2, : breadth - WIDE] = in_column[:, WIDE:]
        totals += jnp.where(lane_is(2 * MEMBERS + at, (1, WIDE)), jnp.sum(in_row), 0.0)
    rows_ref[:16, :] = turn_ref[...].T[:16]
    rows_ref[16:32, :] = extra_ref[...]
    rows_ref[26:27, :] = extra_ref[10:11, :] + totals


def scalar_at(row, index):
    return jnp.sum(jnp.where(lane_is(index, row.shape), row, 0.0))


def updates_of(grads, at, member, turned, columns_ref, mean):
    slab, one, height, breadth = member
    column = columns_ref[2 * at : 2 * at + 1, : min(breadth, WIDE)]
    if breadth > WIDE:
        column = jnp.concatenate([column, columns_ref[2 * at + 1 : 2 * at + 2, : breadth - WIDE]], axis=1)
    row = turned[:height, at : at + 1]
    return grads[slab][one] * lax.rsqrt(row * (column / mean))


def mean_of(scalars, at, height, breadth):
    old, square = scalar_at(scalars, at), scalar_at(scalars, 2 * MEMBERS + at)
    return (DECAY * old + (1.0 - DECAY) * square / breadth) / height


def states_kernel(count, dp, fsdp, *refs):
    grads = refs[:count]
    row_sum_ref, column_sum_ref, old_rows_ref, old_columns_ref = refs[count : count + 4]
    rows_ref, columns_ref, squares_ref, turn_ref = refs[count + 4 :]
    scalars = column_sum_ref[42:43, :]
    rows_ref[...] = jnp.zeros(rows_ref.shape, F32)
    columns_ref[...] = jnp.zeros(columns_ref.shape, F32)
    members = members_of(grads)
    for at, (_, _, height, breadth) in enumerate(members):
        rows_ref[at : at + 1, :] = DECAY * old_rows_ref[at : at + 1, :] + row_sum_ref[at : at + 1, :] * (
            (1.0 - DECAY) / (breadth * fsdp)
        )
        columns_ref[2 * at : 2 * at + 2, :] = DECAY * old_columns_ref[
            2 * at : 2 * at + 2, :
        ] + column_sum_ref[2 * at : 2 * at + 2, :] * ((1.0 - DECAY) / (height * dp))
    turn_ref[:16, :] = rows_ref[...]
    turned = turn_ref[...].T
    found = jnp.zeros((8, 128), F32)
    for at, member in enumerate(members):
        mean = mean_of(scalars, at, member[2] * dp, member[3] * fsdp)
        update = updates_of(grads, at, member, turned, columns_ref, mean)
        found += jnp.where(lane_is(at, (8, 128)), jnp.sum(update * update), 0.0)
    squares_ref[...] = found


def masters_kernel(count, dp, fsdp, *refs):
    grads, masters = refs[:count], refs[count : 2 * count]
    rows_ref, columns_ref, column_sum_ref, squares_ref = refs[2 * count : 2 * count + 4]
    outs, turn_ref = refs[2 * count + 4 : -1], refs[-1]
    scalars = column_sum_ref[42:43, :]
    squares = squares_ref[0:1, :]
    turn_ref[:16, :] = rows_ref[...]
    turned = turn_ref[...].T
    for at, member in enumerate(members_of(grads)):
        slab, one, height, breadth = member
        mean = mean_of(scalars, at, height * dp, breadth * fsdp)
        update = updates_of(grads, at, member, turned, columns_ref, mean)
        entries = height * dp * breadth * fsdp
        row = jnp.zeros((1, 128), F32)
        ratio = jnp.sqrt(row + scalar_at(squares, at) / entries) / CLIP
        scale = jnp.maximum(EPS_SCALE, jnp.sqrt(row + scalar_at(scalars, MEMBERS + at) / entries))
        step = (RATE * scale / jnp.maximum(1.0, ratio))[:, :1]
        outs[slab][one] = masters[slab][one] - step * update


def vmem_call(kernel, operands, shapes, scratch):
    return pl.pallas_call(
        kernel,
        out_shape=[jax.ShapeDtypeStruct(shape, F32) for shape in shapes],
        in_specs=[pl.BlockSpec(memory_space=pltpu.VMEM)] * len(operands),
        out_specs=[pl.BlockSpec(memory_space=pltpu.VMEM)] * len(shapes),
        scratch_shapes=[pltpu.VMEM(shape, F32) for shape in scratch],
        compiler_params=pltpu.CompilerParams(vmem_limit_bytes=40 << 20),
        cost_estimate=pl.CostEstimate(flops=20000000, bytes_accessed=10000000, transcendentals=1200000),
    )(*operands)


def both_axes(value):
    return butterfly(butterfly(value, "fsdp"), "dp")


def fused_update(group, gains_part, late):
    dp, fsdp = lax.axis_size("dp"), lax.axis_size("fsdp")
    masters = [master for master, _, _, _ in group]
    grads = [gradient for _, gradient, _, _ in group]
    rows, columns = [member[2] for member in group], [member[3] for member in group]
    old_sums = jnp.concatenate([jnp.sum(state, axis=1) for state in rows]) / fsdp
    master_squares = jnp.concatenate([jnp.sum(after(master, late) ** 2, axis=(1, 2)) for master in masters])
    scalars = jnp.pad(jnp.concatenate([old_sums, master_squares])[None], ((0, 5), (0, WIDE - 2 * MEMBERS)))
    gains_rows = jnp.pad(gains_part.reshape(10, -1), ((0, 0), (0, WIDE - D // 2)))
    extra = jnp.concatenate([gains_rows, scalars], axis=0)
    old_rows, old_columns = pack_rows(rows), pack_columns(columns)
    count = len(group)
    packed_rows, packed_columns = vmem_call(
        functools.partial(sums_kernel, count), [*grads, extra], [(32, WIDE), (32, WIDE)], [(WIDE, 128)]
    )
    row_sums = butterfly(packed_rows, "fsdp")
    column_sums = butterfly(jnp.concatenate([packed_columns, row_sums[16:]], axis=0), "dp")
    new_rows, new_columns, squares = vmem_call(
        functools.partial(states_kernel, count, dp, fsdp),
        [*grads, row_sums, column_sums, old_rows, old_columns],
        [(16, WIDE), (32, WIDE), (8, 128)],
        [(128, WIDE)],
    )
    squares = both_axes(squares)
    new_masters = vmem_call(
        functools.partial(masters_kernel, count, dp, fsdp),
        [*grads, *masters, new_rows, new_columns, column_sums, squares],
        [master.shape for master in masters],
        [(128, WIDE)],
    )
    finished = []
    at = 0
    for which, (master, gradient, _, _) in enumerate(group):
        many, height, breadth = master.shape
        row_out = new_rows[at : at + many, :height]
        column_out = new_columns[2 * at : 2 * (at + many)].reshape(many, -1)[:, :breadth]
        finished.append([new_masters[which], row_out, column_out, gradient])
        at += many
    gain_total = column_sums[32:42, : D // 2].reshape(5, D)
    return finished, gain_total


def shards(
    latents,
    skip_input,
    text_tokens,
    cotangent,
    timesteps,
    text_lengths,
    positions,
    skip_weight,
    skip_rows,
    skip_columns,
    square_weight,
    square_rows,
    square_columns,
    self_weight,
    self_rows,
    self_columns,
    output_weight,
    output_rows,
    output_columns,
    text_weight,
    text_rows,
    text_columns,
    up_weight,
    up_rows,
    up_columns,
    down_weight,
    down_rows,
    down_columns,
    norm_gains,
    gain_state,
):
    dp = lax.axis_size("dp")
    d_at = lax.axis_index("dp")
    f_at = lax.axis_index("fsdp")
    y_at = f_at // 2
    c_at = f_at % 2
    index = jnp.stack([d_at, f_at]).astype(jnp.int32)

    dp_masks = masks_of("dp")

    fsdp = lax.axis_size("fsdp")
    every = ("dp", "fsdp")
    rows_d = up_weight.shape[0]
    chunk = down_weight.shape[0] // 4
    per_f = up_weight.shape[1] // (4 * chunk)
    quick = fits(rows_d)
    links = Links()
    skip_slots, wide_slots = Slots(skip_weight.shape[0]), Slots(rows_d)
    down_slots = Slots(down_weight.shape[0], True)
    text_slots = Slots(text_weight.shape[0], True)
    skip_block = skip_weight.astype(BF16)[None]
    self_block = self_weight.astype(BF16)[None]
    cross_block = jnp.stack([output_weight[0], square_weight[1], output_weight[1]]).astype(BF16)

    def advance(*flows):
        for flow in flows:
            flow.step()

    text_local = to_latent(text_tokens, y_at)
    places = to_latent(jnp.swapaxes(positions, 1, 2), y_at).T
    text_count = pick(text_lengths, y_at)
    steps = double(timesteps[None], [("dp", mask) for mask in dp_masks])
    rows_q = square_weight.shape[1]
    columns_q = square_weight.shape[2]

    if quick:
        skip_slot = slot_rows(exchange([slot_pieces(skip_block, skip_slots)])[0], skip_slots, 1)
        skip_slot = after(skip_slot, steps, places, text_local)
        skip_flow = Flow(gather_full(links, index, skip_slot, [(0, 1, skip_slots)]))
        skip_flow.step()
        early = skip_flow.pending[0]
    else:
        early = None
    joined = jnp.concatenate([to_latent(latents, y_at), to_latent(skip_input, y_at)], axis=-1).astype(F32)
    shift_block = square_weight[0].astype(BF16)[None]
    if quick:
        self_part, shift_part = after((self_block, shift_block), early)
        got = exchange([slot_pieces(self_part, wide_slots), slot_pieces(shift_part, wide_slots)])
        self_slot = jnp.concatenate([slot_rows(part, wide_slots, 1) for part in got], axis=-1)
        self_flow = Flow(gather_halves(links, index, self_slot, wide_slots))
        advance(skip_flow)
        advance(skip_flow, self_flow)
        advance(skip_flow, self_flow)
        early = skip_flow.pending[0]
    text_part, down_part, up_part, cross_part = after(
        (
            text_weight.astype(BF16)[None],
            down_weight.astype(BF16)[None],
            up_weight.astype(BF16),
            cross_block,
        ),
        early,
    )
    columns_h = per_f * chunk
    up_cuts = [
        [up_part[:, (4 * block + f) * chunk : (4 * block + f + 1) * chunk] for block in range(per_f)]
        for f in range(4)
    ]
    pieces = [
        slot_pieces(down_part, down_slots),
        jnp.stack([jnp.concatenate(cuts, axis=1) for cuts in up_cuts]),
        slot_pieces(text_part, text_slots),
    ]
    if quick:
        pieces.append(slot_pieces(cross_part, wide_slots))
    got = exchange(pieces)
    down_slot = slot_rows(got[0], down_slots, 1)[0]
    up_block = jnp.concatenate([got[1][f] for f in range(4)], axis=1)
    text_slot = slot_rows(got[2], text_slots, 1)
    if quick:
        text_flow = Flow(gather_full(links, index, text_slot, [(0, 1, text_slots)]))
        cross_flow = Flow(gather_halves(links, index, slot_rows(got[3], wide_slots, 3), wide_slots))
        up_flow = Flow(gather_dp(links, index, up_block, True))
        down_flow = Flow(gather_dp(links, index, down_slot, False))
        advance(skip_flow, self_flow)
        advance(self_flow)
    else:
        text_full = lax.all_gather(text_slot[0], every, axis=0, tiled=True)
        down_full = lax.all_gather(down_slot, "dp", axis=0, tiled=True)
    embed_own = jax.nn.silu(time_embed(pick(timesteps, y_at)[None], D)).astype(BF16)

    if quick:
        skip_full = skip_flow.finish()[0][0]
    else:
        skip_full = gather_wide(skip_block)[0]

    normed_skip, pull_skip = jax.vjp(skip_norm, joined, norm_gains[0:2].reshape(-1))
    lowered_skip = normed_skip.astype(BF16)
    stream = matmul(lowered_skip, skip_full)
    links.gate = stream
    if quick:
        advance(self_flow)
        links.gate = stream
        advance(text_flow, cross_flow)
        advance(text_flow, cross_flow, up_flow)
        both_full = self_flow.finish()[0]
        self_full, shift_full = both_full[:, : 3 * D], both_full[:, 3 * D :]
    else:
        self_full, shift_full = gather_wide(self_block)[0], gather_wide(shift_block)[0]
    shift_row = matmul(embed_own, shift_full)
    normed_self, pull_self_norm = jax.vjp(modulated, stream, norm_gains[2], shift_row)
    lowered_self = normed_self.astype(BF16)
    joint = matmul(lowered_self, self_full)
    links.gate = joint
    if quick:
        links.gate = joint
        advance(text_flow, cross_flow, up_flow)
        advance(text_flow, cross_flow, up_flow, down_flow)
        advance(text_flow, cross_flow, down_flow)

    def prepare(linear):
        return head_prep(linear, places)

    query_rows, pull_query = jax.vjp(prepare, joint[:, :D])
    key_local, pull_key = jax.vjp(prepare, joint[:, D : 2 * D])
    queries = query_rows.astype(BF16)
    key_value = jnp.stack([key_local.astype(BF16), joint[:, 2 * D :].astype(BF16)])
    key_value = jnp.concatenate([key_value, swap(key_value, *CORE)], axis=1)
    key_all, value_all = key_value[0], key_value[1]

    upstream = to_latent(after(cotangent, stream), y_at)
    upstream_pair = jnp.concatenate([upstream, swap(upstream, *YAX)], axis=0)
    upstream_far = swap(upstream_pair, *CORE)
    upstream_all = jnp.concatenate([upstream_pair, upstream_far], axis=0)
    attended, self_logsum = attend_forward(queries, key_all, value_all, None)
    attended = after(attended, upstream_far)
    links.gate = attended
    if quick:
        text_full = text_flow.finish()[0][0]
        advance(up_flow, cross_flow, down_flow)
        cross_full = cross_flow.finish()
    else:
        cross_full = gather_wide(cross_block)
    text_joint = matmul(text_local, text_full)
    text_key_local, pull_text_key = jax.vjp(head_norm, text_joint[:, :D])
    text_kv = jnp.stack([text_key_local.astype(BF16), text_joint[:, D:].astype(BF16)])
    text_kv = jnp.concatenate([text_kv, swap(text_kv, *CORE)], axis=1)
    text_key_all, text_value_all = text_kv[0], text_kv[1]

    out_self, square_cross, out_cross = cross_full[0], cross_full[1], cross_full[2]
    self_stream = stream + matmul(attended, out_self)
    normed_cross, pull_cross_norm = jax.vjp(gained, self_stream, norm_gains[3])
    lowered_cross = normed_cross.astype(BF16)
    cross_linear = matmul(lowered_cross, square_cross)
    cross_query_rows, pull_cross_query = jax.vjp(prepare, cross_linear)
    cross_queries = cross_query_rows.astype(BF16)
    own_text = text_tokens.shape[1]
    text_places = jnp.concatenate(
        [(f_at ^ mask) * own_text + jnp.arange(own_text) for mask in (0, 2, 1, 3)]
    )
    valid_keys = text_places < text_count
    cross_attended, cross_logsum = attend_forward(cross_queries, text_key_all, text_value_all, valid_keys)
    cross_stream = self_stream + matmul(cross_attended, out_cross)
    normed_mlp, pull_mlp_norm = jax.vjp(gained, cross_stream, norm_gains[4])
    lowered_mlp = spread_tokens(normed_mlp.astype(BF16))
    if quick:
        up_full = up_flow.finish().reshape(dp * rows_d, -1)
        down_full = down_flow.finish().reshape(dp * chunk, D)
    else:
        up_full = lax.all_gather(up_block, "dp", axis=0, tiled=True)
    hidden_pre = matmul(lowered_mlp, up_full)
    hidden_rows, pull_gelu = jax.vjp(gelu_tanh, hidden_pre)
    hidden_low = hidden_rows.astype(BF16)
    block_partial = matmul(hidden_low, down_full)

    back = Links()

    grad_hidden = matmul_right(upstream_all, down_full)
    grad_pre = pull_gelu(grad_hidden)[0].astype(BF16)
    mlp_partial = matmul_right(grad_pre, up_full)
    term_down = matmul_left(hidden_low, upstream_all).astype(BF16)
    down_rows_sum = lax.psum_scatter(term_down, "dp", scatter_dimension=0, tiled=True)
    term_up = matmul_left(lowered_mlp, grad_pre).astype(BF16)
    up_rows_sum = lax.psum_scatter(term_up, "dp", scatter_dimension=0, tiled=True)
    grad_mlp_in = after(collect_tokens(mlp_partial), term_down, term_up)
    block_rows = (cross_stream + collect_tokens(after(block_partial, grad_mlp_in))).astype(BF16)
    block_output = from_latent(block_rows, y_at)

    grad_cross_part, grad_gain_mlp = pull_mlp_norm(grad_mlp_in)
    grad_cross_stream = upstream.astype(F32) + grad_cross_part
    cross_low = grad_cross_stream.astype(BF16)
    grad_cross_att = matmul_right(cross_low, out_cross).astype(BF16)
    grad_cross_q, grad_text_key, grad_text_value = attend_backward(
        cross_queries, text_key_all, text_value_all, valid_keys, cross_logsum, grad_cross_att
    )
    grad_text_kv = jnp.stack([grad_text_key, grad_text_value])
    text_half = grad_text_kv.shape[1] // 2
    grad_text_got = swap(grad_text_kv[:, text_half:].astype(BF16), *CORE)
    grad_cross_linear = pull_cross_query(grad_cross_q)[0].astype(BF16)
    grad_cross_in = matmul_right(grad_cross_linear, square_cross)
    grad_self_part, grad_gain_cross = pull_cross_norm(grad_cross_in)
    grad_self_stream = grad_cross_stream + grad_self_part
    self_low = grad_self_stream.astype(BF16)
    grad_self_att = matmul_right(self_low, out_self).astype(BF16)
    cross_terms = lax.dot_general(
        jnp.stack([attended, lowered_cross, cross_attended]),
        jnp.stack([self_low, grad_cross_linear, cross_low]),
        (((1,), (1,)), ((0,), (0,))),
        preferred_element_type=F32,
    ).astype(BF16)
    if quick:
        cross_back = Flow(reduce_full(back, cross_terms))
        cross_back.step()
    grad_query, grad_key_all, grad_value_all = attend_backward(
        queries, key_all, value_all, None, self_logsum, grad_self_att
    )
    grad_kv = jnp.stack([grad_key_all, grad_value_all])
    token_half = grad_kv.shape[1] // 2
    grad_kv_got = swap(grad_kv[:, token_half:].astype(BF16), *CORE)

    grad_text_local = grad_text_kv[:, :text_half] + grad_text_got.astype(F32)
    text_grad_joint = jnp.concatenate(
        [pull_text_key(grad_text_local[0])[0], grad_text_local[1]], axis=-1
    ).astype(BF16)
    term_text = matmul_left(text_local, text_grad_joint).astype(BF16)
    text_rows_sum = lax.psum_scatter(after(term_text, term_up), every, scatter_dimension=0, tiled=True)

    grad_kv_local = grad_kv[:, :token_half] + grad_kv_got.astype(F32)
    grad_joint = jnp.concatenate(
        [pull_query(grad_query)[0], pull_key(grad_kv_local[0])[0], grad_kv_local[1]], axis=-1
    ).astype(BF16)
    term_self = matmul_left(lowered_self, grad_joint).astype(BF16)[None]
    if quick:
        back.gate = term_self
        cross_back.step()
        self_back = Flow(reduce_full(back, term_self))
        self_back.step()
    grad_self_in = matmul_right(grad_joint, self_full)
    grad_stream_part, grad_gain_self, grad_shift = pull_self_norm(grad_self_in)
    grad_stream = grad_self_stream + grad_stream_part
    stream_low = grad_stream.astype(BF16)
    term_skip = matmul_left(lowered_skip, stream_low).astype(BF16)[None]
    if quick:
        back.gate = term_skip
        skip_back = Flow(reduce_full(back, term_skip))
        skip_back.step()
    grad_skip_in = matmul_right(stream_low, skip_full)
    if quick:
        back.gate = grad_skip_in
        advance(cross_back, self_back, cross_back, self_back, skip_back, cross_back, skip_back)
    grad_joined, grad_gain_skip = pull_skip(grad_skip_in)
    first_pieces = [
        back_pieces(text_rows_sum.astype(BF16)[None]),
        back_pieces(down_rows_sum.astype(BF16)[None]),
        jnp.swapaxes(up_rows_sum.astype(BF16).reshape(rows_d, 4, per_f * chunk), 0, 1),
    ]
    if quick:
        first_pieces.append(back_pieces(cross_back.finish()))
    latents_grad = from_latent(grad_joined[:, :D].astype(BF16), y_at)
    skip_input_grad = from_latent(grad_joined[:, D:].astype(BF16), y_at)

    quiet = None
    if quick:
        advance(self_back, skip_back, self_back, skip_back)
        quiet = skip_back.pending[0]
        last_pieces = [back_pieces(self_back.finish()), back_pieces(skip_back.finish())]
        first_pieces += last_pieces
    got = exchange(first_pieces, quiet)
    text_sum = back_block(got[0], text_slots, 1).astype(F32)
    down_sum = back_block(got[1], down_slots, 1).astype(F32)
    up_cuts = [
        got[2][f][:, block * chunk : (block + 1) * chunk] for block in range(per_f) for f in range(4)
    ]
    up_sum = jnp.concatenate(up_cuts, axis=1).astype(F32)[None]
    if quick:
        cross_sum = back_block(got[3], wide_slots, 3).astype(F32)
    else:
        cross_sum = reduce_wide(cross_terms)

    embed_all = jax.nn.silu(time_embed(steps.reshape(-1), D)).astype(BF16)
    embed_part = lax.dynamic_slice_in_dim(embed_all, d_at * rows_q, rows_q, axis=1)
    grad_shift = after(grad_shift.reshape(1, D), quiet)
    grad_shift = grad_shift + swap(grad_shift, *CORE)
    other_shift = swap(grad_shift, *YAX)
    shift_pair = jnp.where(
        y_at == 0,
        jnp.concatenate([grad_shift, other_shift]),
        jnp.concatenate([other_shift, grad_shift]),
    )
    shift_pair = lax.dynamic_slice_in_dim(shift_pair, f_at * columns_q, columns_q, axis=1)
    shift_grads = double(shift_pair[None], [("dp", mask) for mask in dp_masks]).reshape(-1, columns_q)
    modulate_sum = lax.dot_general(
        embed_part.astype(F32),
        shift_grads,
        (((0,), (0,)), ((), ())),
        precision=lax.Precision.HIGHEST,
        preferred_element_type=F32,
    )

    gains_part = jnp.concatenate(
        [grad_gain_skip.reshape(2, -1), grad_gain_self[None], grad_gain_cross[None], grad_gain_mlp[None]],
        axis=0,
    )
    square_sum = jnp.stack([modulate_sum, cross_sum[1]])
    output_sum = jnp.stack([cross_sum[0], cross_sum[2]])
    early_group = [
        (square_weight, square_sum, square_rows, square_columns),
        (output_weight, output_sum, output_rows, output_columns),
        (text_weight[None], text_sum, text_rows[None], text_columns[None]),
        (up_weight[None], up_sum, up_rows[None], up_columns[None]),
        (down_weight[None], down_sum, down_rows[None], down_columns[None]),
    ]
    if quick:
        self_sum = back_block(got[4], wide_slots, 1).astype(F32)
        skip_sum = back_block(got[5], skip_slots, 1).astype(F32)
    else:
        self_sum, skip_sum = reduce_wide(term_self), reduce_wide(term_skip)
    late_group = [
        (skip_weight[None], skip_sum, skip_rows[None], skip_columns[None]),
        (self_weight[None], self_sum, self_rows[None], self_columns[None]),
    ]
    groups = late_group + early_group
    if quick:
        finished, gain_total = fused_update(groups, gains_part, joint)
    else:
        states, gain_total = statistics(groups, gains_part, joint)
        update_squares = jnp.concatenate([state[3] for state in states])
        update_all = butterfly(butterfly(update_squares, "fsdp"), "dp")
        update_split = split_all(update_all, [state[3].shape for state in states])
        finished = []
        for (master, gradient, _, _), state, update_sum in zip(groups, states, update_split):
            rows_new, columns_new, update, _, master_sum = state
            entries = gradient.shape[1] * dp * gradient.shape[2] * fsdp
            ratio = jnp.sqrt(update_sum / entries) / CLIP
            step_scale = jnp.maximum(EPS_SCALE, jnp.sqrt(master_sum / entries))
            master_new = master - (RATE * step_scale / jnp.maximum(1.0, ratio))[:, None, None] * update
            finished.append([master_new, rows_new, columns_new, gradient])
    skip_done, self_done, square_done, output_done, text_done, up_done, down_done = finished
    gain_state_new = DECAY * gain_state + (1.0 - DECAY) * (gain_total * gain_total + EPS_SQUARE)
    gain_update = gain_total * lax.rsqrt(gain_state_new)
    gain_ratio = jnp.sqrt(jnp.mean(gain_update * gain_update)) / CLIP
    gain_scale = jnp.maximum(EPS_SCALE, jnp.sqrt(jnp.mean(norm_gains * norm_gains)))
    gains_new = norm_gains - RATE * gain_scale * gain_update / jnp.maximum(1.0, gain_ratio)
    results = [block_output, latents_grad, skip_input_grad]
    for which, group in enumerate(
        [skip_done, square_done, self_done, output_done, text_done, up_done, down_done]
    ):
        if which in (1, 3):
            results.extend(group)
        else:
            results.extend(item[0] for item in group)
    return tuple(results) + (gains_new, gain_state_new, gain_total)


def solution(mesh):
    matrix, row, column = P("dp", "fsdp"), P("dp"), P("fsdp")
    pair, pair_row, pair_column = P(None, "dp", "fsdp"), P(None, "dp"), P(None, "fsdp")
    tokens = P("dp", "fsdp", None)
    kinds = (False, True, False, True, False, False, False)
    in_specs = [tokens] * 4 + [P("dp"), P("dp"), P("dp", None, "fsdp")]
    out_specs = [tokens] * 3
    for paired in kinds:
        if paired:
            in_specs += [pair, pair_row, pair_column]
            out_specs += [pair, pair_row, pair_column, pair]
        else:
            in_specs += [matrix, row, column]
            out_specs += [matrix, row, column, matrix]
    return jax.shard_map(
        shards,
        mesh=mesh,
        in_specs=tuple(in_specs + [P(), P()]),
        out_specs=tuple(out_specs + [P(), P(), P()]),
        check_vma=False,
    )
```

time: 1410 us -> 1270 us (0.901)
  waiting for transfers between devices: 574 us -> 367 us
  local copies, waits for them, and re-layouts: 237 us -> 273 us
  matrix products: 148 us -> 173 us
  other arithmetic: 238 us -> 223 us
    ppermute x102 -> x38, waiting for transfers between devices: 540 us -> 65 us  [swap(): return lax.ppermute(value, axis, [(i, i ^ mask) for i in range(size)])]
    ppermute x0 -> x74, waiting for transfers between devices: none -> 279 us  [send(): got = lax.ppermute(value, axis, pairs)]
    ppermute x0 -> x74, starting transfers between devices: none -> 92.9 us  [send(): got = lax.ppermute(value, axis, pairs)]
    ppermute x102 -> x38, starting transfers between devices: 92.9 us -> 32.1 us  [swap(): return lax.ppermute(value, axis, [(i, i ^ mask) for i in range(size)])]
    all_to_all x12 -> x4, starting transfers between devices: 44.2 us -> 16.8 us  [exchange(): got = lax.all_to_all(after(joined, gate), 'fsdp', 0, 0, tiled=False)]
    concatenate x0 -> x20, other arithmetic: none -> 22.5 us  [the longest x8 7.54 us: columns(): return jnp.concatenate([pair[..., first:last], far], axis=0)]
    another operation x15 -> x38, other arithmetic: 21.2 us -> 43.3 us
    convert_element_type x31, other arithmetic: 79.8 us -> 59.7 us  [the longest x15 40.6 us: send_half(): send = total_of([choose(view, away) for view in views]).astype(BF16)]
  transfers between devices with their start and end apart: 114 -> 119, of which waited for: 49 -> 48; matrix products, arithmetic and copies ran while one was open for 40% -> 45% of each run, Pallas kernels for 3% -> 4%
where the time goes in v2:
time: 1270 us; the launch traced here: 1250 us
  waiting for transfers between devices  367 us (29%)
  local copies, waits for them, and re-layouts  273 us (21%)
  other arithmetic  223 us (18%)
  matrix products  173 us (14%)
  starting transfers between devices  142 us (11%)
  Pallas kernels  52.9 us (4%)
  between operations  21.2 us (2%)
    ppermute x74, waiting for transfers between devices, send(): got = lax.ppermute(value, axis, pairs)  279 us
    ppermute x74, starting transfers between devices, send(): got = lax.ppermute(value, axis, pairs)  92.9 us
    unnamed x714, local copies, waits for them, and re-layouts  86 us
    ppermute x38, waiting for transfers between devices, swap(): return lax.ppermute(value, axis, [(i, i ^ mask) for i in range(size)])  65 us
    dot_general x7, matrix products, matmul_right(): lax.dot_general(left, right, (((1,), (1,)), ((), ())), preferred_element_...  48 us
    dot_general x9, matrix products, matmul(): return jnp.dot(left, right, preferred_element_type=F32)  41.5 us
    convert_element_type x15, other arithmetic, send_half(): send = total_of([choose(view, away) for view in views]).astype(BF16)  40.6 us
    dot_general x5, matrix products, matmul_left(): lax.dot_general(left, right, (((0,), (0,)), ((), ())), preferred_element_...  37 us
  transfers between devices with their start and end apart: 119, of which 48 were waited for; matrix products, arithmetic and copies ran while one was open for 45% of the time, Pallas kernels for 4%

profile of v2, /device:TPU:0, one launch (start us, length us, event | category | flops | bytes accessed | tf_op | source)
XLA Modules:
  0.0 1252.1 jit_solution(14705084804471048925)
XLA Ops:
  53.9 6.5 all-to-all-done.1
  73.9 7.3 collective-permute-done.17
  83.2 8.1 collective-permute-done.9
  100.7 17.3 %collective-permute-done.11.refs_2_ = bf16[4,1,96,1408]{3,2,1,0:T(8,128)(2,1)} collective-permute-done((bf16[4,1,96,1408]{3,2,1,0:T(8,128)(2,1)S(1)}, bf16[4,1,96,1408]{3,2,1,0:T(8,128)(2,1)}, u32[]{:S(2)}, u32[]{:S(2)}) %collective-permute-start.11) | collective-permute-done | bytes 1081376 | tf_op jit(solution)/shard_map/ppermute | solution.py:177
  122.9 9.7 collective-permute-done.19
  152.7 13.0 %collective-permute-done.20 = bf16[4,1,48,2816]{3,2,1,0:T(8,128)(2,1)} collective-permute-done((bf16[4,1,48,2816]{3,2,1,0:T(8,128)(2,1)}, bf16[4,1,48,2816]{3,2,1,0:T(8,128)(2,1)}, u32[]{:S(2)}, u32[]{:S(2)}) %collective-permute-start.20) | collective-permute-done | bytes 1081376 | tf_op jit(solution)/shard_map/ppermute | solution.py:177
  175.9 5.5 fusion.186
  204.3 25.3 %collective-permute-done.21.refs_1_ = bf16[8,1,48,2816]{3,2,1,0:T(8,128)(2,1)} collective-permute-done((bf16[8,1,48,2816]{3,2,1,0:T(8,128)(2,1)S(1)}, bf16[8,1,48,2816]{3,2,1,0:T(8,128)(2,1)}, u32[]{:S(2)}, u32[]{:S(2)}) %collective-permute-start.21) | collective-permute-done | bytes 2162720 | tf_op jit(solution)/shard_map/ppermute | solution.py:177
  246.9 8.9 collective-permute-done.35
  263.4 11.8 shard_map.550
  278.0 7.1 fusion.2
  303.4 11.6 collective-permute-done.36
  323.1 10.9 collective-permute-done.49.refs_1_
  354.5 11.0 collective-permute-done.38
  367.5 5.6 collective-permute-done.59
  379.3 15.3 %shard_map.552 = bf16[1,1024,2816]{2,1,0:T(8,128)(2,1)S(1)} custom-call(s32[2]{0:T(128)S(1)} %pad_add_fusion.12.index_ref, bf16[4,1,32,2816]{3,2,1,0:T(8,128)(2,1)S(1)} %copy-done.38, bf16[4,1,32,2816]{3,2,1,0:T(8,128)(2,1)S(1)} %copy-done.51, bf16[4,1,32,2816]{3,2,1,0:T(8,128)(2,1)} %collective-permute-done.42.refs_2_, ...), custom_call_target="tpu_custom_call" | custom-call | bytes 11534336 | tf_op jit(solution)/shard_map/pallas_call | solution.py:364
  426.0 18.7 %collective-permute-done.58 = bf16[2,176,1536]{2,1,0:T(8,128)(2,1)S(1)} collective-permute-done((bf16[2,176,1536]{2,1,0:T(8,128)(2,1)}, bf16[2,176,1536]{2,1,0:T(8,128)(2,1)S(1)}, u32[]{:S(2)}, u32[]{:S(2)}) %collective-permute-start.58) | collective-permute-done | bytes 1081376 | tf_op jit(solution)/shard_map/ppermute | solution.py:177
  456.2 8.7 shard_map.551
  471.7 6.6 copy.265
  497.3 15.3 %collective-permute-done.55 = bf16[256,1408]{1,0:T(8,128)(2,1)S(1)} collective-permute-done((bf16[256,1408]{1,0:T(8,128)(2,1)S(1)}, bf16[256,1408]{1,0:T(8,128)(2,1)S(1)}, u32[]{:S(2)}, u32[]{:S(2)}) %collective-permute-start.55) | collective-permute-done | bytes 720928 | tf_op jit(solution)/shard_map/ppermute | solution.py:144
  515.4 7.2 collective-permute-done.63
  535.4 10.8 fusion.14
  546.2 6.9 fusion.190
  557.0 11.0 convolution_convert_fusion.4
  568.1 10.5 fusion.161
  582.2 6.9 convolution_convert_fusion.3
  589.1 10.0 collective-permute-done.65
  644.0 7.3 multiply_reduce_fusion.2
  653.4 5.8 multiply_convert_fusion.2
  711.5 6.0 multiply_reduce_fusion
  726.7 9.9 convolution_convert_fusion.1
  753.6 8.1 convolution_convert_fusion
  761.8 6.1 constant_dynamic-slice_fusion.5
  788.3 9.6 multiply_reduce_fusion.5
  808.7 9.4 fusion.39
  823.8 6.8 convolution_convert_fusion.2
  830.6 30.7 %collective-permute-done.76 = bf16[3,2,2,2,48,640]{5,4,0,3,2,1:T(8,128)(2,1)} collective-permute-done((bf16[3,2,2,2,48,640]{5,4,0,3,2,1:T(8,128)(2,1)}, bf16[3,2,2,2,48,640]{5,4,0,3,2,1:T(8,128)(2,1)}, u32[]{:S(2)}, u32[]{:S(2)}) %collective-permute-start.76) | collective-permute-done | bytes 1474592 | tf_op jit(solution)/shard_map/ppermute | solution.py:177
  889.3 42.1 %collective-permute-done.75 = bf16[3,2,2,1,48,768]{5,4,0,3,2,1:T(8,128)(2,1)} collective-permute-done((bf16[3,2,2,1,48,768]{5,4,0,3,2,1:T(8,128)(2,1)}, bf16[3,2,2,1,48,768]{5,4,0,3,2,1:T(8,128)(2,1)}, u32[]{:S(2)}, u32[]{:S(2)}) %collective-permute-start.75) | collective-permute-done | bytes 884768 | tf_op jit(solution)/shard_map/ppermute | solution.py:177
  934.6 9.3 collective-permute-start.78
  952.9 6.7 collective-permute-done.78
  962.6 6.3 collective-permute-done.85
  974.9 7.8 collective-permute-start.86
  982.7 6.0 fusion.163
  1004.4 6.3 collective-permute-done.86
  1022.0 9.8 collective-permute-done.90
  1068.5 7.2 collective-permute-start.96
  1102.9 16.9 %all-to-all-done.3 = bf16[4,816,384]{2,1,0:T(8,128)(2,1)} async-done(((bf16[4,816,384]{2,1,0:T(8,128)(2,1)}), bf16[4,816,384]{2,1,0:T(8,128)(2,1)}, u32[]{:S(2)}, u32[]{:S(2)}) %all-to-all-start.3) | async-done | bytes 2506784 | tf_op jit(solution)/shard_map/all_to_all | solution.py:249
  1146.1 8.1 collective-permute-done.103
  (1398 shorter events, 717.0 us)
Async XLA Ops:
  22.7 48.3 %collective-permute-start = (bf16[128,1408]{1,0:T(8,128)(2,1)}, bf16[128,1408]{1,0:T(8,128)(2,1)S(1)}, u32[]{:S(2)}, u32[]{:S(2)}) collective-permute-start(bf16[128,1408]{1,0:T(8,128)(2,1)} %get-tuple-element.468), channel_id=1, source_target_pairs={{0,2},{1,3},{2,0},{3,1},{4,6},{5,7},{6,4},{7,5},{8,10},{9,11},{10,... | collective-permute-start | bytes 1081352 | tf_op jit(solution)/shard_map/ppermute | solution.py:144
  23.6 47.4 %collective-permute-start.1 = (bf16[128,1408]{1,0:T(8,128)(2,1)}, bf16[128,1408]{1,0:T(8,128)(2,1)}, u32[]{:S(2)}, u32[]{:S(2)}) collective-permute-start(bf16[128,1408]{1,0:T(8,128)(2,1)} %get-tuple-element.470), channel_id=1, source_target_pairs={{0,2},{1,3},{2,0},{3,1},{4,6},{5,7},{6,4},{7,5},{8,10},{9,11},{10,... | collective-permute-start | bytes 1081352 | tf_op jit(solution)/shard_map/ppermute | solution.py:144
  96.5 48.0 %collective-permute-start.12 = (bf16[4,1,96,1408]{3,2,1,0:T(8,128)(2,1)S(1)}, bf16[4,1,96,1408]{3,2,1,0:T(8,128)(2,1)}, u32[]{:S(2)}, u32[]{:S(2)}) collective-permute-start(bf16[4,1,96,1408]{3,2,1,0:T(8,128)(2,1)S(1)} %pad_maximum_fusion.20.refs_0_), channel_id=1, source_target_pairs={{0,6},{1,7},{2,4},{3,5},{4,2},{5,3},{6,0},{7,1},{8,14},{9,15},{10,... | collective-permute-start | bytes 3244040 | tf_op jit(solution)/shard_map/ppermute | solution.py:177
  98.8 33.8 %collective-permute-start.19 = (bf16[2,1,48,5632]{3,2,1,0:T(8,128)(2,1)S(1)}, bf16[2,1,48,5632]{3,2,1,0:T(8,128)(2,1)S(1)}, u32[]{:S(2)}, u32[]{:S(2)}) collective-permute-start(bf16[2,1,48,5632]{3,2,1,0:T(8,128)(2,1)S(1)} %collective-permute-done.18), channel_id=1, source_target_pairs={{8,0},{12,4},{16,24},{20,28},{9,1},{13,5},{17,25},{21,29},{10,2},{... | collective-permute-start | bytes 3244040 | tf_op jit(solution)/shard_map/ppermute | solution.py:177
  118.0 52.4 %collective-permute-start.15 = (bf16[4,1,96,1408]{3,2,1,0:T(8,128)(2,1)}, bf16[4,1,96,1408]{3,2,1,0:T(8,128)(2,1)}, u32[]{:S(2)}, u32[]{:S(2)}) collective-permute-start(bf16[4,1,96,1408]{3,2,1,0:T(8,128)(2,1)} %collective-permute-done.11.refs_2_), channel_id=1, source_target_pairs={{0,1},{1,0},{2,3},{3,2},{4,5},{5,4},{6,7},{7,6},{8,9},{9,8},{10,11... | collective-permute-start | bytes 3244040 | tf_op jit(solution)/shard_map/ppermute | solution.py:177
  134.7 31.0 %collective-permute-start.20 = (bf16[4,1,48,2816]{3,2,1,0:T(8,128)(2,1)}, bf16[4,1,48,2816]{3,2,1,0:T(8,128)(2,1)}, u32[]{:S(2)}, u32[]{:S(2)}) collective-permute-start(bf16[4,1,48,2816]{3,2,1,0:T(8,128)(2,1)} %pad_maximum_fusion.21), channel_id=1, source_target_pairs={{0,2},{1,3},{2,0},{3,1},{4,6},{5,7},{6,4},{7,5},{8,10},{9,11},{10,... | collective-permute-start | bytes 3244040 | tf_op jit(solution)/shard_map/ppermute | solution.py:177
  148.2 39.1 %all-to-all-start.2 = ((bf16[4,576,384]{2,1,0:T(8,128)(2,1)}), bf16[4,576,384]{2,1,0:T(8,128)(2,1)}, u32[]{:S(2)}, u32[]{:S(2)}) async-start(bf16[4,576,384]{2,1,0:T(8,128)(2,1)} %fusion.63), calls=%async_computation.2 | async-start | bytes 3538944 | tf_op jit(solution)/shard_map/all_to_all | solution.py:249
  152.6 836.1 %reduce-scatter.6.cloned.1.call-start = ((), (), s32[]{:S(2)}) async-start(), calls=%async_computation.8 | async-start | bytes 4866048 | tf_op jit(solution)/shard_map/reduce_scatter | solution.py:1103
  181.4 48.2 %collective-permute-start.21 = (bf16[8,1,48,2816]{3,2,1,0:T(8,128)(2,1)S(1)}, bf16[8,1,48,2816]{3,2,1,0:T(8,128)(2,1)}, u32[]{:S(2)}, u32[]{:S(2)}) collective-permute-start(bf16[8,1,48,2816]{3,2,1,0:T(8,128)(2,1)S(1)} %pad_maximum_fusion.5.refs_0_), channel_id=1, source_target_pairs={{0,4},{4,0},{8,12},{12,8},{16,20},{20,16},{24,28},{28,24},{1,5},{5... | collective-permute-start | bytes 6488072 | tf_op jit(solution)/shard_map/ppermute | solution.py:177
  181.9 48.7 %collective-permute-start.22 = (bf16[8,1,48,2816]{3,2,1,0:T(8,128)(2,1)S(1)}, bf16[8,1,48,2816]{3,2,1,0:T(8,128)(2,1)}, u32[]{:S(2)}, u32[]{:S(2)}) collective-permute-start(bf16[8,1,48,2816]{3,2,1,0:T(8,128)(2,1)S(1)} %pad_maximum_fusion.5.refs_0_), channel_id=1, source_target_pairs={{0,1},{1,0},{2,3},{3,2},{4,5},{5,4},{6,7},{7,6},{8,9},{9,8},{10,11... | collective-permute-start | bytes 6488072 | tf_op jit(solution)/shard_map/ppermute | solution.py:177
  181.9 50.1 %collective-permute-start.25 = (bf16[8,1,48,2816]{3,2,1,0:T(8,128)(2,1)}, bf16[8,1,48,2816]{3,2,1,0:T(8,128)(2,1)}, u32[]{:S(2)}, u32[]{:S(2)}) collective-permute-start(bf16[8,1,48,2816]{3,2,1,0:T(8,128)(2,1)} %pad_maximum_fusion.6.refs_4_), channel_id=1, source_target_pairs={{0,2},{1,3},{2,0},{3,1},{4,6},{5,7},{6,4},{7,5},{8,10},{9,11},{10,... | collective-permute-start | bytes 6488072 | tf_op jit(solution)/shard_map/ppermute | solution.py:177
  182.5 49.5 %collective-permute-start.26 = (bf16[8,1,48,2816]{3,2,1,0:T(8,128)(2,1)}, bf16[8,1,48,2816]{3,2,1,0:T(8,128)(2,1)}, u32[]{:S(2)}, u32[]{:S(2)}) collective-permute-start(bf16[8,1,48,2816]{3,2,1,0:T(8,128)(2,1)} %pad_maximum_fusion.6.refs_4_), channel_id=1, source_target_pairs={{0,1},{1,0},{2,3},{3,2},{4,5},{5,4},{6,7},{7,6},{8,9},{9,8},{10,11... | collective-permute-start | bytes 6488072 | tf_op jit(solution)/shard_map/ppermute | solution.py:177
  203.4 29.7 %collective-permute-start.34 = (bf16[1,32,2816]{2,1,0:T(8,128)(2,1)S(1)}, bf16[1,32,2816]{2,1,0:T(8,128)(2,1)S(1)}, u32[]{:S(2)}, u32[]{:S(2)}) collective-permute-start(bf16[1,32,2816]{2,1,0:T(8,128)(2,1)S(1)} %copy-done.260), channel_id=1, source_target_pairs={{0,8},{4,12},{8,0},{12,4},{16,24},{20,28},{24,16},{28,20},{1,9},{5... | collective-permute-start | bytes 540680 | tf_op jit(solution)/shard_map/ppermute | solution.py:177
  230.6 32.8 %collective-permute-start.23 = (bf16[8,1,48,2816]{3,2,1,0:T(8,128)(2,1)}, bf16[8,1,48,2816]{3,2,1,0:T(8,128)(2,1)S(1)}, u32[]{:S(2)}, u32[]{:S(2)}) collective-permute-start(bf16[8,1,48,2816]{3,2,1,0:T(8,128)(2,1)} %collective-permute-done.21.refs_1_), channel_id=1, source_target_pairs={{0,1},{1,0},{2,3},{3,2},{4,5},{5,4},{6,7},{7,6},{8,9},{9,8},{10,11... | collective-permute-start | bytes 6488072 | tf_op jit(solution)/shard_map/ppermute | solution.py:177
  232.0 31.3 %collective-permute-start.27 = (bf16[8,1,48,2816]{3,2,1,0:T(8,128)(2,1)}, bf16[8,1,48,2816]{3,2,1,0:T(8,128)(2,1)S(1)}, u32[]{:S(2)}, u32[]{:S(2)}) collective-permute-start(bf16[8,1,48,2816]{3,2,1,0:T(8,128)(2,1)} %collective-permute-done.25.refs_5_), channel_id=1, source_target_pairs={{0,1},{1,0},{2,3},{3,2},{4,5},{5,4},{6,7},{7,6},{8,9},{9,8},{10,11... | collective-permute-start | bytes 6488072 | tf_op jit(solution)/shard_map/ppermute | solution.py:177
  233.2 52.0 %collective-permute-start.40 = (bf16[2,1,32,2816]{3,2,1,0:T(8,128)(2,1)S(1)}, bf16[2,1,32,2816]{3,2,1,0:T(8,128)(2,1)}, u32[]{:S(2)}, u32[]{:S(2)}) collective-permute-start(bf16[2,1,32,2816]{3,2,1,0:T(8,128)(2,1)S(1)} %pad_maximum_fusion.46), channel_id=1, source_target_pairs={{8,16},{12,20},{16,8},{20,12},{9,17},{13,21},{17,9},{21,13},{10,18... | collective-permute-start | bytes 1081352 | tf_op jit(solution)/shard_map/ppermute | solution.py:177
  255.8 31.2 %collective-permute-start.33 = (bf16[2,3,48,1408]{3,2,1,0:T(8,128)(2,1)S(1)}, bf16[2,3,48,1408]{3,2,1,0:T(8,128)(2,1)}, u32[]{:S(2)}, u32[]{:S(2)}) collective-permute-start(bf16[2,3,48,1408]{3,2,1,0:T(8,128)(2,1)S(1)} %pad_maximum_fusion.25), channel_id=1, source_target_pairs={{8,16},{12,20},{16,8},{20,12},{9,17},{13,21},{17,9},{21,13},{10,18... | collective-permute-start | bytes 2433032 | tf_op jit(solution)/shard_map/ppermute | solution.py:177
  289.6 46.0 %collective-permute-start.57 = (bf16[2,176,1536]{2,1,0:T(8,128)(2,1)}, bf16[2,176,1536]{2,1,0:T(8,128)(2,1)}, u32[]{:S(2)}, u32[]{:S(2)}) collective-permute-start(bf16[2,176,1536]{2,1,0:T(8,128)(2,1)} %pad_maximum_fusion.23), channel_id=1, source_target_pairs={{8,16},{12,20},{16,8},{20,12},{9,17},{13,21},{17,9},{21,13},{10,18... | collective-permute-start | bytes 3244040 | tf_op jit(solution)/shard_map/ppermute | solution.py:177
  299.2 37.0 %collective-permute-start.28 = (bf16[2,256,1408]{2,1,0:T(8,128)(2,1)S(1)}, bf16[2,256,1408]{2,1,0:T(8,128)(2,1)S(1)}, u32[]{:S(2)}, u32[]{:S(2)}) collective-permute-start(bf16[2,256,1408]{2,1,0:T(8,128)(2,1)S(1)} %pad_maximum_fusion.14), channel_id=1, source_target_pairs={{0,1},{1,0},{2,3},{3,2},{4,5},{5,4},{6,7},{7,6},{8,9},{9,8},{10,11... | collective-permute-start | bytes 4325384 | tf_op jit(solution)/shard_map/ppermute | solution.py:144
  321.7 29.6 %collective-permute-start.31 = (bf16[512,1408]{1,0:T(8,128)(2,1)}, bf16[512,1408]{1,0:T(8,128)(2,1)}, u32[]{:S(2)}, u32[]{:S(2)}) collective-permute-start(bf16[512,1408]{1,0:T(8,128)(2,1)} %pad_maximum_fusion.15), channel_id=1, source_target_pairs={{0,1},{1,0},{2,3},{3,2},{4,5},{5,4},{6,7},{7,6},{8,9},{9,8},{10,11... | collective-permute-start | bytes 4325384 | tf_op jit(solution)/shard_map/ppermute | solution.py:144
  334.1 31.4 %collective-permute-start.38 = (bf16[4,3,48,640]{3,2,1,0:T(8,128)(2,1)}, bf16[4,3,48,640]{3,2,1,0:T(8,128)(2,1)}, u32[]{:S(2)}, u32[]{:S(2)}) collective-permute-start(bf16[4,3,48,640]{3,2,1,0:T(8,128)(2,1)} %pad_maximum_fusion.30), channel_id=1, source_target_pairs={{0,4},{4,0},{8,12},{12,8},{16,20},{20,16},{24,28},{28,24},{1,5},{5... | collective-permute-start | bytes 2211848 | tf_op jit(solution)/shard_map/ppermute | solution.py:177
  335.6 40.2 %collective-permute-start.37 = (bf16[4,3,48,768]{3,2,1,0:T(8,128)(2,1)}, bf16[4,3,48,768]{3,2,1,0:T(8,128)(2,1)}, u32[]{:S(2)}, u32[]{:S(2)}) collective-permute-start(bf16[4,3,48,768]{3,2,1,0:T(8,128)(2,1)} %pad_maximum_fusion.27), channel_id=1, source_target_pairs={{0,2},{1,3},{2,0},{3,1},{4,6},{5,7},{6,4},{7,5},{8,10},{9,11},{10,... | collective-permute-start | bytes 2654216 | tf_op jit(solution)/shard_map/ppermute | solution.py:177
  349.7 29.0 %collective-permute-start.44 = (bf16[4,1,32,2816]{3,2,1,0:T(8,128)(2,1)}, bf16[4,1,32,2816]{3,2,1,0:T(8,128)(2,1)S(1)}, u32[]{:S(2)}, u32[]{:S(2)}) collective-permute-start(bf16[4,1,32,2816]{3,2,1,0:T(8,128)(2,1)} %collective-permute-done.42.refs_2_), channel_id=1, source_target_pairs={{0,1},{1,0},{2,3},{3,2},{4,5},{5,4},{6,7},{7,6},{8,9},{9,8},{10,11... | collective-permute-start | bytes 2162696 | tf_op jit(solution)/shard_map/ppermute | solution.py:177
  366.8 57.9 %collective-permute-start.47 = (bf16[8,3,48,640]{3,2,1,0:T(8,128)(2,1)S(1)}, bf16[8,3,48,640]{3,2,1,0:T(8,128)(2,1)}, u32[]{:S(2)}, u32[]{:S(2)}) collective-permute-start(bf16[8,3,48,640]{3,2,1,0:T(8,128)(2,1)S(1)} %pad_maximum_fusion.13.refs_4_), channel_id=1, source_target_pairs={{0,2},{1,3},{2,0},{3,1},{4,6},{5,7},{6,4},{7,5},{8,10},{9,11},{10,... | collective-permute-start | bytes 4423688 | tf_op jit(solution)/shard_map/ppermute | solution.py:177
  374.6 42.2 %collective-permute-start.61 = (bf16[2,192,1408]{2,1,0:T(8,128)(2,1)}, bf16[2,192,1408]{2,1,0:T(8,128)(2,1)}, u32[]{:S(2)}, u32[]{:S(2)}) collective-permute-start(bf16[2,192,1408]{2,1,0:T(8,128)(2,1)} %get-tuple-element.172), channel_id=1, source_target_pairs={{0,8},{4,12},{8,0},{12,4},{16,24},{20,28},{24,16},{28,20},{1,9},{5... | collective-permute-start | bytes 3244040 | tf_op jit(solution)/shard_map/ppermute | solution.py:177
  377.1 43.8 %collective-permute-start.39 = (bf16[8,3,48,768]{3,2,1,0:T(8,128)(2,1)S(1)}, bf16[8,3,48,768]{3,2,1,0:T(8,128)(2,1)}, u32[]{:S(2)}, u32[]{:S(2)}) collective-permute-start(bf16[8,3,48,768]{3,2,1,0:T(8,128)(2,1)S(1)} %pad_maximum_fusion.12.refs_0_), channel_id=1, source_target_pairs={{0,4},{4,0},{8,12},{12,8},{16,20},{20,16},{24,28},{28,24},{1,5},{5... | collective-permute-start | bytes 5308424 | tf_op jit(solution)/shard_map/ppermute | solution.py:177
  378.8 45.8 %collective-permute-start.45 = (bf16[8,3,48,768]{3,2,1,0:T(8,128)(2,1)S(1)}, bf16[8,3,48,768]{3,2,1,0:T(8,128)(2,1)}, u32[]{:S(2)}, u32[]{:S(2)}) collective-permute-start(bf16[8,3,48,768]{3,2,1,0:T(8,128)(2,1)S(1)} %pad_maximum_fusion.12.refs_0_), channel_id=1, source_target_pairs={{0,1},{1,0},{2,3},{3,2},{4,5},{5,4},{6,7},{7,6},{8,9},{9,8},{10,11... | collective-permute-start | bytes 5308424 | tf_op jit(solution)/shard_map/ppermute | solution.py:177
  378.8 47.1 %collective-permute-start.52 = (bf16[8,3,48,640]{3,2,1,0:T(8,128)(2,1)S(1)}, bf16[8,3,48,640]{3,2,1,0:T(8,128)(2,1)}, u32[]{:S(2)}, u32[]{:S(2)}) collective-permute-start(bf16[8,3,48,640]{3,2,1,0:T(8,128)(2,1)S(1)} %pad_maximum_fusion.13.refs_4_), channel_id=1, source_target_pairs={{0,1},{1,0},{2,3},{3,2},{4,5},{5,4},{6,7},{7,6},{8,9},{9,8},{10,11... | collective-permute-start | bytes 4423688 | tf_op jit(solution)/shard_map/ppermute | solution.py:177
  421.0 31.1 %collective-permute-start.62 = (bf16[2,2,192,1408]{3,2,1,0:T(8,128)(2,1)}, bf16[2,2,192,1408]{3,2,1,0:T(8,128)(2,1)}, u32[]{:S(2)}, u32[]{:S(2)}) collective-permute-start(bf16[2,2,192,1408]{3,2,1,0:T(8,128)(2,1)} %pad_maximum_fusion.8), channel_id=1, source_target_pairs={{8,16},{12,20},{16,8},{20,12},{9,17},{13,21},{17,9},{21,13},{10,18... | collective-permute-start | bytes 6488072 | tf_op jit(solution)/shard_map/ppermute | solution.py:177
  424.7 28.7 %collective-permute-start.46 = (bf16[8,3,48,768]{3,2,1,0:T(8,128)(2,1)}, bf16[8,3,48,768]{3,2,1,0:T(8,128)(2,1)}, u32[]{:S(2)}, u32[]{:S(2)}) collective-permute-start(bf16[8,3,48,768]{3,2,1,0:T(8,128)(2,1)} %collective-permute-done.39.refs_1_), channel_id=1, source_target_pairs={{0,1},{1,0},{2,3},{3,2},{4,5},{5,4},{6,7},{7,6},{8,9},{9,8},{10,11... | collective-permute-start | bytes 5308424 | tf_op jit(solution)/shard_map/ppermute | solution.py:177
  445.1 67.7 %collective-permute-start.60 = (bf16[4,176,1536]{2,1,0:T(8,128)(2,1)S(1)}, bf16[4,176,1536]{2,1,0:T(8,128)(2,1)}, u32[]{:S(2)}, u32[]{:S(2)}) collective-permute-start(bf16[4,176,1536]{2,1,0:T(8,128)(2,1)S(1)} %pad_maximum_fusion.7.refs_0_), channel_id=1, source_target_pairs={{0,4},{4,0},{8,12},{12,8},{16,20},{20,16},{24,28},{28,24},{1,5},{5... | collective-permute-start | bytes 6488072 | tf_op jit(solution)/shard_map/ppermute | solution.py:177
  452.1 70.5 %collective-permute-start.63 = (bf16[2,2,192,1408]{3,2,1,0:T(8,128)(2,1)}, bf16[2,2,192,1408]{3,2,1,0:T(8,128)(2,1)}, u32[]{:S(2)}, u32[]{:S(2)}) collective-permute-start(bf16[2,2,192,1408]{3,2,1,0:T(8,128)(2,1)} %collective-permute-done.62), channel_id=1, source_target_pairs={{8,0},{12,4},{16,24},{20,28},{9,1},{13,5},{17,25},{21,29},{10,2},{... | collective-permute-start | bytes 6488072 | tf_op jit(solution)/shard_map/ppermute | solution.py:177
  628.6 424.5 %reduce-scatter.4.cloned.1.call-start = ((), (), s32[]{:S(2)}) async-start(), calls=%async_computation.7 | async-start | bytes 5947392 | tf_op jit(solution)/shard_map/reduce_scatter | solution.py:1147
  709.9 353.0 %reduce-scatter.8.cloned.1.call-start = ((), (), s32[]{:S(2)}) async-start(), calls=%async_computation.9 | async-start | bytes 4866048 | tf_op jit(solution)/shard_map/reduce_scatter | solution.py:1105
  743.6 55.2 %collective-permute-start.73 = (bf16[3,2,2,2,96,1408]{5,4,0,3,2,1:T(8,128)(2,1)}, bf16[3,2,2,2,96,1408]{5,4,0,3,2,1:T(8,128)(2,1)}, u32[]{:S(2)}, u32[]{:S(2)}) collective-permute-start(bf16[3,2,2,2,96,1408]{5,4,0,3,2,1:T(8,128)(2,1)} %copy.303), channel_id=1, source_target_pairs={{0,1},{1,0},{2,3},{3,2},{4,5},{5,4},{6,7},{7,6},{8,9},{9,8},{10,11... | collective-permute-start | bytes 19464200 | tf_op jit(solution)/shard_map/ppermute | solution.py:177
  767.9 100.1 %collective-permute-start.81 = (bf16[1,2,2,2,96,4224]{5,4,3,2,1,0:T(8,128)(2,1)}, bf16[1,2,2,2,96,4224]{5,4,3,2,1,0:T(8,128)(2,1)}, u32[]{:S(2)}, u32[]{:S(2)}) collective-permute-start(bf16[1,2,2,2,96,4224]{5,4,3,2,1,0:T(8,128)(2,1)} %constant_dynamic-slice_fusion.5), channel_id=1, source_target_pairs={{0,1},{1,0},{2,3},{3,2},{4,5},{5,4},{6,7},{7,6},{8,9},{9,8},{10,11... | collective-permute-start | bytes 19464200 | tf_op jit(solution)/shard_map/ppermute | solution.py:177
  787.2 355.8 %collective-permute-start.68 = (bf16[128,1408]{1,0:T(8,128)(2,1)}, bf16[128,1408]{1,0:T(8,128)(2,1)}, u32[]{:S(2)}, u32[]{:S(2)}) collective-permute-start(bf16[128,1408]{1,0:T(8,128)(2,1)} %get-tuple-element.464), channel_id=1, source_target_pairs={{0,2},{1,3},{2,0},{3,1},{4,6},{5,7},{6,4},{7,5},{8,10},{9,11},{10,... | collective-permute-start | bytes 1081352 | tf_op jit(solution)/shard_map/ppermute | solution.py:144
  802.8 58.5 %collective-permute-start.76 = (bf16[3,2,2,2,48,640]{5,4,0,3,2,1:T(8,128)(2,1)}, bf16[3,2,2,2,48,640]{5,4,0,3,2,1:T(8,128)(2,1)}, u32[]{:S(2)}, u32[]{:S(2)}) collective-permute-start(bf16[3,2,2,2,48,640]{5,4,0,3,2,1:T(8,128)(2,1)} %add_convert_fusion.3), channel_id=1, source_target_pairs={{0,2},{1,3},{2,0},{3,1},{4,6},{5,7},{6,4},{7,5},{8,10},{9,11},{10,... | collective-permute-start | bytes 4423688 | tf_op jit(solution)/shard_map/ppermute | solution.py:177
  808.0 66.5 %collective-permute-start.74 = (bf16[3,2,2,1,96,768]{5,4,0,3,2,1:T(8,128)(2,1)}, bf16[3,2,2,1,96,768]{5,4,0,3,2,1:T(8,128)(2,1)}, u32[]{:S(2)}, u32[]{:S(2)}) collective-permute-start(bf16[3,2,2,1,96,768]{5,4,0,3,2,1:T(8,128)(2,1)} %add_convert_fusion), channel_id=1, source_target_pairs={{0,4},{4,0},{8,12},{12,8},{16,20},{20,16},{24,28},{28,24},{1,5},{5... | collective-permute-start | bytes 5308424 | tf_op jit(solution)/shard_map/ppermute | solution.py:177
  871.8 72.8 %collective-permute-start.84 = (bf16[1,2,2,2,48,2048]{5,4,3,2,1,0:T(8,128)(2,1)}, bf16[1,2,2,2,48,2048]{5,4,3,2,1,0:T(8,128)(2,1)}, u32[]{:S(2)}, u32[]{:S(2)}) collective-permute-start(bf16[1,2,2,2,48,2048]{5,4,3,2,1,0:T(8,128)(2,1)} %add_convert_fusion.2), channel_id=1, source_target_pairs={{0,2},{1,3},{2,0},{3,1},{4,6},{5,7},{6,4},{7,5},{8,10},{9,11},{10,... | collective-permute-start | bytes 4718600 | tf_op jit(solution)/shard_map/ppermute | solution.py:177
  877.5 54.0 %collective-permute-start.75 = (bf16[3,2,2,1,48,768]{5,4,0,3,2,1:T(8,128)(2,1)}, bf16[3,2,2,1,48,768]{5,4,0,3,2,1:T(8,128)(2,1)}, u32[]{:S(2)}, u32[]{:S(2)}) collective-permute-start(bf16[3,2,2,1,48,768]{5,4,0,3,2,1:T(8,128)(2,1)} %add_convert_fusion.8), channel_id=1, source_target_pairs={{0,2},{1,3},{2,0},{3,1},{4,6},{5,7},{6,4},{7,5},{8,10},{9,11},{10,... | collective-permute-start | bytes 2654216 | tf_op jit(solution)/shard_map/ppermute | solution.py:177
  881.0 68.1 %collective-permute-start.82 = (bf16[1,2,2,1,96,2176]{5,4,3,2,1,0:T(8,128)(2,1)}, bf16[1,2,2,1,96,2176]{5,4,3,2,1,0:T(8,128)(2,1)}, u32[]{:S(2)}, u32[]{:S(2)}) collective-permute-start(bf16[1,2,2,1,96,2176]{5,4,3,2,1,0:T(8,128)(2,1)} %add_convert_fusion.1), channel_id=1, source_target_pairs={{0,4},{4,0},{8,12},{12,8},{16,20},{20,16},{24,28},{28,24},{1,5},{5... | collective-permute-start | bytes 5013512 | tf_op jit(solution)/shard_map/ppermute | solution.py:177
  886.5 111.3 %collective-permute-start.89 = (bf16[1,2,2,2,192,1408]{5,4,3,2,1,0:T(8,128)(2,1)}, bf16[1,2,2,2,192,1408]{5,4,3,2,1,0:T(8,128)(2,1)}, u32[]{:S(2)}, u32[]{:S(2)}) collective-permute-start(bf16[1,2,2,2,192,1408]{5,4,3,2,1,0:T(8,128)(2,1)} %constant_dynamic-slice_fusion.1), channel_id=1, source_target_pairs={{0,1},{1,0},{2,3},{3,2},{4,5},{5,4},{6,7},{7,6},{8,9},{9,8},{10,11... | collective-permute-start | bytes 12976136 | tf_op jit(solution)/shard_map/ppermute | solution.py:177
  960.7 32.8 %collective-permute-start.79 = (bf16[3,1,2,1,48,1408]{5,4,0,3,2,1:T(8,128)(2,1)}, bf16[3,1,2,1,48,1408]{5,4,0,3,2,1:T(8,128)(2,1)}, u32[]{:S(2)}, u32[]{:S(2)}) collective-permute-start(bf16[3,1,2,1,48,1408]{5,4,0,3,2,1:T(8,128)(2,1)} %add_convert_fusion.12), channel_id=1, source_target_pairs={{8,16},{12,20},{16,8},{20,12},{9,17},{13,21},{17,9},{21,13},{10,18... | collective-permute-start | bytes 2433032 | tf_op jit(solution)/shard_map/ppermute | solution.py:177
  974.9 35.9 %collective-permute-start.86 = (bf16[1,1,2,1,48,4224]{5,4,3,2,1,0:T(8,128)(2,1)}, bf16[1,1,2,1,48,4224]{5,4,3,2,1,0:T(8,128)(2,1)}, u32[]{:S(2)}, u32[]{:S(2)}) collective-permute-start(bf16[1,1,2,1,48,4224]{5,4,3,2,1,0:T(8,128)(2,1)} %fusion.86), channel_id=1, source_target_pairs={{0,8},{4,12},{24,16},{28,20},{1,9},{5,13},{25,17},{29,21},{2,10},{... | collective-permute-start | bytes 2433032 | tf_op jit(solution)/shard_map/ppermute | solution.py:177
  995.4 40.4 %collective-permute-start.80 = (bf16[3,1,1,1,48,1408]{5,4,0,3,2,1:T(8,128)(2,1)}, bf16[3,1,1,1,48,1408]{5,4,0,3,2,1:T(8,128)(2,1)}, u32[]{:S(2)}, u32[]{:S(2)}) collective-permute-start(bf16[3,1,1,1,48,1408]{5,4,0,3,2,1:T(8,128)(2,1)} %add_convert_fusion.30), channel_id=1, source_target_pairs={{0,8},{4,12},{8,0},{12,4},{16,24},{20,28},{24,16},{28,20},{1,9},{5... | collective-permute-start | bytes 1216520 | tf_op jit(solution)/shard_map/ppermute | solution.py:177
  1013.0 38.3 %collective-permute-start.87 = (bf16[1,1,2,1,48,4224]{5,4,3,2,1,0:T(8,128)(2,1)}, bf16[1,1,2,1,48,4224]{5,4,3,2,1,0:T(8,128)(2,1)}, u32[]{:S(2)}, u32[]{:S(2)}) collective-permute-start(bf16[1,1,2,1,48,4224]{5,4,3,2,1,0:T(8,128)(2,1)} %add_convert_fusion.11), channel_id=1, source_target_pairs={{8,16},{12,20},{16,8},{20,12},{9,17},{13,21},{17,9},{21,13},{10,18... | collective-permute-start | bytes 2433032 | tf_op jit(solution)/shard_map/ppermute | solution.py:177
  1084.8 35.0 %all-to-all-start.3 = ((bf16[4,816,384]{2,1,0:T(8,128)(2,1)}), bf16[4,816,384]{2,1,0:T(8,128)(2,1)}, u32[]{:S(2)}, u32[]{:S(2)}) async-start(bf16[4,816,384]{2,1,0:T(8,128)(2,1)} %pad_dynamic-update-slice_fusion.3), calls=%async_computation.6 | async-start | bytes 5013504 | tf_op jit(solution)/shard_map/all_to_all | solution.py:249
  (419 other events, 4071.9 us)
Sparse Core Ops, SparseCore 0:
  628.7 103.6 reduce-scatter.5
  734.8 151.0 reduce-scatter.3
  889.9 114.9 reduce-scatter.7

commit v3 on v2

--- a/solution.py
+++ b/solution.py
@@ -1021,9 +1021,11 @@
     links.gate = stream
     if quick:
         advance(self_flow)
+        links.gate = None
+        advance(cross_flow)
         links.gate = stream
-        advance(text_flow, cross_flow)
-        advance(text_flow, cross_flow, up_flow)
+        advance(text_flow)
+        advance(text_flow, up_flow)
         both_full = self_flow.finish()[0]
         self_full, shift_full = both_full[:, : 3 * D], both_full[:, 3 * D :]
     else:
@@ -1031,13 +1033,17 @@
     shift_row = matmul(embed_own, shift_full)
     normed_self, pull_self_norm = jax.vjp(modulated, stream, norm_gains[2], shift_row)
     lowered_self = normed_self.astype(BF16)
+    if quick:
+        links.gate = None
+        lowered_self = cross_flow.step(lowered_self)
     joint = matmul(lowered_self, self_full)
     links.gate = joint
     if quick:
+        advance(cross_flow)
         links.gate = joint
-        advance(text_flow, cross_flow, up_flow)
+        advance(text_flow, up_flow)
         advance(text_flow, cross_flow, up_flow, down_flow)
-        advance(text_flow, cross_flow, down_flow)
+        advance(text_flow, down_flow)
 
     def prepare(linear):
         return head_prep(linear, places)
@@ -1144,31 +1150,31 @@
         [pull_text_key(grad_text_local[0])[0], grad_text_local[1]], axis=-1
     ).astype(BF16)
     term_text = matmul_left(text_local, text_grad_joint).astype(BF16)
-    text_rows_sum = lax.psum_scatter(after(term_text, term_up), every, scatter_dimension=0, tiled=True)
-
+    text_rows_sum = lax.psum_scatter(after(term_text, up_rows_sum), every, scatter_dimension=0, tiled=True)
+
+    if quick:
+        grad_kv_got = cross_back.step(grad_kv_got)
     grad_kv_local = grad_kv[:, :token_half] + grad_kv_got.astype(F32)
     grad_joint = jnp.concatenate(
         [pull_query(grad_query)[0], pull_key(grad_kv_local[0])[0], grad_kv_local[1]], axis=-1
     ).astype(BF16)
     term_self = matmul_left(lowered_self, grad_joint).astype(BF16)[None]
     if quick:
-        back.gate = term_self
-        cross_back.step()
         self_back = Flow(reduce_full(back, term_self))
         self_back.step()
     grad_self_in = matmul_right(grad_joint, self_full)
     grad_stream_part, grad_gain_self, grad_shift = pull_self_norm(grad_self_in)
     grad_stream = grad_self_stream + grad_stream_part
     stream_low = grad_stream.astype(BF16)
+    if quick:
+        stream_low = self_back.step(cross_back.step(stream_low))
     term_skip = matmul_left(lowered_skip, stream_low).astype(BF16)[None]
     if quick:
-        back.gate = term_skip
         skip_back = Flow(reduce_full(back, term_skip))
         skip_back.step()
     grad_skip_in = matmul_right(stream_low, skip_full)
     if quick:
-        back.gate = grad_skip_in
-        advance(cross_back, self_back, cross_back, self_back, skip_back, cross_back, skip_back)
+        advance(cross_back, self_back, skip_back, cross_back, skip_back)
     grad_joined, grad_gain_skip = pull_skip(grad_skip_in)
     first_pieces = [
         back_pieces(text_rows_sum.astype(BF16)[None]),

time: 1270 us -> 1260 us (level)
  starting transfers between devices: 142 us -> 169 us
  local copies, waits for them, and re-layouts: 273 us -> 252 us
    ppermute x74, starting transfers between devices: 92.9 us -> 114 us  [send(): got = lax.ppermute(value, axis, pairs)]
    unnamed x714 -> x718, local copies, waits for them, and re-layouts: 86 us -> 78.7 us
  transfers between devices with their start and end apart: 119 -> 119, of which waited for: 48 -> 52; matrix products, arithmetic and copies ran while one was open for 45% -> 44% of each run, Pallas kernels for 4% -> 4%
where the time goes in v3:
time: 1260 us; the launch traced here: 1240 us
  waiting for transfers between devices  365 us (29%)
  local copies, waits for them, and re-layouts  252 us (20%)
  other arithmetic  218 us (17%)
  starting transfers between devices  169 us (13%)
  matrix products  164 us (13%)
  Pallas kernels  54.8 us (4%)
  between operations  21 us (2%)
    ppermute x74, waiting for transfers between devices, send(): got = lax.ppermute(value, axis, pairs)  267 us
    ppermute x74, starting transfers between devices, send(): got = lax.ppermute(value, axis, pairs)  114 us
    unnamed x718, local copies, waits for them, and re-layouts  78.7 us
    ppermute x38, waiting for transfers between devices, swap(): return lax.ppermute(value, axis, [(i, i ^ mask) for i in range(size)])  75.9 us
    dot_general x7, matrix products, matmul_right(): lax.dot_general(left, right, (((1,), (1,)), ((), ())), preferred_element_...  48.1 us
    dot_general x9, matrix products, matmul(): return jnp.dot(left, right, preferred_element_type=F32)  40.2 us
    convert_element_type x15, other arithmetic, send_half(): send = total_of([choose(view, away) for view in views]).astype(BF16)  38.1 us
    ppermute x38, starting transfers between devices, swap(): return lax.ppermute(value, axis, [(i, i ^ mask) for i in range(size)])  37.8 us
  transfers between devices with their start and end apart: 119, of which 52 were waited for; matrix products, arithmetic and copies ran while one was open for 44% of the time, Pallas kernels for 4%

profile of v3, /device:TPU:0, one launch (start us, length us, event | category | flops | bytes accessed | tf_op | source)
XLA Modules:
  0.0 1243.5 jit_solution(14287070467048840419)
XLA Ops:
  53.9 6.5 all-to-all-done.1
  73.9 7.3 collective-permute-done.17
  83.2 8.1 collective-permute-done.9
  100.3 17.7 %collective-permute-done.11.refs_2_ = bf16[4,1,96,1408]{3,2,1,0:T(8,128)(2,1)} collective-permute-done((bf16[4,1,96,1408]{3,2,1,0:T(8,128)(2,1)S(1)}, bf16[4,1,96,1408]{3,2,1,0:T(8,128)(2,1)}, u32[]{:S(2)}, u32[]{:S(2)}) %collective-permute-start.11) | collective-permute-done | bytes 1081376 | tf_op jit(solution)/shard_map/ppermute | solution.py:177
  122.9 9.7 collective-permute-done.19
  152.7 12.9 %collective-permute-done.20 = bf16[4,1,48,2816]{3,2,1,0:T(8,128)(2,1)} collective-permute-done((bf16[4,1,48,2816]{3,2,1,0:T(8,128)(2,1)}, bf16[4,1,48,2816]{3,2,1,0:T(8,128)(2,1)}, u32[]{:S(2)}, u32[]{:S(2)}) %collective-permute-start.20) | collective-permute-done | bytes 1081376 | tf_op jit(solution)/shard_map/ppermute | solution.py:177
  170.4 5.5 shard_map.549
  196.6 9.8 collective-permute-done.28
  206.6 22.6 %collective-permute-done.21.refs_1_ = bf16[8,1,48,2816]{3,2,1,0:T(8,128)(2,1)} collective-permute-done((bf16[8,1,48,2816]{3,2,1,0:T(8,128)(2,1)S(1)}, bf16[8,1,48,2816]{3,2,1,0:T(8,128)(2,1)}, u32[]{:S(2)}, u32[]{:S(2)}) %collective-permute-start.21) | collective-permute-done | bytes 2162720 | tf_op jit(solution)/shard_map/ppermute | solution.py:177
  236.0 9.3 collective-permute-done.30
  253.9 8.7 collective-permute-done.31
  263.9 11.8 shard_map.550
  278.9 7.0 fusion.2
  305.5 10.1 collective-permute-done.35
  346.3 10.7 collective-permute-done.48
  360.0 6.9 collective-permute-done.41
  368.4 7.0 collective-permute-start.61
  378.4 15.5 %shard_map.552 = bf16[1,1024,2816]{2,1,0:T(8,128)(2,1)S(1)} custom-call(s32[2]{0:T(128)S(1)} %pad_add_fusion.12.index_ref, bf16[4,1,32,2816]{3,2,1,0:T(8,128)(2,1)S(1)} %copy-done.42, bf16[4,1,32,2816]{3,2,1,0:T(8,128)(2,1)S(1)} %copy-done.55, bf16[4,1,32,2816]{3,2,1,0:T(8,128)(2,1)} %collective-permute-done.43.refs_2_, ...), custom_call_target="tpu_custom_call" | custom-call | bytes 11534336 | tf_op jit(solution)/shard_map/pallas_call | solution.py:364
  426.8 17.7 %collective-permute-done.59 = bf16[2,176,1536]{2,1,0:T(8,128)(2,1)S(1)} collective-permute-done((bf16[2,176,1536]{2,1,0:T(8,128)(2,1)}, bf16[2,176,1536]{2,1,0:T(8,128)(2,1)S(1)}, u32[]{:S(2)}, u32[]{:S(2)}) %collective-permute-start.59) | collective-permute-done | bytes 1081376 | tf_op jit(solution)/shard_map/ppermute | solution.py:177
  457.5 10.2 shard_map.551
  473.9 6.4 copy.266
  498.5 15.4 %collective-permute-done.56 = bf16[256,1408]{1,0:T(8,128)(2,1)S(1)} collective-permute-done((bf16[256,1408]{1,0:T(8,128)(2,1)S(1)}, bf16[256,1408]{1,0:T(8,128)(2,1)S(1)}, u32[]{:S(2)}, u32[]{:S(2)}) %collective-permute-start.56) | collective-permute-done | bytes 720928 | tf_op jit(solution)/shard_map/ppermute | solution.py:144
  516.7 5.6 collective-permute-done.63
  532.5 9.8 fusion.14
  544.0 6.4 convolution_convert_fusion.3
  550.5 8.4 fusion.190
  559.2 9.8 fusion.161
  571.9 9.2 convolution_convert_fusion.4
  581.1 7.9 collective-permute-done.65
  619.6 9.4 collective-permute-done.67
  676.7 9.3 convolution_convert_fusion.1
  699.0 6.6 multiply_reduce_fusion
  743.0 7.8 convolution_convert_fusion
  750.8 6.1 constant_dynamic-slice_fusion.9
  773.7 25.2 %collective-permute-done.72 = bf16[3,2,2,2,48,640]{5,4,0,3,2,1:T(8,128)(2,1)} collective-permute-done((bf16[3,2,2,2,48,640]{5,4,0,3,2,1:T(8,128)(2,1)}, bf16[3,2,2,2,48,640]{5,4,0,3,2,1:T(8,128)(2,1)}, u32[]{:S(2)}, u32[]{:S(2)}) %collective-permute-start.72) | collective-permute-done | bytes 1474592 | tf_op jit(solution)/shard_map/ppermute | solution.py:177
  801.9 11.5 collective-permute-done.71
  815.8 9.0 multiply_reduce_fusion.5
  824.8 8.7 collective-permute-done.78
  835.4 14.9 %collective-permute-done.77 = bf16[3,2,2,1,48,768]{5,4,0,3,2,1:T(8,128)(2,1)S(1)} collective-permute-done((bf16[3,2,2,1,48,768]{5,4,0,3,2,1:T(8,128)(2,1)S(1)}, bf16[3,2,2,1,48,768]{5,4,0,3,2,1:T(8,128)(2,1)S(1)}, u32[]{:S(2)}, u32[]{:S(2)}) %collective-permute-start.77) | collective-permute-done | bytes 884768 | tf_op jit(solution)/shard_map/ppermute | solution.py:177
  852.3 35.3 %collective-permute-start.79 = (bf16[3,1,2,1,48,1408]{5,4,0,3,2,1:T(8,128)(2,1)S(1)}, bf16[3,1,2,1,48,1408]{5,4,0,3,2,1:T(8,128)(2,1)}, u32[]{:S(2)}, u32[]{:S(2)}) collective-permute-start(bf16[3,1,2,1,48,1408]{5,4,0,3,2,1:T(8,128)(2,1)S(1)} %fusion.84), channel_id=1, source_target_pairs={{0,8},{4,12},{24,16},{28,20},{1,9},{5,13},{25,17},{29,21},{2,10},{... | collective-permute-start | bytes 2433032 | tf_op jit(solution)/shard_map/ppermute | solution.py:177
  892.0 14.6 %collective-permute-done.79 = bf16[3,1,2,1,48,1408]{5,4,0,3,2,1:T(8,128)(2,1)} collective-permute-done((bf16[3,1,2,1,48,1408]{5,4,0,3,2,1:T(8,128)(2,1)S(1)}, bf16[3,1,2,1,48,1408]{5,4,0,3,2,1:T(8,128)(2,1)}, u32[]{:S(2)}, u32[]{:S(2)}) %collective-permute-start.79) | collective-permute-done | bytes 811040 | tf_op jit(solution)/shard_map/ppermute | solution.py:177
  953.6 6.1 collective-permute-done.84
  969.7 6.5 collective-permute-done.85
  995.7 8.0 fusion.39
  1003.7 8.1 collective-permute-done.92
  1016.0 7.1 collective-permute-done.90
  1095.9 15.4 %all-to-all-done.3 = bf16[4,816,384]{2,1,0:T(8,128)(2,1)} async-done(((bf16[4,816,384]{2,1,0:T(8,128)(2,1)}), bf16[4,816,384]{2,1,0:T(8,128)(2,1)}, u32[]{:S(2)}, u32[]{:S(2)}) %all-to-all-start.3) | async-done | bytes 2506784 | tf_op jit(solution)/shard_map/all_to_all | solution.py:249
  1137.5 8.1 collective-permute-done.103
  (1403 shorter events, 710.9 us)
Async XLA Ops:
  22.7 48.3 %collective-permute-start = (bf16[128,1408]{1,0:T(8,128)(2,1)}, bf16[128,1408]{1,0:T(8,128)(2,1)S(1)}, u32[]{:S(2)}, u32[]{:S(2)}) collective-permute-start(bf16[128,1408]{1,0:T(8,128)(2,1)} %get-tuple-element.462), channel_id=1, source_target_pairs={{0,2},{1,3},{2,0},{3,1},{4,6},{5,7},{6,4},{7,5},{8,10},{9,11},{10,... | collective-permute-start | bytes 1081352 | tf_op jit(solution)/shard_map/ppermute | solution.py:144
  23.6 47.4 %collective-permute-start.1 = (bf16[128,1408]{1,0:T(8,128)(2,1)}, bf16[128,1408]{1,0:T(8,128)(2,1)}, u32[]{:S(2)}, u32[]{:S(2)}) collective-permute-start(bf16[128,1408]{1,0:T(8,128)(2,1)} %get-tuple-element.464), channel_id=1, source_target_pairs={{0,2},{1,3},{2,0},{3,1},{4,6},{5,7},{6,4},{7,5},{8,10},{9,11},{10,... | collective-permute-start | bytes 1081352 | tf_op jit(solution)/shard_map/ppermute | solution.py:144
  96.5 48.0 %collective-permute-start.12 = (bf16[4,1,96,1408]{3,2,1,0:T(8,128)(2,1)S(1)}, bf16[4,1,96,1408]{3,2,1,0:T(8,128)(2,1)}, u32[]{:S(2)}, u32[]{:S(2)}) collective-permute-start(bf16[4,1,96,1408]{3,2,1,0:T(8,128)(2,1)S(1)} %pad_maximum_fusion.20.refs_0_), channel_id=1, source_target_pairs={{0,6},{1,7},{2,4},{3,5},{4,2},{5,3},{6,0},{7,1},{8,14},{9,15},{10,... | collective-permute-start | bytes 3244040 | tf_op jit(solution)/shard_map/ppermute | solution.py:177
  98.8 33.8 %collective-permute-start.19 = (bf16[2,1,48,5632]{3,2,1,0:T(8,128)(2,1)S(1)}, bf16[2,1,48,5632]{3,2,1,0:T(8,128)(2,1)S(1)}, u32[]{:S(2)}, u32[]{:S(2)}) collective-permute-start(bf16[2,1,48,5632]{3,2,1,0:T(8,128)(2,1)S(1)} %collective-permute-done.18), channel_id=1, source_target_pairs={{8,0},{12,4},{16,24},{20,28},{9,1},{13,5},{17,25},{21,29},{10,2},{... | collective-permute-start | bytes 3244040 | tf_op jit(solution)/shard_map/ppermute | solution.py:177
  118.0 52.4 %collective-permute-start.15 = (bf16[4,1,96,1408]{3,2,1,0:T(8,128)(2,1)}, bf16[4,1,96,1408]{3,2,1,0:T(8,128)(2,1)}, u32[]{:S(2)}, u32[]{:S(2)}) collective-permute-start(bf16[4,1,96,1408]{3,2,1,0:T(8,128)(2,1)} %collective-permute-done.11.refs_2_), channel_id=1, source_target_pairs={{0,1},{1,0},{2,3},{3,2},{4,5},{5,4},{6,7},{7,6},{8,9},{9,8},{10,11... | collective-permute-start | bytes 3244040 | tf_op jit(solution)/shard_map/ppermute | solution.py:177
  134.6 31.0 %collective-permute-start.20 = (bf16[4,1,48,2816]{3,2,1,0:T(8,128)(2,1)}, bf16[4,1,48,2816]{3,2,1,0:T(8,128)(2,1)}, u32[]{:S(2)}, u32[]{:S(2)}) collective-permute-start(bf16[4,1,48,2816]{3,2,1,0:T(8,128)(2,1)} %pad_maximum_fusion.21), channel_id=1, source_target_pairs={{0,2},{1,3},{2,0},{3,1},{4,6},{5,7},{6,4},{7,5},{8,10},{9,11},{10,... | collective-permute-start | bytes 3244040 | tf_op jit(solution)/shard_map/ppermute | solution.py:177
  148.2 37.6 %all-to-all-start.2 = ((bf16[4,576,384]{2,1,0:T(8,128)(2,1)}), bf16[4,576,384]{2,1,0:T(8,128)(2,1)}, u32[]{:S(2)}, u32[]{:S(2)}) async-start(bf16[4,576,384]{2,1,0:T(8,128)(2,1)} %fusion.63), calls=%async_computation.2 | async-start | bytes 3538944 | tf_op jit(solution)/shard_map/all_to_all | solution.py:249
  152.6 621.0 %reduce-scatter.4.cloned.1.call-start = ((), (), s32[]{:S(2)}) async-start(), calls=%async_computation.7 | async-start | bytes 4866048 | tf_op jit(solution)/shard_map/reduce_scatter | solution.py:1111
  181.0 48.2 %collective-permute-start.21 = (bf16[8,1,48,2816]{3,2,1,0:T(8,128)(2,1)S(1)}, bf16[8,1,48,2816]{3,2,1,0:T(8,128)(2,1)}, u32[]{:S(2)}, u32[]{:S(2)}) collective-permute-start(bf16[8,1,48,2816]{3,2,1,0:T(8,128)(2,1)S(1)} %pad_maximum_fusion.5.refs_0_), channel_id=1, source_target_pairs={{0,4},{4,0},{8,12},{12,8},{16,20},{20,16},{24,28},{28,24},{1,5},{5... | collective-permute-start | bytes 6488072 | tf_op jit(solution)/shard_map/ppermute | solution.py:177
  181.5 47.7 %collective-permute-start.22 = (bf16[8,1,48,2816]{3,2,1,0:T(8,128)(2,1)S(1)}, bf16[8,1,48,2816]{3,2,1,0:T(8,128)(2,1)}, u32[]{:S(2)}, u32[]{:S(2)}) collective-permute-start(bf16[8,1,48,2816]{3,2,1,0:T(8,128)(2,1)S(1)} %pad_maximum_fusion.5.refs_0_), channel_id=1, source_target_pairs={{0,1},{1,0},{2,3},{3,2},{4,5},{5,4},{6,7},{7,6},{8,9},{9,8},{10,11... | collective-permute-start | bytes 6488072 | tf_op jit(solution)/shard_map/ppermute | solution.py:177
  181.5 49.8 %collective-permute-start.25 = (bf16[8,1,48,2816]{3,2,1,0:T(8,128)(2,1)}, bf16[8,1,48,2816]{3,2,1,0:T(8,128)(2,1)}, u32[]{:S(2)}, u32[]{:S(2)}) collective-permute-start(bf16[8,1,48,2816]{3,2,1,0:T(8,128)(2,1)} %pad_maximum_fusion.6.refs_4_), channel_id=1, source_target_pairs={{0,2},{1,3},{2,0},{3,1},{4,6},{5,7},{6,4},{7,5},{8,10},{9,11},{10,... | collective-permute-start | bytes 6488072 | tf_op jit(solution)/shard_map/ppermute | solution.py:177
  182.1 49.2 %collective-permute-start.26 = (bf16[8,1,48,2816]{3,2,1,0:T(8,128)(2,1)}, bf16[8,1,48,2816]{3,2,1,0:T(8,128)(2,1)}, u32[]{:S(2)}, u32[]{:S(2)}) collective-permute-start(bf16[8,1,48,2816]{3,2,1,0:T(8,128)(2,1)} %pad_maximum_fusion.6.refs_4_), channel_id=1, source_target_pairs={{0,1},{1,0},{2,3},{3,2},{4,5},{5,4},{6,7},{7,6},{8,9},{9,8},{10,11... | collective-permute-start | bytes 6488072 | tf_op jit(solution)/shard_map/ppermute | solution.py:177
  229.2 34.7 %collective-permute-start.23 = (bf16[8,1,48,2816]{3,2,1,0:T(8,128)(2,1)}, bf16[8,1,48,2816]{3,2,1,0:T(8,128)(2,1)S(1)}, u32[]{:S(2)}, u32[]{:S(2)}) collective-permute-start(bf16[8,1,48,2816]{3,2,1,0:T(8,128)(2,1)} %collective-permute-done.21.refs_1_), channel_id=1, source_target_pairs={{0,1},{1,0},{2,3},{3,2},{4,5},{5,4},{6,7},{7,6},{8,9},{9,8},{10,11... | collective-permute-start | bytes 6488072 | tf_op jit(solution)/shard_map/ppermute | solution.py:177
  231.3 32.6 %collective-permute-start.27 = (bf16[8,1,48,2816]{3,2,1,0:T(8,128)(2,1)}, bf16[8,1,48,2816]{3,2,1,0:T(8,128)(2,1)S(1)}, u32[]{:S(2)}, u32[]{:S(2)}) collective-permute-start(bf16[8,1,48,2816]{3,2,1,0:T(8,128)(2,1)} %collective-permute-done.25.refs_5_), channel_id=1, source_target_pairs={{0,1},{1,0},{2,3},{3,2},{4,5},{5,4},{6,7},{7,6},{8,9},{9,8},{10,11... | collective-permute-start | bytes 6488072 | tf_op jit(solution)/shard_map/ppermute | solution.py:177
  246.1 41.7 %collective-permute-start.33 = (bf16[2,3,48,1408]{3,2,1,0:T(8,128)(2,1)S(1)}, bf16[2,3,48,1408]{3,2,1,0:T(8,128)(2,1)}, u32[]{:S(2)}, u32[]{:S(2)}) collective-permute-start(bf16[2,3,48,1408]{3,2,1,0:T(8,128)(2,1)S(1)} %pad_maximum_fusion.25), channel_id=1, source_target_pairs={{8,16},{12,20},{16,8},{20,12},{9,17},{13,21},{17,9},{21,13},{10,18... | collective-permute-start | bytes 2433032 | tf_op jit(solution)/shard_map/ppermute | solution.py:177
  251.4 34.6 %collective-permute-start.37 = (bf16[2,1,32,2816]{3,2,1,0:T(8,128)(2,1)S(1)}, bf16[2,1,32,2816]{3,2,1,0:T(8,128)(2,1)}, u32[]{:S(2)}, u32[]{:S(2)}) collective-permute-start(bf16[2,1,32,2816]{3,2,1,0:T(8,128)(2,1)S(1)} %pad_maximum_fusion.46), channel_id=1, source_target_pairs={{8,16},{12,20},{16,8},{20,12},{9,17},{13,21},{17,9},{21,13},{10,18... | collective-permute-start | bytes 1081352 | tf_op jit(solution)/shard_map/ppermute | solution.py:177
  290.4 34.4 %collective-permute-start.58 = (bf16[2,176,1536]{2,1,0:T(8,128)(2,1)}, bf16[2,176,1536]{2,1,0:T(8,128)(2,1)}, u32[]{:S(2)}, u32[]{:S(2)}) collective-permute-start(bf16[2,176,1536]{2,1,0:T(8,128)(2,1)} %pad_maximum_fusion.23), channel_id=1, source_target_pairs={{8,16},{12,20},{16,8},{20,12},{9,17},{13,21},{17,9},{21,13},{10,18... | collective-permute-start | bytes 3244040 | tf_op jit(solution)/shard_map/ppermute | solution.py:177
  323.7 33.2 %collective-permute-start.48 = (bf16[4,3,48,640]{3,2,1,0:T(8,128)(2,1)}, bf16[4,3,48,640]{3,2,1,0:T(8,128)(2,1)}, u32[]{:S(2)}, u32[]{:S(2)}) collective-permute-start(bf16[4,3,48,640]{3,2,1,0:T(8,128)(2,1)} %pad_maximum_fusion.30), channel_id=1, source_target_pairs={{0,4},{4,0},{8,12},{12,8},{16,20},{20,16},{24,28},{28,24},{1,5},{5... | collective-permute-start | bytes 2211848 | tf_op jit(solution)/shard_map/ppermute | solution.py:177
  324.8 50.6 %collective-permute-start.36 = (bf16[4,3,48,768]{3,2,1,0:T(8,128)(2,1)}, bf16[4,3,48,768]{3,2,1,0:T(8,128)(2,1)}, u32[]{:S(2)}, u32[]{:S(2)}) collective-permute-start(bf16[4,3,48,768]{3,2,1,0:T(8,128)(2,1)} %pad_maximum_fusion.27), channel_id=1, source_target_pairs={{0,2},{1,3},{2,0},{3,1},{4,6},{5,7},{6,4},{7,5},{8,10},{9,11},{10,... | collective-permute-start | bytes 2654216 | tf_op jit(solution)/shard_map/ppermute | solution.py:177
  342.8 35.6 %collective-permute-start.45 = (bf16[4,1,32,2816]{3,2,1,0:T(8,128)(2,1)}, bf16[4,1,32,2816]{3,2,1,0:T(8,128)(2,1)S(1)}, u32[]{:S(2)}, u32[]{:S(2)}) collective-permute-start(bf16[4,1,32,2816]{3,2,1,0:T(8,128)(2,1)} %collective-permute-done.43.refs_2_), channel_id=1, source_target_pairs={{0,1},{1,0},{2,3},{3,2},{4,5},{5,4},{6,7},{7,6},{8,9},{9,8},{10,11... | collective-permute-start | bytes 2162696 | tf_op jit(solution)/shard_map/ppermute | solution.py:177
  342.8 35.5 %collective-permute-start.52 = (bf16[4,1,32,2816]{3,2,1,0:T(8,128)(2,1)}, bf16[4,1,32,2816]{3,2,1,0:T(8,128)(2,1)S(1)}, u32[]{:S(2)}, u32[]{:S(2)}) collective-permute-start(bf16[4,1,32,2816]{3,2,1,0:T(8,128)(2,1)} %collective-permute-done.50.refs_3_), channel_id=1, source_target_pairs={{0,1},{1,0},{2,3},{3,2},{4,5},{5,4},{6,7},{7,6},{8,9},{9,8},{10,11... | collective-permute-start | bytes 2162696 | tf_op jit(solution)/shard_map/ppermute | solution.py:177
  358.3 66.1 %collective-permute-start.49 = (bf16[8,3,48,640]{3,2,1,0:T(8,128)(2,1)S(1)}, bf16[8,3,48,640]{3,2,1,0:T(8,128)(2,1)}, u32[]{:S(2)}, u32[]{:S(2)}) collective-permute-start(bf16[8,3,48,640]{3,2,1,0:T(8,128)(2,1)S(1)} %pad_maximum_fusion.13.refs_4_), channel_id=1, source_target_pairs={{0,2},{1,3},{2,0},{3,1},{4,6},{5,7},{6,4},{7,5},{8,10},{9,11},{10,... | collective-permute-start | bytes 4423688 | tf_op jit(solution)/shard_map/ppermute | solution.py:177
  368.4 48.1 %collective-permute-start.61 = (bf16[2,192,1408]{2,1,0:T(8,128)(2,1)}, bf16[2,192,1408]{2,1,0:T(8,128)(2,1)}, u32[]{:S(2)}, u32[]{:S(2)}) collective-permute-start(bf16[2,192,1408]{2,1,0:T(8,128)(2,1)} %get-tuple-element.170), channel_id=1, source_target_pairs={{0,8},{4,12},{8,0},{12,4},{16,24},{20,28},{24,16},{28,20},{1,9},{5... | collective-permute-start | bytes 3244040 | tf_op jit(solution)/shard_map/ppermute | solution.py:177
  376.8 43.9 %collective-permute-start.42 = (bf16[8,3,48,768]{3,2,1,0:T(8,128)(2,1)S(1)}, bf16[8,3,48,768]{3,2,1,0:T(8,128)(2,1)}, u32[]{:S(2)}, u32[]{:S(2)}) collective-permute-start(bf16[8,3,48,768]{3,2,1,0:T(8,128)(2,1)S(1)} %pad_maximum_fusion.12.refs_0_), channel_id=1, source_target_pairs={{0,4},{4,0},{8,12},{12,8},{16,20},{20,16},{24,28},{28,24},{1,5},{5... | collective-permute-start | bytes 5308424 | tf_op jit(solution)/shard_map/ppermute | solution.py:177
  378.4 45.9 %collective-permute-start.46 = (bf16[8,3,48,768]{3,2,1,0:T(8,128)(2,1)S(1)}, bf16[8,3,48,768]{3,2,1,0:T(8,128)(2,1)}, u32[]{:S(2)}, u32[]{:S(2)}) collective-permute-start(bf16[8,3,48,768]{3,2,1,0:T(8,128)(2,1)S(1)} %pad_maximum_fusion.12.refs_0_), channel_id=1, source_target_pairs={{0,1},{1,0},{2,3},{3,2},{4,5},{5,4},{6,7},{7,6},{8,9},{9,8},{10,11... | collective-permute-start | bytes 5308424 | tf_op jit(solution)/shard_map/ppermute | solution.py:177
  416.5 28.0 %collective-permute-start.59 = (bf16[2,176,1536]{2,1,0:T(8,128)(2,1)}, bf16[2,176,1536]{2,1,0:T(8,128)(2,1)S(1)}, u32[]{:S(2)}, u32[]{:S(2)}) collective-permute-start(bf16[2,176,1536]{2,1,0:T(8,128)(2,1)} %collective-permute-done.58), channel_id=1, source_target_pairs={{8,0},{12,4},{16,24},{20,28},{9,1},{13,5},{17,25},{21,29},{10,2},{... | collective-permute-start | bytes 3244040 | tf_op jit(solution)/shard_map/ppermute | solution.py:177
  420.7 31.2 %collective-permute-start.62 = (bf16[2,2,192,1408]{3,2,1,0:T(8,128)(2,1)}, bf16[2,2,192,1408]{3,2,1,0:T(8,128)(2,1)}, u32[]{:S(2)}, u32[]{:S(2)}) collective-permute-start(bf16[2,2,192,1408]{3,2,1,0:T(8,128)(2,1)} %pad_maximum_fusion.8), channel_id=1, source_target_pairs={{8,16},{12,20},{16,8},{20,12},{9,17},{13,21},{17,9},{21,13},{10,18... | collective-permute-start | bytes 6488072 | tf_op jit(solution)/shard_map/ppermute | solution.py:177
  424.4 28.8 %collective-permute-start.47 = (bf16[8,3,48,768]{3,2,1,0:T(8,128)(2,1)}, bf16[8,3,48,768]{3,2,1,0:T(8,128)(2,1)}, u32[]{:S(2)}, u32[]{:S(2)}) collective-permute-start(bf16[8,3,48,768]{3,2,1,0:T(8,128)(2,1)} %collective-permute-done.42.refs_1_), channel_id=1, source_target_pairs={{0,1},{1,0},{2,3},{3,2},{4,5},{5,4},{6,7},{7,6},{8,9},{9,8},{10,11... | collective-permute-start | bytes 5308424 | tf_op jit(solution)/shard_map/ppermute | solution.py:177
  444.9 69.2 %collective-permute-start.60 = (bf16[4,176,1536]{2,1,0:T(8,128)(2,1)S(1)}, bf16[4,176,1536]{2,1,0:T(8,128)(2,1)}, u32[]{:S(2)}, u32[]{:S(2)}) collective-permute-start(bf16[4,176,1536]{2,1,0:T(8,128)(2,1)S(1)} %pad_maximum_fusion.7.refs_0_), channel_id=1, source_target_pairs={{0,4},{4,0},{8,12},{12,8},{16,20},{20,16},{24,28},{28,24},{1,5},{5... | collective-permute-start | bytes 6488072 | tf_op jit(solution)/shard_map/ppermute | solution.py:177
  451.9 70.3 %collective-permute-start.63 = (bf16[2,2,192,1408]{3,2,1,0:T(8,128)(2,1)}, bf16[2,2,192,1408]{3,2,1,0:T(8,128)(2,1)}, u32[]{:S(2)}, u32[]{:S(2)}) collective-permute-start(bf16[2,2,192,1408]{3,2,1,0:T(8,128)(2,1)} %collective-permute-done.62), channel_id=1, source_target_pairs={{8,0},{12,4},{16,24},{20,28},{9,1},{13,5},{17,25},{21,29},{10,2},{... | collective-permute-start | bytes 6488072 | tf_op jit(solution)/shard_map/ppermute | solution.py:177
  550.5 394.4 %reduce-scatter.8.cloned.1.call-start = ((), (), s32[]{:S(2)}) async-start(), calls=%async_computation.9 | async-start | bytes 4866048 | tf_op jit(solution)/shard_map/reduce_scatter | solution.py:1109
  615.7 429.2 %reduce-scatter.6.cloned.1.call-start = ((), (), s32[]{:S(2)}) async-start(), calls=%async_computation.8 | async-start | bytes 5947392 | tf_op jit(solution)/shard_map/reduce_scatter | solution.py:1153
  667.6 57.2 %collective-permute-start.76 = (bf16[2,168,1408]{2,1,0:T(8,128)(2,1)}, bf16[2,168,1408]{2,1,0:T(8,128)(2,1)}, u32[]{:S(2)}, u32[]{:S(2)}) collective-permute-start(bf16[2,168,1408]{2,1,0:T(8,128)(2,1)} %fusion.61), channel_id=1, source_target_pairs={{0,1},{1,0},{2,3},{3,2},{4,5},{5,4},{6,7},{7,6},{8,9},{9,8},{10,11... | collective-permute-start | bytes 2838536 | tf_op jit(solution)/shard_map/ppermute | solution.py:144
  692.7 44.1 %collective-permute-start.70 = (bf16[3,2,2,2,96,1408]{5,4,0,3,2,1:T(8,128)(2,1)}, bf16[3,2,2,2,96,1408]{5,4,0,3,2,1:T(8,128)(2,1)}, u32[]{:S(2)}, u32[]{:S(2)}) collective-permute-start(bf16[3,2,2,2,96,1408]{5,4,0,3,2,1:T(8,128)(2,1)} %copy.302), channel_id=1, source_target_pairs={{0,1},{1,0},{2,3},{3,2},{4,5},{5,4},{6,7},{7,6},{8,9},{9,8},{10,11... | collective-permute-start | bytes 19464200 | tf_op jit(solution)/shard_map/ppermute | solution.py:177
  756.8 153.6 %collective-permute-start.73 = (bf16[1,2,2,2,96,4224]{5,4,3,2,1,0:T(8,128)(2,1)}, bf16[1,2,2,2,96,4224]{5,4,3,2,1,0:T(8,128)(2,1)}, u32[]{:S(2)}, u32[]{:S(2)}) collective-permute-start(bf16[1,2,2,2,96,4224]{5,4,3,2,1,0:T(8,128)(2,1)} %constant_dynamic-slice_fusion.9), channel_id=1, source_target_pairs={{0,1},{1,0},{2,3},{3,2},{4,5},{5,4},{6,7},{7,6},{8,9},{9,8},{10,11... | collective-permute-start | bytes 19464200 | tf_op jit(solution)/shard_map/ppermute | solution.py:177
  763.5 35.4 %collective-permute-start.72 = (bf16[3,2,2,2,48,640]{5,4,0,3,2,1:T(8,128)(2,1)}, bf16[3,2,2,2,48,640]{5,4,0,3,2,1:T(8,128)(2,1)}, u32[]{:S(2)}, u32[]{:S(2)}) collective-permute-start(bf16[3,2,2,2,48,640]{5,4,0,3,2,1:T(8,128)(2,1)} %add_convert_fusion.3), channel_id=1, source_target_pairs={{0,2},{1,3},{2,0},{3,1},{4,6},{5,7},{6,4},{7,5},{8,10},{9,11},{10,... | collective-permute-start | bytes 4423688 | tf_op jit(solution)/shard_map/ppermute | solution.py:177
  767.8 45.6 %collective-permute-start.71 = (bf16[3,2,2,1,96,768]{5,4,0,3,2,1:T(8,128)(2,1)S(1)}, bf16[3,2,2,1,96,768]{5,4,0,3,2,1:T(8,128)(2,1)}, u32[]{:S(2)}, u32[]{:S(2)}) collective-permute-start(bf16[3,2,2,1,96,768]{5,4,0,3,2,1:T(8,128)(2,1)S(1)} %add_convert_fusion), channel_id=1, source_target_pairs={{0,4},{4,0},{8,12},{12,8},{16,20},{20,16},{24,28},{28,24},{1,5},{5... | collective-permute-start | bytes 5308424 | tf_op jit(solution)/shard_map/ppermute | solution.py:177
  801.4 32.1 %collective-permute-start.78 = (bf16[3,2,2,1,48,640]{5,4,0,3,2,1:T(8,128)(2,1)}, bf16[3,2,2,1,48,640]{5,4,0,3,2,1:T(8,128)(2,1)S(1)}, u32[]{:S(2)}, u32[]{:S(2)}) collective-permute-start(bf16[3,2,2,1,48,640]{5,4,0,3,2,1:T(8,128)(2,1)} %add_convert_fusion.16), channel_id=1, source_target_pairs={{0,4},{4,0},{8,12},{12,8},{16,20},{20,16},{24,28},{28,24},{1,5},{5... | collective-permute-start | bytes 2211848 | tf_op jit(solution)/shard_map/ppermute | solution.py:177
  815.5 34.8 %collective-permute-start.77 = (bf16[3,2,2,1,48,768]{5,4,0,3,2,1:T(8,128)(2,1)S(1)}, bf16[3,2,2,1,48,768]{5,4,0,3,2,1:T(8,128)(2,1)S(1)}, u32[]{:S(2)}, u32[]{:S(2)}) collective-permute-start(bf16[3,2,2,1,48,768]{5,4,0,3,2,1:T(8,128)(2,1)S(1)} %add_convert_fusion.8), channel_id=1, source_target_pairs={{0,2},{1,3},{2,0},{3,1},{4,6},{5,7},{6,4},{7,5},{8,10},{9,11},{10,... | collective-permute-start | bytes 2654216 | tf_op jit(solution)/shard_map/ppermute | solution.py:177
  852.3 54.3 %collective-permute-start.79 = (bf16[3,1,2,1,48,1408]{5,4,0,3,2,1:T(8,128)(2,1)S(1)}, bf16[3,1,2,1,48,1408]{5,4,0,3,2,1:T(8,128)(2,1)}, u32[]{:S(2)}, u32[]{:S(2)}) collective-permute-start(bf16[3,1,2,1,48,1408]{5,4,0,3,2,1:T(8,128)(2,1)S(1)} %fusion.84), channel_id=1, source_target_pairs={{0,8},{4,12},{24,16},{28,20},{1,9},{5,13},{25,17},{29,21},{2,10},{... | collective-permute-start | bytes 2433032 | tf_op jit(solution)/shard_map/ppermute | solution.py:177
  908.8 29.7 %collective-permute-start.80 = (bf16[3,1,2,1,48,1408]{5,4,0,3,2,1:T(8,128)(2,1)}, bf16[3,1,2,1,48,1408]{5,4,0,3,2,1:T(8,128)(2,1)}, u32[]{:S(2)}, u32[]{:S(2)}) collective-permute-start(bf16[3,1,2,1,48,1408]{5,4,0,3,2,1:T(8,128)(2,1)} %add_convert_fusion.12), channel_id=1, source_target_pairs={{8,16},{12,20},{16,8},{20,12},{9,17},{13,21},{17,9},{21,13},{10,18... | collective-permute-start | bytes 2433032 | tf_op jit(solution)/shard_map/ppermute | solution.py:177
  914.3 45.4 %collective-permute-start.84 = (bf16[1,2,2,2,48,2048]{5,4,3,2,1,0:T(8,128)(2,1)}, bf16[1,2,2,2,48,2048]{5,4,3,2,1,0:T(8,128)(2,1)}, u32[]{:S(2)}, u32[]{:S(2)}) collective-permute-start(bf16[1,2,2,2,48,2048]{5,4,3,2,1,0:T(8,128)(2,1)} %add_convert_fusion.2), channel_id=1, source_target_pairs={{0,2},{1,3},{2,0},{3,1},{4,6},{5,7},{6,4},{7,5},{8,10},{9,11},{10,... | collective-permute-start | bytes 4718600 | tf_op jit(solution)/shard_map/ppermute | solution.py:177
  918.0 44.5 %collective-permute-start.82 = (bf16[1,2,2,1,96,2176]{5,4,3,2,1,0:T(8,128)(2,1)}, bf16[1,2,2,1,96,2176]{5,4,3,2,1,0:T(8,128)(2,1)}, u32[]{:S(2)}, u32[]{:S(2)}) collective-permute-start(bf16[1,2,2,1,96,2176]{5,4,3,2,1,0:T(8,128)(2,1)} %add_convert_fusion.1), channel_id=1, source_target_pairs={{0,4},{4,0},{8,12},{12,8},{16,20},{20,16},{24,28},{28,24},{1,5},{5... | collective-permute-start | bytes 5013512 | tf_op jit(solution)/shard_map/ppermute | solution.py:177
  930.0 57.7 %collective-permute-start.89 = (bf16[1,2,2,2,192,1408]{5,4,3,2,1,0:T(8,128)(2,1)}, bf16[1,2,2,2,192,1408]{5,4,3,2,1,0:T(8,128)(2,1)}, u32[]{:S(2)}, u32[]{:S(2)}) collective-permute-start(bf16[1,2,2,2,192,1408]{5,4,3,2,1,0:T(8,128)(2,1)} %constant_dynamic-slice_fusion.1), channel_id=1, source_target_pairs={{0,1},{1,0},{2,3},{3,2},{4,5},{5,4},{6,7},{7,6},{8,9},{9,8},{10,11... | collective-permute-start | bytes 12976136 | tf_op jit(solution)/shard_map/ppermute | solution.py:177
  944.1 190.2 %collective-permute-start.68 = (bf16[128,1408]{1,0:T(8,128)(2,1)}, bf16[128,1408]{1,0:T(8,128)(2,1)}, u32[]{:S(2)}, u32[]{:S(2)}) collective-permute-start(bf16[128,1408]{1,0:T(8,128)(2,1)} %get-tuple-element.458), channel_id=1, source_target_pairs={{0,2},{1,3},{2,0},{3,1},{4,6},{5,7},{6,4},{7,5},{8,10},{9,11},{10,... | collective-permute-start | bytes 1081352 | tf_op jit(solution)/shard_map/ppermute | solution.py:144
  984.9 41.6 %collective-permute-start.86 = (bf16[1,1,2,1,48,4224]{5,4,3,2,1,0:T(8,128)(2,1)}, bf16[1,1,2,1,48,4224]{5,4,3,2,1,0:T(8,128)(2,1)}, u32[]{:S(2)}, u32[]{:S(2)}) collective-permute-start(bf16[1,1,2,1,48,4224]{5,4,3,2,1,0:T(8,128)(2,1)} %fusion.86), channel_id=1, source_target_pairs={{0,8},{4,12},{24,16},{28,20},{1,9},{5,13},{25,17},{29,21},{2,10},{... | collective-permute-start | bytes 2433032 | tf_op jit(solution)/shard_map/ppermute | solution.py:177
  993.9 29.2 %collective-permute-start.90 = (bf16[1,2,2,1,192,768]{5,4,3,2,1,0:T(8,128)(2,1)}, bf16[1,2,2,1,192,768]{5,4,3,2,1,0:T(8,128)(2,1)}, u32[]{:S(2)}, u32[]{:S(2)}) collective-permute-start(bf16[1,2,2,1,192,768]{5,4,3,2,1,0:T(8,128)(2,1)} %add_convert_fusion.5), channel_id=1, source_target_pairs={{0,4},{4,0},{8,12},{12,8},{16,20},{20,16},{24,28},{28,24},{1,5},{5... | collective-permute-start | bytes 3538952 | tf_op jit(solution)/shard_map/ppermute | solution.py:177
  1076.6 34.7 %all-to-all-start.3 = ((bf16[4,816,384]{2,1,0:T(8,128)(2,1)}), bf16[4,816,384]{2,1,0:T(8,128)(2,1)}, u32[]{:S(2)}, u32[]{:S(2)}) async-start(bf16[4,816,384]{2,1,0:T(8,128)(2,1)} %pad_dynamic-update-slice_fusion.3), calls=%async_computation.6 | async-start | bytes 5013504 | tf_op jit(solution)/shard_map/all_to_all | solution.py:249
  (421 other events, 4447.1 us)
Sparse Core Ops, SparseCore 0:
  550.6 106.9 reduce-scatter.3
  661.6 89.5 reduce-scatter.7
  773.8 164.2 reduce-scatter.5
